TPU v7x, 32 devices: a whole 2x2x4 slice. The times are simulated.
32 devices in a mesh: seq: 8 (over z, y), mp: 4 (over x, core).
Axes of the slice: x: 2, y: 2, z: 4, core: 2. Of those that a mesh axis runs over, the one named last changes fastest.
Arguments:
- activations: bfloat16 [8192, 768], P('seq'), may hold values from -6 to 6
- cotangent: bfloat16 [8192, 768], P('seq'), may hold values from -6 to 6
- segments: int32 [8192], P('seq'), may hold values from 1 to 8, as said below
- dilated_heads: int32 [2], replicated, may hold values from 0 to 11, as said below
- owners: int32 [8], replicated, may hold values from 0 to 7, each once
- attn_weights: float32 [2, 4, 768, 768], P(None, None, 'seq', 'mp')
- attn_first: float32 [2, 4, 768, 768], P(None, None, 'seq', 'mp')
- attn_second: float32 [2, 4, 768, 768], P(None, None, 'seq', 'mp'), as said below
- attn_average: float32 [2, 4, 768, 768], P(None, None, 'seq', 'mp')
- attn_basis: float32 [2, 4, 8, 4, 192, 192], P(None, None, 'seq', 'mp'), as said below
- ffn_weights: float32 [2, 2, 768, 3072], P(None, None, 'seq', 'mp')
- ffn_first: float32 [2, 2, 768, 3072], P(None, None, 'seq', 'mp')
- ffn_second: float32 [2, 2, 768, 3072], P(None, None, 'seq', 'mp'), as said below
- ffn_average: float32 [2, 2, 768, 3072], P(None, None, 'seq', 'mp')
- ffn_basis: float32 [2, 2, 8, 4, 768, 768], P(None, None, 'seq', 'mp'), as said below
- split_biases: float32 [2, 4, 1152], P(None, 'mp'), may hold values from -1.8 to 1.8
- split_first: float32 [2, 4, 1152], P(None, 'mp')
- split_second: float32 [2, 4, 1152], P(None, 'mp'), as said below
- shared_vectors: float32 [2, 6, 768], replicated
- shared_first: float32 [2, 6, 768], replicated
- shared_second: float32 [2, 6, 768], replicated, as said below
Outputs:
- output: float32 [8192, 768], P('seq')
- input_grad: float32 [8192, 768], P('seq')
- attn_new: float32 [2, 4, 768, 768], P(None, None, 'seq', 'mp')
- attn_first_new: float32 [2, 4, 768, 768], P(None, None, 'seq', 'mp')
- attn_second_new: float32 [2, 3, 768, 768], P(None, None, 'seq', 'mp')
- projection_second: float32 [2, 768, 768], P(None, 'seq', 'mp')
- attn_average_new: float32 [2, 4, 768, 768], P(None, None, 'seq', 'mp')
- updated_ffn_weights: float32 [2, 2, 768, 3072], P(None, None, 'seq', 'mp')
- ffn_first_new: float32 [2, 2, 768, 3072], P(None, None, 'seq', 'mp')
- ffn_second_new: float32 [2, 2, 768, 3072], P(None, None, 'seq', 'mp')
- ffn_average_new: float32 [2, 2, 768, 3072], P(None, None, 'seq', 'mp')
- split_new: float32 [2, 4, 1152], P(None, 'mp')
- updated_split_first_moment: float32 [2, 4, 1152], P(None, 'mp')
- split_second_new: float32 [2, 4, 1152], P(None, 'mp')
- shared_new: float32 [2, 6, 768], replicated
- shared_first_new: float32 [2, 6, 768], replicated
- shared_second_new: float32 [2, 6, 768], replicated
- grad_norm: float32 [], replicated
Inputs may be any that keep to these rules, and one draw needn't show every extreme that they name: `segments`: ids never fall and rise by one at each new document, starting at 1; there are 8 documents, and the i-th document boundary lies within 256 tokens of i * 1024. `dilated_heads`: 2 different head numbers, the last of them 12 - 1. `attn_basis`: every block [l, m, s, j] is an orthogonal matrix. `ffn_basis`: every block [l, m, s, j] is an orthogonal matrix. `attn_second`: positive. `ffn_second`: positive. `split_second`: positive. `shared_second`: positive.
All inputs are finite; a program needn't handle non-finite values.
Results may differ from a plain program's by a relative error of at most 0.03.
Values may be sent and summed in bfloat16 or wider, within the bound.
A program may use at most 192 MiB of HBM per device.

v0:
```python
from functools import partial

import jax
import jax.numpy as jnp
from jax import lax
from jax.sharding import PartitionSpec as P

D = 768
DH = 64
FF = 3072
WIN = 256
STEP = 10


HIGHEST_PRECISION = lax.Precision.HIGHEST
NORM_EPSILON = 1e-05
MASK_FILL = -1e30
CLIP_LEVEL = 1.0
BETA_FIRST = 0.5
BETA_SECOND = 0.5
ADAM_EPSILON = 1e-08
DECAY_RATE = 0.01
AVERAGE_RATE = 0.7
VECTOR_RATE = 0.3


def with_halo(cells, sides, width):
    for axis, dim in sides:
        count = lax.axis_size(axis)
        ends = count - 1
        head = lax.slice_in_dim(cells, 0, width, axis=dim)
        tail = lax.slice_in_dim(cells, cells.shape[dim] - width, cells.shape[dim], axis=dim)
        cells = jnp.concatenate(
            [
                lax.ppermute(tail, axis, [(i, (i + 1) % count) for i in range(ends)]),
                cells,
                lax.ppermute(head, axis, [((i + 1) % count, i) for i in range(ends)]),
            ],
            axis=dim,
        )
    return cells


def from_behind(block, axis, distance):
    devices = range(lax.axis_size(axis))
    route = [(i - distance, i) for i in devices if i - distance in devices]
    return lax.ppermute(block, axis, route)


def normalize_layer(values, gain, shift):
    center = values - jnp.mean(values, axis=-1, keepdims=True)
    spread = jnp.mean(center * center, axis=-1, keepdims=True)
    return center * lax.rsqrt(spread + NORM_EPSILON) * gain + shift


def head_masks(offsets, dilated):
    near = jnp.abs(offsets) <= WIN
    far = jnp.logical_and(jnp.abs(offsets) <= 2 * WIN, offsets % 2 == 0)
    return jnp.where(dilated[:, None, None], far[None, :, :], near[None, :, :])


def join_heads(term):
    return lax.psum(term.astype(jnp.bfloat16), "mp").astype(jnp.float32)


def join_grads(term):
    return lax.psum(term, "mp")


def fetch_rims(pair, rim_width):
    return with_halo(pair, (("seq", 0),), rim_width)


def masked_scores(query_block, key_block, seg_query, seg_keys, dilated, rim_width):
    block_rows = query_block.shape[0]
    key_rows = key_block.shape[0]
    offsets = (
        jnp.arange(block_rows, dtype=jnp.int32)[:, None]
        - jnp.arange(key_rows, dtype=jnp.int32)[None, :]
        + rim_width
    )
    allowed = jnp.logical_and(
        head_masks(offsets, dilated), (seg_query[:, None] == seg_keys[None, :])[None, :, :]
    )
    raw = jnp.einsum(
        "qhd,khd->hqk", query_block, key_block, preferred_element_type=jnp.float32
    ) * DH ** (-0.5)
    return jnp.where(allowed, raw, MASK_FILL)


def attend(query, key_pad, value_pad, seg_own, seg_near, dilated, rim_width):
    row_count = query.shape[0]
    block_rows = min(512, row_count)
    key_rows = block_rows + 2 * rim_width

    def one_block(first_row):
        query_block = lax.dynamic_slice_in_dim(query, first_row, block_rows, 0)
        key_block = lax.dynamic_slice_in_dim(key_pad, first_row, key_rows, 0)
        value_block = lax.dynamic_slice_in_dim(value_pad, first_row, key_rows, 0)
        scores = masked_scores(
            query_block,
            key_block,
            lax.dynamic_slice_in_dim(seg_own, first_row, block_rows, 0),
            lax.dynamic_slice_in_dim(seg_near, first_row, key_rows, 0),
            dilated,
            rim_width,
        )
        row_max = jnp.max(scores, axis=2, keepdims=True)
        exponent = jnp.exp(scores - row_max)
        row_total = jnp.sum(exponent, axis=2, keepdims=True)
        softmax = (exponent / row_total).astype(jnp.bfloat16)
        mixed_block = jnp.einsum(
            "hqk,khd->qhd", softmax, value_block, preferred_element_type=jnp.float32
        )
        return (mixed_block, (row_max + jnp.log(row_total))[:, :, 0])

    starts = jnp.arange(row_count // block_rows, dtype=jnp.int32) * block_rows
    mixed_heads, log_totals = lax.map(one_block, starts)
    return (mixed_heads.reshape(row_count, -1), log_totals)


def attend_back(query, padded, log_totals, grad_mixed, seg_own, seg_near, dilated, rim_width):
    row_count, head_count, _ = query.shape
    head_width = head_count * DH
    block_rows = min(512, row_count)
    key_rows = block_rows + 2 * rim_width
    key_pad = padded[:, :head_width].reshape(-1, head_count, DH)
    value_pad = padded[:, head_width:].reshape(-1, head_count, DH)
    grad_heads = grad_mixed.reshape(row_count, head_count, DH)
    score_scale = DH ** (-0.5)

    def one_step(carry, inputs):
        first_row, totals_block = inputs
        query_block = lax.dynamic_slice_in_dim(query, first_row, block_rows, 0)
        key_block = lax.dynamic_slice_in_dim(key_pad, first_row, key_rows, 0)
        value_block = lax.dynamic_slice_in_dim(value_pad, first_row, key_rows, 0)
        grad_block = lax.dynamic_slice_in_dim(grad_heads, first_row, block_rows, 0)
        scores = masked_scores(
            query_block,
            key_block,
            lax.dynamic_slice_in_dim(seg_own, first_row, block_rows, 0),
            lax.dynamic_slice_in_dim(seg_near, first_row, key_rows, 0),
            dilated,
            rim_width,
        )
        softmax = jnp.exp(scores - totals_block[:, :, None])
        grad_value = jnp.einsum(
            "hqk,qhd->khd",
            softmax.astype(jnp.bfloat16),
            grad_block,
            preferred_element_type=jnp.float32,
        )
        grad_soft = jnp.einsum(
            "qhd,khd->hqk", grad_block, value_block, preferred_element_type=jnp.float32
        )
        row_dot = jnp.sum(grad_soft * softmax, axis=2, keepdims=True)
        grad_scores = (softmax * (grad_soft - row_dot)).astype(jnp.bfloat16)
        grad_query = (
            jnp.einsum("hqk,khd->qhd", grad_scores, key_block, preferred_element_type=jnp.float32)
            * score_scale
        )
        grad_key = (
            jnp.einsum("hqk,qhd->khd", grad_scores, query_block, preferred_element_type=jnp.float32)
            * score_scale
        )
        update = jnp.concatenate(
            [grad_key.reshape(key_rows, head_width), grad_value.reshape(key_rows, head_width)],
            axis=1,
        )
        current = lax.dynamic_slice_in_dim(carry, first_row, key_rows, 0)
        carry = lax.dynamic_update_slice_in_dim(carry, current + update, first_row, 0)
        return (carry, grad_query.reshape(block_rows, head_width))

    starts = jnp.arange(row_count // block_rows, dtype=jnp.int32) * block_rows
    initial = jnp.zeros((row_count + 2 * rim_width, 2 * head_width), jnp.float32)
    grad_pad, grad_query = lax.scan(one_step, initial, (starts, log_totals))
    from_above = from_behind(grad_pad[:rim_width], "seq", -1)
    from_below = from_behind(grad_pad[row_count + rim_width :], "seq", 1)
    grad_pair = grad_pad[rim_width : row_count + rim_width]
    grad_pair = (
        grad_pair
        + jnp.pad(from_below, ((0, row_count - rim_width), (0, 0)))
        + jnp.pad(from_above, ((row_count - rim_width, 0), (0, 0)))
    )
    return (grad_query.reshape(row_count, head_width), grad_pair)


def layer_forward(inputs, attn, ffn, shared, split, seg_own, seg_pad, dilated, rim_width):
    head_width = attn.shape[2]
    row_count = inputs.shape[0]
    inputs_low = inputs.astype(jnp.bfloat16)
    biases = jnp.stack(
        [
            split[0, :head_width],
            jnp.zeros((head_width,), jnp.float32),
            split[0, head_width : 2 * head_width],
        ]
    )
    projected = (
        jnp.einsum("td,mdc->tmc", inputs_low, attn[:3], preferred_element_type=jnp.float32)
        + biases[None]
    ).astype(jnp.bfloat16)
    query = projected[:, 0].reshape(row_count, -1, DH)
    padded = fetch_rims(jnp.concatenate([projected[:, 1], projected[:, 2]], axis=1), rim_width)
    key_pad = padded[:, :head_width].reshape(-1, head_width // DH, DH)
    value_pad = padded[:, head_width:].reshape(-1, head_width // DH, DH)
    seg_near = lax.slice_in_dim(
        seg_pad, 2 * WIN - rim_width, 2 * WIN + row_count + rim_width, axis=0
    )
    mixed_heads, log_totals = attend(
        query, key_pad, value_pad, seg_own, seg_near, dilated, rim_width
    )
    mixed_heads = mixed_heads.astype(jnp.bfloat16)
    attn_sum = (
        inputs
        + join_heads(
            jnp.einsum("tc,dc->td", mixed_heads, attn[3], preferred_element_type=jnp.float32)
        )
        + shared[0]
    )
    normed = normalize_layer(attn_sum, shared[1], shared[2])
    normed_low = normed.astype(jnp.bfloat16)
    pre_gelu = (
        jnp.dot(normed_low, ffn[0], preferred_element_type=jnp.float32) + split[0, 2 * head_width :]
    )
    hidden = jax.nn.gelu(pre_gelu, approximate=False).astype(jnp.bfloat16)
    ffn_sum = (
        normed
        + join_heads(jnp.einsum("tc,dc->td", hidden, ffn[1], preferred_element_type=jnp.float32))
        + shared[3]
    )
    result = normalize_layer(ffn_sum, shared[4], shared[5])
    return (
        result,
        (
            inputs_low,
            query,
            padded,
            log_totals,
            mixed_heads,
            attn_sum,
            normed_low,
            pre_gelu,
            hidden,
            ffn_sum,
        ),
    )


def layer_backward(grad_out, saved, attn, ffn, shared, seg_own, seg_pad, dilated, rim_width):
    (
        inputs_low,
        query,
        padded,
        log_totals,
        mixed_heads,
        attn_sum,
        normed_low,
        pre_gelu,
        hidden,
        ffn_sum,
    ) = saved
    head_width = attn.shape[2]
    row_count = inputs_low.shape[0]
    seg_near = lax.slice_in_dim(
        seg_pad, 2 * WIN - rim_width, 2 * WIN + row_count + rim_width, axis=0
    )
    _, pull_out = jax.vjp(normalize_layer, ffn_sum, shared[4], shared[5])
    grad_ffn_sum, grad_gain_two, grad_shift_two = pull_out(grad_out)
    grad_branch = grad_ffn_sum.astype(jnp.bfloat16)
    grad_down = jnp.einsum("td,tc->dc", grad_branch, hidden, preferred_element_type=jnp.float32)
    grad_hidden = jnp.dot(grad_branch, ffn[1], preferred_element_type=jnp.float32)
    _, pull_gelu = jax.vjp(partial(jax.nn.gelu, approximate=False), pre_gelu)
    grad_pre = pull_gelu(grad_hidden)[0].astype(jnp.bfloat16)
    grad_up = jnp.einsum("td,tc->dc", normed_low, grad_pre, preferred_element_type=jnp.float32)
    grad_normed = grad_ffn_sum + join_grads(
        jnp.einsum("tc,dc->td", grad_pre, ffn[0], preferred_element_type=jnp.float32)
    )
    _, pull_mid = jax.vjp(normalize_layer, attn_sum, shared[1], shared[2])
    grad_attn_sum, grad_gain_one, grad_shift_one = pull_mid(grad_normed)
    grad_attn_out = grad_attn_sum.astype(jnp.bfloat16)
    grad_out_proj = jnp.einsum(
        "td,tc->dc", grad_attn_out, mixed_heads, preferred_element_type=jnp.float32
    )
    grad_mixed = jnp.dot(grad_attn_out, attn[3], preferred_element_type=jnp.float32).astype(
        jnp.bfloat16
    )
    grad_query, grad_pair = attend_back(
        query, padded, log_totals, grad_mixed, seg_own, seg_near, dilated, rim_width
    )
    grad_proj = jnp.stack(
        [grad_query, grad_pair[:, :head_width], grad_pair[:, head_width:]], axis=1
    ).astype(jnp.bfloat16)
    grad_in_proj = jnp.einsum(
        "td,tmc->mdc", inputs_low, grad_proj, preferred_element_type=jnp.float32
    )
    grad_inputs = grad_attn_sum + join_grads(
        jnp.einsum("tmc,mdc->td", grad_proj, attn[:3], preferred_element_type=jnp.float32)
    )
    proj_sums = jnp.sum(grad_proj.astype(jnp.float32), axis=0)
    split_grad = jnp.concatenate(
        [proj_sums[0], proj_sums[2], jnp.sum(grad_pre.astype(jnp.float32), axis=0)]
    )
    shared_grad = jnp.stack(
        [
            jnp.sum(grad_attn_sum, axis=0),
            grad_gain_one,
            grad_shift_one,
            jnp.sum(grad_ffn_sum, axis=0),
            grad_gain_two,
            grad_shift_two,
        ]
    )
    attn_grad = jnp.concatenate([grad_in_proj, grad_out_proj[None]], axis=0)
    ffn_grad = jnp.stack([grad_up, grad_down])
    return (grad_inputs, attn_grad, ffn_grad, shared_grad, split_grad)


def from_slots(gathered, owners, slot_count):
    layer_count, matrix_count, row_count, col_count = gathered.shape
    blocks = gathered.reshape(
        layer_count, matrix_count, slot_count, row_count // slot_count, col_count
    )
    return jnp.take(blocks, owners, axis=2).reshape(gathered.shape)


def to_slots(grads, inverse, slot_count):
    matrix_count, row_count, col_count = grads.shape
    blocks = grads.reshape(matrix_count, slot_count, row_count // slot_count, col_count)
    return jnp.take(blocks, inverse, axis=1).reshape(grads.shape)


def rotate_update(weight, grad_now, first, second, running_average, basis, rates):
    turn = basis[:, :, 0, 0]
    turned = jnp.einsum("lmre,lmec->lmrc", grad_now, turn, precision=HIGHEST_PRECISION)
    first_new = BETA_FIRST * first + (1.0 - BETA_FIRST) * turned
    second_new = BETA_SECOND * second + (1.0 - BETA_SECOND) * turned * turned
    direction = (
        first_new
        / (1.0 - BETA_FIRST**STEP)
        / (jnp.sqrt(second_new / (1.0 - BETA_SECOND**STEP)) + ADAM_EPSILON)
    )
    back = jnp.einsum("lmrc,lmec->lmre", direction, turn, precision=HIGHEST_PRECISION)
    weight_new = weight - rates[None, :, None, None] * (back + DECAY_RATE * weight)
    average_new = AVERAGE_RATE * running_average + (1.0 - AVERAGE_RATE) * weight_new
    return (weight_new, first_new, second_new, average_new)


def vector_update(current, grad_now, first, second):
    first_new = BETA_FIRST * first + (1.0 - BETA_FIRST) * grad_now
    second_new = BETA_SECOND * second + (1.0 - BETA_SECOND) * grad_now * grad_now
    direction = (
        first_new
        / (1.0 - BETA_FIRST**STEP)
        / (jnp.sqrt(second_new / (1.0 - BETA_SECOND**STEP)) + ADAM_EPSILON)
    )
    return (current - VECTOR_RATE * direction, first_new, second_new)


def local(
    activations,
    cotangent,
    segments,
    dilated_heads,
    owners,
    attn_weights,
    attn_first,
    attn_second,
    attn_average,
    attn_basis,
    ffn_weights,
    ffn_first,
    ffn_second,
    ffn_average,
    ffn_basis,
    split_biases,
    split_first,
    split_second,
    shared_vectors,
    shared_first,
    shared_second,
):
    slot_count = lax.axis_size("seq")
    layer_count = attn_weights.shape[0]
    attn_full, ffn_full = (
        lax.all_gather(attn_weights.astype(jnp.bfloat16), "seq", axis=2, tiled=True),
        lax.all_gather(ffn_weights.astype(jnp.bfloat16), "seq", axis=2, tiled=True),
    )
    attn_full = from_slots(attn_full, owners, slot_count)
    ffn_full = from_slots(ffn_full, owners, slot_count)
    seg_pad = with_halo(segments, (("seq", 0),), 2 * WIN)
    head_width = attn_full.shape[3]
    head_count = head_width // DH
    heads_here = lax.axis_index("mp") * head_count + jnp.arange(head_count, dtype=jnp.int32)
    head_flags = jnp.any(heads_here[:, None] == dilated_heads[None, :], axis=1)
    current = activations.astype(jnp.float32)
    saved_list = []
    for layer_index in range(layer_count):
        dilated = jnp.logical_and(head_flags, layer_index % 2 == 1)
        rim_width = 2 * WIN if layer_index % 2 == 1 else WIN
        current, saved = layer_forward(
            current,
            attn_full[layer_index],
            ffn_full[layer_index],
            shared_vectors[layer_index],
            split_biases[layer_index],
            segments,
            seg_pad,
            dilated,
            rim_width,
        )
        saved_list.append(saved)
    slot_range = jnp.arange(slot_count, dtype=jnp.int32)
    inverse = jnp.sum(
        jnp.where(owners[None, :] == slot_range[:, None], slot_range[None, :], 0), axis=1
    )
    grad_now = cotangent.astype(jnp.float32)
    attn_list = [None] * layer_count
    ffn_list = [None] * layer_count
    shared_list = [None] * layer_count
    split_list = [None] * layer_count
    for layer_index in range(layer_count - 1, -1, -1):
        dilated = jnp.logical_and(head_flags, layer_index % 2 == 1)
        rim_width = 2 * WIN if layer_index % 2 == 1 else WIN
        grad_now, attn_grad, ffn_grad, shared_grad, split_grad = layer_backward(
            grad_now,
            saved_list[layer_index],
            attn_full[layer_index],
            ffn_full[layer_index],
            shared_vectors[layer_index],
            segments,
            seg_pad,
            dilated,
            rim_width,
        )
        attn_grad = to_slots(attn_grad, inverse, slot_count)
        ffn_grad = to_slots(ffn_grad, inverse, slot_count)
        attn_list[layer_index] = attn_grad
        ffn_list[layer_index] = ffn_grad
        shared_list[layer_index] = shared_grad
        split_list[layer_index] = split_grad[None, :]
    attn_grads = jnp.stack(attn_list)
    ffn_grads = jnp.stack(ffn_list)
    attn_grads, ffn_grads = (
        lax.psum_scatter(attn_grads, "seq", scatter_dimension=2, tiled=True),
        lax.psum_scatter(ffn_grads, "seq", scatter_dimension=2, tiled=True),
    )
    shared_grads, split_grads = lax.psum((jnp.stack(shared_list), jnp.stack(split_list)), "seq")
    first_seq = lax.axis_index("seq") == 0
    first_both = jnp.logical_and(first_seq, lax.axis_index("mp") == 0)
    local_sum = jnp.sum(attn_grads * attn_grads) + jnp.sum(ffn_grads * ffn_grads)
    local_sum = (
        local_sum
        + jnp.where(first_seq, jnp.sum(split_grads * split_grads), 0.0)
        + jnp.where(first_both, jnp.sum(shared_grads * shared_grads), 0.0)
    )
    grad_norm = jnp.sqrt(lax.psum(local_sum, ("seq", "mp")))
    factor = CLIP_LEVEL / jnp.maximum(grad_norm, CLIP_LEVEL)
    attn_rates = jnp.array([0.5 * D ** (-0.5)] * 3 + [0.5 * (WIN / D) ** 0.5], jnp.float32)
    ffn_rates = jnp.array([0.5 * D ** (-0.5), 0.5 * FF ** (-0.5)], jnp.float32)
    attn_out = rotate_update(
        attn_weights,
        factor * attn_grads,
        attn_first,
        attn_second,
        attn_average,
        attn_basis,
        attn_rates,
    )
    ffn_out = rotate_update(
        ffn_weights, factor * ffn_grads, ffn_first, ffn_second, ffn_average, ffn_basis, ffn_rates
    )
    split_out = vector_update(split_biases, factor * split_grads, split_first, split_second)
    shared_out = vector_update(shared_vectors, factor * shared_grads, shared_first, shared_second)
    return (
        current,
        grad_now,
        attn_out[0],
        attn_out[1],
        attn_out[2][:, :3],
        attn_out[2][:, 3],
        attn_out[3],
        ffn_out[0],
        ffn_out[1],
        ffn_out[2],
        ffn_out[3],
        split_out[0],
        split_out[1],
        split_out[2],
        shared_out[0],
        shared_out[1],
        shared_out[2],
        grad_norm,
    )


def solution(mesh):
    placed = (
        P("seq", None),
        P("seq", None),
        P("seq"),
        P(),
        P(),
        P(None, None, "seq", "mp"),
        P(None, None, "seq", "mp"),
        P(None, None, "seq", "mp"),
        P(None, None, "seq", "mp"),
        P(None, None, "seq", "mp", None, None),
        P(None, None, "seq", "mp"),
        P(None, None, "seq", "mp"),
        P(None, None, "seq", "mp"),
        P(None, None, "seq", "mp"),
        P(None, None, "seq", "mp", None, None),
        P(None, "mp", None),
        P(None, "mp", None),
        P(None, "mp", None),
        P(),
        P(),
        P(),
    )
    return jax.shard_map(
        local,
        mesh=mesh,
        in_specs=placed,
        out_specs=(
            P("seq", None),
            P("seq", None),
            P(None, None, "seq", "mp"),
            P(None, None, "seq", "mp"),
            P(None, None, "seq", "mp"),
            P(None, "seq", "mp"),
            P(None, None, "seq", "mp"),
            P(None, None, "seq", "mp"),
            P(None, None, "seq", "mp"),
            P(None, None, "seq", "mp"),
            P(None, None, "seq", "mp"),
            P(None, "mp", None),
            P(None, "mp", None),
            P(None, "mp", None),
            P(),
            P(),
            P(),
            P(),
        ),
        check_vma=False,
    )
```

profile of v0, /device:TPU:0, one launch (start us, length us, event | category | flops | bytes accessed | tf_op | source)
XLA Modules:
  0.0 1481.4 jit_solution(815637760976634588)
XLA Ops:
  21.6 52.4 %all-gather.3.cloned.1.call-done = bf16[2,4,768,192]{3,2,1,0:T(8,128)(2,1)} async-done(((bf16[2,4,96,192]{3,2,1,0:T(8,128)(2,1)}), bf16[2,4,768,192]{3,2,1,0:T(8,128)(2,1)}) %all-gather.3.cloned.1.call-update) | async-done | bytes 2359312 | tf_op jit(solution)/shard_map/all_gather | solution.py:386
  104.8 28.6 %while.52 = (s32[]{:T(128)}, bf16[2,512,3,64]{1,3,2,0:T(8,128)(2,1)}, f32[2,3,512]{2,1,0:T(4,128)}, s32[2]{0:T(128)}, bf16[1536,3,64]{0,2,1:T(8,128)(2,1)}, /*in...) while((s32[]{:T(128)}, ...), condition=%wide.region_3.4_spmd, body=%wide.region_0.3_spmd.sunk | while | flops 424671744 | bytes 25567520 | solution.py:118
  143.4 40.2 %all-reduce.14.cloned.1.call-done = bf16[1024,768]{1,0:T(8,128)(2,1)} async-done(((bf16[1024,768]{1,0:T(8,128)(2,1)}), bf16[1024,768]{1,0:T(8,128)(2,1)}) %all-reduce.14.cloned.1.call-update) | async-done | bytes 1572880 | tf_op jit(solution)/shard_map/psum | solution.py:63
  186.6 79.7 %all-gather.5.cloned.1.call-done = bf16[2,2,768,768]{3,2,1,0:T(8,128)(2,1)} async-done(((bf16[2,2,96,768]{3,2,1,0:T(8,128)(2,1)}), bf16[2,2,768,768]{3,2,1,0:T(8,128)(2,1)}) %all-gather.5.cloned.1.call-update) | async-done | bytes 4718608 | tf_op jit(solution)/shard_map/all_gather | solution.py:387
  276.3 9.8 multiply_convert_fusion.3
  295.4 35.6 %all-reduce.16.cloned.1.call-done = bf16[1024,768]{1,0:T(8,128)(2,1)} async-done(((bf16[1024,768]{1,0:T(8,128)(2,1)}), bf16[1024,768]{1,0:T(8,128)(2,1)}) %all-reduce.16.cloned.1.call-update) | async-done | bytes 1572880 | tf_op jit(solution)/shard_map/psum | solution.py:63
  345.2 13.8 collective-permute-done.4
  360.8 33.4 %while.53 = (s32[]{:T(128)}, bf16[2,512,3,64]{1,3,2,0:T(8,128)(2,1)}, f32[2,3,512]{2,1,0:T(4,128)}, s32[2]{0:T(128)}, bf16[2048,3,64]{0,2,1:T(8,128)(2,1)S(1)}, ...) while((s32[]{:T(128)}, ...), condition=%wide.region_14.15_spmd, body=%wide.region_11.14_spmd.sunk | while | flops 642513408 | bytes 38127968 | solution.py:118
  400.7 42.7 %all-reduce.18.cloned.1.call-done = bf16[1024,768]{1,0:T(8,128)(2,1)} async-done(((bf16[1024,768]{1,0:T(8,128)(2,1)}), bf16[1024,768]{1,0:T(8,128)(2,1)}) %all-reduce.18.cloned.1.call-update) | async-done | bytes 1572880 | tf_op jit(solution)/shard_map/psum | solution.py:63
  449.1 9.7 multiply_convert_fusion.2
  462.7 43.0 %all-reduce.20.cloned.1.call-done = bf16[1024,768]{1,0:T(8,128)(2,1)} async-done(((bf16[1024,768]{1,0:T(8,128)(2,1)}), bf16[1024,768]{1,0:T(8,128)(2,1)}) %all-reduce.20.cloned.1.call-update) | async-done | bytes 1572880 | tf_op jit(solution)/shard_map/psum | solution.py:63
  525.4 68.6 %all-reduce.22.cloned.1.call-done = f32[1024,768]{1,0:T(8,128)} async-done(((f32[1024,768]{1,0:T(8,128)}), f32[1024,768]{1,0:T(8,128)}) %all-reduce.22.cloned.1.call-update) | async-done | bytes 3145744 | tf_op jit(solution)/shard_map/psum | solution.py:67
  605.6 99.0 %while.54 = (s32[]{:T(128)}, f32[2048,384]{0,1:T(8,128)}, bf16[2,512,192]{1,2,0:T(8,128)(2,1)}, s32[2]{0:T(128)S(1)}, bf16[1024,3,64]{0,2,1:T(8,128)(2,1)S(1)}, ...) while((s32[]{:T(128)}, f32[2048,384]{0,1:T(8,128)}, ...), condition=%wide.region_28.29_spmd, body=%wide.region_26.28_spmd.sunk | while | flops 1552513536 | bytes 173105808 | solution.py:176
  626.2 9.4 multiply_convert_fusion.6
  644.7 10.8 dynamic_update_slice.58
  675.7 9.4 multiply_convert_fusion.6
  694.2 10.4 dynamic_update_slice.58
  714.7 29.8 %collective-permute-done.6 = f32[512,384]{0,1:T(8,128)} collective-permute-done((f32[512,384]{0,1:T(8,128)}, f32[512,384]{0,1:T(8,128)}, u32[]{:S(2)}, u32[]{:S(2)}) %collective-permute-start.6) | collective-permute-done | bytes 786464 | tf_op jit(solution)/shard_map/ppermute | solution.py:47
  750.7 69.9 %all-reduce.24.cloned.1.call-done = f32[1024,768]{1,0:T(8,128)} async-done(((f32[1024,768]{1,0:T(8,128)}), f32[1024,768]{1,0:T(8,128)}) %all-reduce.24.cloned.1.call-update) | async-done | bytes 3145744 | tf_op jit(solution)/shard_map/psum | solution.py:67
  838.8 68.6 %all-reduce.26.cloned.1.call-done = f32[1024,768]{1,0:T(8,128)} async-done(((f32[1024,768]{1,0:T(8,128)}), f32[1024,768]{1,0:T(8,128)}) %all-reduce.26.cloned.1.call-update) | async-done | bytes 3145744 | tf_op jit(solution)/shard_map/psum | solution.py:67
  918.6 59.0 %while.55 = (s32[]{:T(128)}, f32[1536,384]{0,1:T(8,128)}, bf16[2,512,192]{1,2,0:T(8,128)(2,1)}, s32[2]{0:T(128)}, bf16[1024,3,64]{0,2,1:T(8,128)(2,1)S(1)}, /*in...) while((s32[]{:T(128)}, f32[1536,384]{0,1:T(8,128)}, ...), condition=%wide.region_37.38_spmd, body=%wide.region_35.37_spmd.sunk | while | flops 1034549760 | bytes 70775088 | solution.py:176
  940.6 7.8 dynamic_update_slice.60
  970.4 7.2 dynamic_update_slice.60
  988.6 11.5 collective-permute-done.8
  1035.3 40.6 %all-reduce.28.cloned.1.call-done = f32[1024,768]{1,0:T(8,128)} async-done(((f32[1024,768]{1,0:T(8,128)}), f32[1024,768]{1,0:T(8,128)}) %all-reduce.28.cloned.1.call-update) | async-done | bytes 3145744 | tf_op jit(solution)/shard_map/psum | solution.py:67
  1120.8 7.3 copy.135
  1128.0 8.3 reshape.699
  1186.7 38.8 %all-reduce.4 = (f32[2,1,1152]{2,1,0:T(1,128)S(1)}, f32[2,6,768]{2,1,0:T(8,128)S(1)}) all-reduce(f32[2,1,1152]{2,1,0:T(1,128)S(1)} %pad_maximum_fusion.14, f32[2,6,768]{2,1,0:T(8,128)S(1)} %pad_maximum_fusion.13), channel_id=1, replica_groups=mesh['seq'=8,'mp'=4] {'seq'}, use_global_device_ids=true, to_apply=%region_48.51 | all-reduce | flops 11520 | bytes 92160 | tf_op jit(solution)/shard_map/psum | solution.py:448
  1235.6 163.8 %reduce-scatter.5.cloned.1.call-done = f32[2,2,96,768]{3,2,1,0:T(8,128)} async-done(((f32[2,2,768,768]{3,2,1,0:T(8,128)}), f32[2,2,96,768]{3,2,1,0:T(8,128)}) %reduce-scatter.5.cloned.1.call-update) | async-done | bytes 1179664 | tf_op jit(solution)/shard_map/reduce_scatter | solution.py:446
  1402.9 39.4 %psum.87 = f32[]{:T(128)} all-reduce(f32[]{:T(128)S(6)} %add.575), channel_id=1, replica_groups=mesh['seq'=8,'mp'=4] {'seq','mp'}, use_global_device_ids=true, to_apply=%region_64.67 | all-reduce | flops 1 | bytes 8 | tf_op jit(solution)/shard_map/psum | solution.py:457
  1454.0 8.6 multiply_add_fusion.4
  1462.8 10.2 multiply_add_fusion.5
  (690 shorter events, 487.1 us)
Async XLA Ops:
  7.2 1435.8 %copy-start = (f32[2,4,1,1,192,192]{5,4,3,2,1,0:T(8,128)S(1)}, f32[2,4,1,1,192,192]{5,4,3,2,1,0:T(8,128)}, u32[]{:S(2)}) copy-start(f32[2,4,1,1,192,192]{5,4,3,2,1,0:T(8,128)} %param.44) | copy-start | bytes 3538948
  7.2 66.9 %all-gather.3.cloned.1.call-start = ((), (), s32[]{:S(2)}) async-start(), calls=%async_computation.2 | async-start | bytes 3538944 | tf_op jit(solution)/shard_map/all_gather | solution.py:386
  9.3 174.2 %all-reduce.14.cloned.1.call-start = ((), (), s32[]{:S(2)}) async-start(), calls=%async_computation.3 | async-start | bytes 3145728 | tf_op jit(solution)/shard_map/psum | solution.py:63
  10.1 10.9 collective-permute-start.3
  11.4 8.9 collective-permute-start.2
  91.9 5.9 collective-permute-start
  94.4 7.9 collective-permute-start.1
  138.6 127.7 %all-gather.5.cloned.1.call-start = ((), (), s32[]{:S(2)}) async-start(), calls=%async_computation.4 | async-start | bytes 5308416 | tf_op jit(solution)/shard_map/all_gather | solution.py:387
  140.8 190.2 %all-reduce.16.cloned.1.call-start = ((), (), s32[]{:S(2)}) async-start(), calls=%async_computation.5 | async-start | bytes 3145728 | tf_op jit(solution)/shard_map/psum | solution.py:63
  141.8 134.5 %copy-start.145 = (f32[768]{0:T(1024)}, f32[768]{0:T(1024)S(1)}, u32[]{:S(2)}) copy-start(f32[768]{0:T(1024)S(1)} %slice_reduce_fusion.1) | copy-start | bytes 9220
  143.4 187.6 %copy-start.82 = (f32[768]{0:T(1024)}, f32[768]{0:T(1024)S(1)}, u32[]{:S(2)}) copy-start(f32[768]{0:T(1024)S(1)} %get-tuple-element.506) | copy-start | bytes 9220
  143.4 187.6 %copy-start.102 = (f32[768]{0:T(1024)}, f32[768]{0:T(1024)S(1)}, u32[]{:S(2)}) copy-start(f32[768]{0:T(1024)S(1)} %get-tuple-element.505) | copy-start | bytes 9220
  143.4 187.6 %copy-start.135 = (f32[768]{0:T(1024)}, f32[768]{0:T(1024)S(1)}, u32[]{:S(2)}) copy-start(f32[768]{0:T(1024)S(1)} %get-tuple-element.504) | copy-start | bytes 9220
  143.4 191.4 %copy-start.108 = (f32[768]{0:T(1024)}, f32[768]{0:T(1024)S(1)}, u32[]{:S(2)}) copy-start(f32[768]{0:T(1024)S(1)} %get-tuple-element.502) | copy-start | bytes 9220
  143.4 191.4 %copy-start.139 = (f32[768]{0:T(1024)}, f32[768]{0:T(1024)S(1)}, u32[]{:S(2)}) copy-start(f32[768]{0:T(1024)S(1)} %get-tuple-element.501) | copy-start | bytes 9220
  185.7 145.4 %copy-start.86 = (f32[1024]{0:T(1024)}, f32[1024]{0:T(1024)S(1)}, u32[]{:S(2)}) copy-start(f32[1024]{0:T(1024)S(1)} %broadcast_multiply_fusion.3) | copy-start | bytes 12292
  186.6 144.5 %copy-start.93 = (f32[1024]{0:T(1024)}, f32[1024]{0:T(1024)S(1)}, u32[]{:S(2)}) copy-start(f32[1024]{0:T(1024)S(1)} %fusion.155) | copy-start | bytes 12292
  289.9 153.6 %all-reduce.18.cloned.1.call-start = ((), (), s32[]{:S(2)}) async-start(), calls=%async_computation.6 | async-start | bytes 3145728 | tf_op jit(solution)/shard_map/psum | solution.py:63
  338.7 20.3 %collective-permute-start.4 = (bf16[512,384]{0,1:T(8,128)(2,1)}, bf16[512,384]{0,1:T(8,128)(2,1)S(1)}, u32[]{:S(2)}, u32[]{:S(2)}) collective-permute-start(bf16[512,384]{0,1:T(8,128)(2,1)} %get-tuple-element.671), channel_id=1, source_target_pairs={{0,4},{4,8},{8,12},{12,16},{16,20},{20,24},{24,28},{1,5},{5,9},{9,... | collective-permute-start | bytes 1179656 | tf_op jit(solution)/shard_map/ppermute | solution.py:35
  342.1 16.9 %collective-permute-start.5 = (bf16[512,384]{0,1:T(8,128)(2,1)}, bf16[512,384]{0,1:T(8,128)(2,1)S(1)}, u32[]{:S(2)}, u32[]{:S(2)}) collective-permute-start(bf16[512,384]{0,1:T(8,128)(2,1)} %get-tuple-element.672), channel_id=1, source_target_pairs={{4,0},{8,4},{12,8},{16,12},{20,16},{24,20},{28,24},{5,1},{9,5},{13... | collective-permute-start | bytes 1179656 | tf_op jit(solution)/shard_map/ppermute | solution.py:37
  399.2 106.5 %all-reduce.20.cloned.1.call-start = ((), (), s32[]{:S(2)}) async-start(), calls=%async_computation.7 | async-start | bytes 3145728 | tf_op jit(solution)/shard_map/psum | solution.py:63
  447.0 152.5 %copy-start.91 = (f32[1024]{0:T(1024)}, f32[1024]{0:T(1024)S(1)}, u32[]{:S(2)}) copy-start(f32[1024]{0:T(1024)S(1)} %broadcast_multiply_fusion.1) | copy-start | bytes 12292
  462.6 131.4 %all-reduce.22.cloned.1.call-start = ((), (), s32[]{:S(2)}) async-start(), calls=%async_computation.8 | async-start | bytes 6291456 | tf_op jit(solution)/shard_map/psum | solution.py:67
  525.4 295.2 %all-reduce.24.cloned.1.call-start = ((), (), s32[]{:S(2)}) async-start(), calls=%async_computation.9 | async-start | bytes 6291456 | tf_op jit(solution)/shard_map/psum | solution.py:67
  707.2 37.2 %collective-permute-start.6 = (f32[512,384]{0,1:T(8,128)}, f32[512,384]{0,1:T(8,128)}, u32[]{:S(2)}, u32[]{:S(2)}) collective-permute-start(f32[512,384]{0,1:T(8,128)} %get-tuple-element.645), channel_id=1, source_target_pairs={{0,4},{4,8},{8,12},{12,16},{16,20},{20,24},{24,28},{1,5},{5,9},{9,... | collective-permute-start | bytes 2359304 | tf_op jit(solution)/shard_map/ppermute | solution.py:47
  711.5 32.9 %collective-permute-start.7 = (f32[512,384]{0,1:T(8,128)}, f32[512,384]{0,1:T(8,128)}, u32[]{:S(2)}, u32[]{:S(2)}) collective-permute-start(f32[512,384]{0,1:T(8,128)} %get-tuple-element.646), channel_id=1, source_target_pairs={{4,0},{8,4},{12,8},{16,12},{20,16},{24,20},{28,24},{5,1},{9,5},{13... | collective-permute-start | bytes 2359304 | tf_op jit(solution)/shard_map/ppermute | solution.py:47
  750.6 156.7 %all-reduce.26.cloned.1.call-start = ((), (), s32[]{:S(2)}) async-start(), calls=%async_computation.10 | async-start | bytes 6291456 | tf_op jit(solution)/shard_map/psum | solution.py:67
  838.7 237.2 %all-reduce.28.cloned.1.call-start = ((), (), s32[]{:S(2)}) async-start(), calls=%async_computation.11 | async-start | bytes 6291456 | tf_op jit(solution)/shard_map/psum | solution.py:67
  979.7 20.4 %collective-permute-start.8 = (f32[256,384]{0,1:T(8,128)}, f32[256,384]{0,1:T(8,128)}, u32[]{:S(2)}, u32[]{:S(2)}) collective-permute-start(f32[256,384]{0,1:T(8,128)} %get-tuple-element.651), channel_id=1, source_target_pairs={{0,4},{4,8},{8,12},{12,16},{16,20},{20,24},{24,28},{1,5},{5,9},{9,... | collective-permute-start | bytes 1179656 | tf_op jit(solution)/shard_map/ppermute | solution.py:47
  983.8 16.2 %collective-permute-start.9 = (f32[256,384]{0,1:T(8,128)}, f32[256,384]{0,1:T(8,128)}, u32[]{:S(2)}, u32[]{:S(2)}) collective-permute-start(f32[256,384]{0,1:T(8,128)} %get-tuple-element.652), channel_id=1, source_target_pairs={{4,0},{8,4},{12,8},{16,12},{20,16},{24,20},{28,24},{5,1},{9,5},{13... | collective-permute-start | bytes 1179656 | tf_op jit(solution)/shard_map/ppermute | solution.py:47
  1006.0 226.7 %reduce-scatter.7.cloned.1.call-start = ((), (), s32[]{:S(2)}) async-start(), calls=%async_computation.13 | async-start | bytes 5308416
  1136.4 263.0 %reduce-scatter.5.cloned.1.call-start = ((), (), s32[]{:S(2)}) async-start(), calls=%async_computation.12 | async-start | bytes 10616832 | tf_op jit(solution)/shard_map/reduce_scatter | solution.py:446
  (178 other events, 1990.9 us)
Sparse Core Ops, SparseCore 0:
  10.8 63.2 all-gather.2
  138.7 44.7 all-reduce.13
  186.3 79.9 all-gather.4
  290.0 40.9 all-reduce.15
  399.4 44.0 all-reduce.17
  462.8 42.8 all-reduce.19
  525.5 68.4 all-reduce.21
  750.8 69.7 all-reduce.23
  838.8 68.5 all-reduce.25
  1006.1 69.7 all-reduce.27
  1136.5 96.1 reduce-scatter.6
  1236.2 163.1 reduce-scatter.4
where the time goes:
time: 1490 us; the launch traced here: 1480 us
  waiting for transfers between devices  770 us (52%)
  local copies, waits for them, and re-layouts  217 us (15%)
  matrix products  189 us (13%)
  other arithmetic  152 us (10%)
  blocking collectives  78.1 us (5%)
  starting transfers between devices  28.2 us (2%)
  loops' own time  26.1 us (2%)
  between operations  21 us (1%)
    psum x4, waiting for transfers between devices, join_grads(): return lax.psum(term, 'mp')  248 us
    reduce_scatter x1, waiting for transfers between devices, local(): lax.psum_scatter(ffn_grads, 'seq', scatter_dimension=2, tiled=True)  164 us
    psum x4, waiting for transfers between devices, join_heads(): return lax.psum(term.astype(jnp.bfloat16), 'mp').astype(jnp.float32)  161 us
    all_gather x1, waiting for transfers between devices, local(): lax.all_gather(ffn_weights.astype(jnp.bfloat16), 'seq', axis=2, tiled=True)  79.7 us
    all_gather x1, waiting for transfers between devices, local(): lax.all_gather(attn_weights.astype(jnp.bfloat16), 'seq', axis=2, tiled=True)  52.4 us
    ppermute x4, waiting for transfers between devices, from_behind(): return lax.ppermute(block, axis, route)  41.3 us
    unnamed x315, local copies, waits for them, and re-layouts  40.7 us
    psum x1, blocking collectives, local(): grad_norm = jnp.sqrt(lax.psum(local_sum, ('seq', 'mp')))  39.4 us
  transfers between devices with their start and end apart: 22, of which 16 were waited for; matrix products, arithmetic and copies ran while one was open for 7% of the time, Pallas kernels for 0%

commit v1 on v0

v1 whole, which is shorter than its diff:
```python
from types import SimpleNamespace

import jax
import jax.numpy as jnp
from jax import lax
from jax.experimental import pallas as pl
from jax.experimental.pallas import tpu as pltpu
from jax.sharding import PartitionSpec as P

D = 768
DH = 64
FF = 3072
WIN = 256
STEP = 10

HIGHEST_PRECISION = lax.Precision.HIGHEST
NORM_EPSILON = 1e-05
MASK_FILL = -1e30
CLIP_LEVEL = 1.0
BETA_FIRST = 0.5
BETA_SECOND = 0.5
ADAM_EPSILON = 1e-08
DECAY_RATE = 0.01
AVERAGE_RATE = 0.7
VECTOR_RATE = 0.3

BF = jnp.bfloat16
F32 = jnp.float32
MESH = pl.DeviceIdType.MESH
BLOCK = 256
CHUNK = 128
HALF = 64
VMEM_LIMIT = 56 * 1024 * 1024
SCORE_SCALE = DH ** (-0.5)


def dot(left, right):
    return jnp.dot(left, right, preferred_element_type=F32)


def dot_nt(left, right):
    return lax.dot_general(left, right, (((1,), (1,)), ((), ())), preferred_element_type=F32)


def dot_tn(left, right):
    return lax.dot_general(left, right, (((0,), (0,)), ((), ())), preferred_element_type=F32)


def run_kernel(body, name, inputs, outputs, scratch, collective=None, flops=0, grid=None, specs=None, in_smem=()):
    specs = specs or {}
    labels = list(inputs) + list(outputs) + list(scratch)

    def kernel(*refs):
        body(SimpleNamespace(**dict(zip(labels, refs))))

    def spec_of(key):
        if key in specs:
            return specs[key]
        return pl.BlockSpec(memory_space=pltpu.SMEM if key in in_smem else pltpu.VMEM)

    shapes = [jax.ShapeDtypeStruct(shape, dtype) for shape, dtype in outputs.values()]
    moved = sum(v.size * v.dtype.itemsize for v in inputs.values())
    moved += sum(v.size * v.dtype.itemsize for v in shapes)
    extra = {} if grid is None else {"grid": grid}
    params = {"vmem_limit_bytes": VMEM_LIMIT}
    if collective is not None:
        params["collective_id"] = collective
        params["has_side_effects"] = True
    results = pl.pallas_call(
        kernel,
        out_shape=shapes,
        in_specs=[spec_of(key) for key in inputs],
        out_specs=[spec_of(key) for key in outputs],
        scratch_shapes=list(scratch.values()),
        compiler_params=pltpu.CompilerParams(**params),
        cost_estimate=pl.CostEstimate(flops=int(flops), bytes_accessed=int(moved), transcendentals=0),
        name=name,
        **extra,
    )(*inputs.values())
    return SimpleNamespace(**dict(zip(outputs, results)))


def parity_matrix():
    row = lax.broadcasted_iota(jnp.int32, (2 * BLOCK, 2 * BLOCK), 0)
    col = lax.broadcasted_iota(jnp.int32, (2 * BLOCK, 2 * BLOCK), 1)
    source = 2 * (row % BLOCK) + row // BLOCK
    return jnp.where(col == source, 1.0, 0.0).astype(BF)


def head_lanes(count):
    lane = lax.broadcasted_iota(jnp.int32, (1, count * DH), 1)
    return [lane // DH == head for head in range(count)]


def arrange_rows(natural, sort):
    groups = natural.shape[0] // (2 * BLOCK)
    parts = [
        dot(sort, natural[g * 2 * BLOCK : (g + 1) * 2 * BLOCK]).astype(BF) for g in range(groups)
    ]
    return jnp.concatenate([p[:BLOCK] for p in parts] + [p[BLOCK:] for p in parts], axis=0)


def restore_rows(arranged, sort):
    groups = arranged.shape[0] // (2 * BLOCK)
    half = groups * BLOCK
    parts = []
    for g in range(groups):
        pair = jnp.concatenate(
            [
                arranged[g * BLOCK : (g + 1) * BLOCK],
                arranged[half + g * BLOCK : half + (g + 1) * BLOCK],
            ],
            axis=0,
        )
        parts.append(dot_tn(sort, pair))
    return jnp.concatenate(parts, axis=0)


def attend(qkv, left, right, seg_query, seg_keys, flags, flag_lanes, mixed):
    rows, width = qkv.shape[1:]
    rim = left.shape[1]
    heads = width // DH
    blocks = rows // BLOCK
    keys = 3 * BLOCK
    slots = 2 * blocks if mixed else blocks + 2

    def body(r):
        step = pl.program_id(0)

        @pl.when(step == 0)
        def _():
            for which, held in ((1, r.keys), (2, r.values)):
                padded = jnp.concatenate(
                    [r.left[which - 1], r.qkv[which], r.right[which - 1]], axis=0
                )
                if mixed:
                    middle = jnp.concatenate(
                        [
                            padded[BLOCK : (blocks + 1) * BLOCK],
                            padded[(blocks - 1) * BLOCK : (2 * blocks - 1) * BLOCK],
                        ],
                        axis=0,
                    )
                    sort = parity_matrix()
                    held[...] = jnp.where(r.lanes[...] > 0, arrange_rows(padded, sort), middle)
                else:
                    held[...] = padded
            query = (r.qkv[0].astype(F32) * SCORE_SCALE).astype(BF)
            if mixed:
                query = jnp.where(r.lanes[...] > 0, arrange_rows(query, parity_matrix()), query)
            r.query[...] = query

        row = lax.broadcasted_iota(jnp.int32, (BLOCK, keys), 0)
        col = lax.broadcasted_iota(jnp.int32, (BLOCK, keys), 1)
        window = jnp.abs(row - col + BLOCK) <= WIN
        first = step + 2 * (step >= blocks // 2) if mixed else step
        own = pl.ds(pl.multiple_of(step * BLOCK, BLOCK), BLOCK)
        near = pl.ds(pl.multiple_of(first * BLOCK, BLOCK), keys)
        key_block = r.keys[near, :]
        value_block = r.values[near, :]
        query_block = r.query[own, :]
        gathered = jnp.zeros((BLOCK, width), F32)
        for head, lanes in enumerate(head_lanes(heads)):
            if mixed:
                flag = r.flags[head] > 0
                mine = jnp.where(flag, r.seg_query[own, 1:2], r.seg_query[own, 0:1])
                theirs = jnp.where(flag, r.seg_keys[1:2, near], r.seg_keys[0:1, near])
            else:
                mine = r.seg_query[own, 0:1]
                theirs = r.seg_keys[0:1, near]
            allowed = jnp.logical_and(window, mine == theirs)
            raw = dot_nt(jnp.where(lanes, query_block, 0.0).astype(BF), key_block)
            scores = jnp.where(allowed, raw, MASK_FILL)
            top = jnp.max(scores, axis=1, keepdims=True)
            exponent = jnp.exp(scores - top)
            total = jnp.sum(exponent, axis=1, keepdims=True)
            soft = (exponent * (1.0 / total)).astype(BF)
            r.soft[head] = soft
            gathered = jnp.where(lanes, dot(soft, value_block), gathered)
        r.arranged[own, :] = gathered.astype(BF)

        @pl.when(step == blocks - 1)
        def _():
            arranged = r.arranged[...]
            if mixed:
                natural = restore_rows(arranged, parity_matrix()).astype(BF)
                r.out[...] = jnp.where(r.lanes[...] > 0, natural, arranged)
            else:
                r.out[...] = arranged

    return run_kernel(
        body,
        "attend",
        dict(
            qkv=qkv, left=left, right=right, seg_query=seg_query, seg_keys=seg_keys, flags=flags, lanes=flag_lanes
        ),
        dict(
            out=((rows, width), BF),
            arranged=((rows, width), BF),
            query=((rows, width), BF),
            keys=((slots * BLOCK, width), BF),
            values=((slots * BLOCK, width), BF),
            soft=((heads, rows, keys), BF),
        ),
        {},
        flops=4 * rows * keys * 256 * heads,
        grid=(blocks,),
        specs=dict(soft=pl.BlockSpec((heads, BLOCK, keys), lambda i: (0, i, 0))),
        in_smem=("flags",),
    )


def attend_back(saved, grad_out, flag_lanes, rim, mixed):
    rows, width = grad_out.shape
    heads = width // DH
    blocks = rows // BLOCK
    keys = 3 * BLOCK
    slots = 2 * blocks if mixed else blocks + 2

    def body(r):
        step = pl.program_id(0)

        @pl.when(step == 0)
        def _():
            grad = r.grad_out[...]
            if mixed:
                grad = jnp.where(r.lanes[...] > 0, arrange_rows(grad, parity_matrix()), grad)
            r.grad[...] = grad
            r.grad_keys[...] = jnp.zeros_like(r.grad_keys)
            r.grad_values[...] = jnp.zeros_like(r.grad_values)

        first = step + 2 * (step >= blocks // 2) if mixed else step
        own = pl.ds(pl.multiple_of(step * BLOCK, BLOCK), BLOCK)
        near = pl.ds(pl.multiple_of(first * BLOCK, BLOCK), keys)
        key_block = r.keys[near, :]
        value_block = r.values[near, :]
        query_block = r.query[own, :]
        grad_block = r.grad[own, :]
        product = grad_block.astype(F32) * r.arranged[own, :].astype(F32)
        grad_query = jnp.zeros((BLOCK, width), F32)
        grad_key = jnp.zeros((keys, width), F32)
        grad_value = jnp.zeros((keys, width), F32)
        for head, lanes in enumerate(head_lanes(heads)):
            soft = r.soft[head]
            grad_head = jnp.where(lanes, grad_block, 0.0).astype(BF)
            row_dot = jnp.sum(jnp.where(lanes, product, 0.0), axis=1, keepdims=True)
            grad_soft = dot_nt(grad_head, value_block)
            grad_scores = (soft.astype(F32) * (grad_soft - row_dot)).astype(BF)
            grad_value += dot_tn(soft, grad_head)
            grad_key += dot_tn(grad_scores, jnp.where(lanes, query_block, 0.0).astype(BF))
            grad_query = jnp.where(lanes, dot(grad_scores, key_block), grad_query)
        r.grad_query[own, :] = (grad_query * SCORE_SCALE).astype(BF)
        r.grad_keys[near, :] += grad_key
        r.grad_values[near, :] += grad_value

        @pl.when(step == blocks - 1)
        def _():
            if mixed:
                sort = parity_matrix()
                marked = r.lanes[...] > 0
                arranged = r.grad_query[...]
                natural = restore_rows(arranged, sort).astype(BF)
                r.out_query[...] = jnp.where(marked, natural, arranged)
            else:
                r.out_query[...] = r.grad_query[...]
            for which, held in ((0, r.grad_keys), (1, r.grad_values)):
                total = held[...]
                if mixed:
                    half = blocks * BLOCK
                    edge = jnp.zeros((BLOCK, width), F32)
                    lap = 2 * BLOCK
                    middle = jnp.concatenate(
                        [
                            edge,
                            total[:lap],
                            total[lap:half] + total[half : half + lap],
                            total[half + lap :],
                            edge,
                        ],
                        axis=0,
                    )
                    total = jnp.where(marked, restore_rows(total.astype(BF), sort), middle)
                r.out_left[which] = total[:rim].astype(BF)
                r.out_own[which] = total[rim : rim + rows].astype(BF)
                r.out_right[which] = total[rim + rows :].astype(BF)

    return run_kernel(
        body,
        "attend_back",
        dict(
            grad_out=grad_out,
            arranged=saved.arranged,
            query=saved.query,
            keys=saved.keys,
            values=saved.values,
            soft=saved.soft,
            lanes=flag_lanes,
        ),
        dict(
            out_query=((rows, width), BF),
            out_own=((2, rows, width), BF),
            out_left=((2, rim, width), BF),
            out_right=((2, rim, width), BF),
        ),
        dict(
            grad=pltpu.VMEM((rows, width), BF),
            grad_query=pltpu.VMEM((rows, width), BF),
            grad_keys=pltpu.VMEM((slots * BLOCK, width), F32),
            grad_values=pltpu.VMEM((slots * BLOCK, width), F32),
        ),
        flops=8 * rows * keys * 256 * heads,
        grid=(blocks,),
        specs=dict(soft=pl.BlockSpec((heads, BLOCK, keys), lambda i: (0, i, 0))),
    )


class Partners:
    def __init__(self):
        seq = lax.axis_index("seq")
        here = lax.axis_index("mp")
        self.core = lax.rem(here, 2)
        self.sibling = (seq, here + 1 - 2 * self.core)
        self.across = (seq, lax.rem(here + 2, 4))

    def meet(self):
        barrier = pltpu.get_barrier_semaphore()
        for other in (self.sibling, self.across):
            pl.semaphore_signal(barrier, inc=1, device_id=other, device_id_type=MESH)
        pl.semaphore_wait(barrier, 2)

    def chunk(self, t):
        return pl.ds(pl.multiple_of(t * CHUNK, CHUNK), CHUNK)

    def own(self, t):
        return pl.ds(pl.multiple_of(t * CHUNK + self.core * HALF, HALF), HALF)

    def other(self, t):
        return pl.ds(pl.multiple_of(t * CHUNK + (1 - self.core) * HALF, HALF), HALF)

    def half(self, t):
        return pl.ds(pl.multiple_of(t * HALF, HALF), HALF)


def copy_to(source, target, sent, arrived, device):
    return pltpu.make_async_remote_copy(
        src_ref=source, dst_ref=target, send_sem=sent, recv_sem=arrived, device_id=device, device_id_type=MESH
    )


def exchange_scratch(rows):
    count = rows // CHUNK
    return dict(
        part=pltpu.VMEM((rows, D), BF),
        near=pltpu.VMEM((rows // 2, D), BF),
        pair=pltpu.VMEM((rows // 2, D), BF),
        far=pltpu.VMEM((rows // 2, D), BF),
        core_sent=pltpu.SemaphoreType.DMA((count,)),
        core_came=pltpu.SemaphoreType.DMA((count,)),
        far_sent=pltpu.SemaphoreType.DMA((count,)),
        far_came=pltpu.SemaphoreType.DMA((count,)),
    )


def gather_scratch(rows, width=D, dtype=BF):
    count = rows // CHUNK
    return dict(
        full=pltpu.VMEM((rows, width), dtype),
        sent=pltpu.SemaphoreType.DMA((count,)),
        came=pltpu.SemaphoreType.DMA((count,)),
    )


class Exchange:
    def __init__(self, who, refs):
        self.who, self.r = who, refs

    def core_copy(self, t):
        who, r = self.who, self.r
        return copy_to(
            r.part.at[who.other(t), :], r.near.at[who.half(t), :], r.core_sent.at[t], r.core_came.at[t], who.sibling
        )

    def far_copy(self, t):
        who, r = self.who, self.r
        rows = who.half(t)
        return copy_to(r.pair.at[rows, :], r.far.at[rows, :], r.far_sent.at[t], r.far_came.at[t], who.across)

    def give(self, t, part):
        self.r.part[self.who.chunk(t), :] = part.astype(BF)
        self.core_copy(t).start()

    def add(self, t):
        who, r = self.who, self.r
        self.core_copy(t).wait_recv()
        pair = r.part[who.own(t), :].astype(F32) + r.near[who.half(t), :].astype(F32)
        r.pair[who.half(t), :] = pair.astype(BF)
        self.far_copy(t).start()

    def take(self, t):
        who, r = self.who, self.r
        self.far_copy(t).wait_recv()
        return r.pair[who.half(t), :].astype(F32) + r.far[who.half(t), :].astype(F32)

    def finish(self, t):
        self.core_copy(t).wait_send()
        self.far_copy(t).wait_send()


class Gather:
    def __init__(self, who, refs):
        self.who, self.r = who, refs

    def copy(self, rows, t):
        r = self.r
        return copy_to(r.full.at[rows, :], r.full.at[rows, :], r.sent.at[t], r.came.at[t], self.who.sibling)

    def give(self, t, value):
        rows = self.who.own(t)
        self.r.full[rows, :] = value.astype(self.r.full.dtype)
        self.copy(rows, t).start()

    def take(self, t):
        self.wait(t)
        return self.r.full[self.who.chunk(t), :]

    def wait(self, t):
        self.copy(self.who.other(t), t).wait_recv()

    def finish(self, t):
        self.copy(self.who.own(t), t).wait_send()


def pick(r, prefix):
    start = prefix + "_"
    return SimpleNamespace(
        **{key[len(start) :]: value for key, value in vars(r).items() if key.startswith(start)}
    )


def prefixed(prefix, entries):
    return {prefix + "_" + key: value for key, value in entries.items()}


def run_stages(count, stages):
    last = max(delay for delay, _ in stages)

    def step(i, carry):
        for delay, stage in stages:

            @pl.when(jnp.logical_and(i >= delay, i < count + delay))
            def _(delay=delay, stage=stage):
                stage(i - delay)

        return carry

    lax.fori_loop(0, count + last, step, 0)


def norm_forward(total, gain, shift):
    center = total - jnp.mean(total, axis=1, keepdims=True)
    spread = jnp.mean(center * center, axis=1, keepdims=True)
    inverse = lax.rsqrt(spread + NORM_EPSILON)
    unit = center * inverse
    return unit, inverse, unit * gain + shift


def norm_back(grad, unit, inverse, gain):
    grad_unit = grad * gain
    first = jnp.mean(grad_unit, axis=1, keepdims=True)
    second = jnp.mean(grad_unit * unit, axis=1, keepdims=True)
    return inverse * (grad_unit - first - unit * second)


def column_sum(value):
    return jnp.sum(value, axis=0, keepdims=True)


def split_two(value):
    high = value.astype(BF)
    return high, (value - high.astype(F32)).astype(BF)


def unturned(value, turn):
    high, rest = split_two(value)
    return dot_nt(high, turn) + dot_nt(rest, turn)


def wide(column):
    return jnp.broadcast_to(column, (column.shape[0], 128))


def forward_refs(rows, width, units):
    return dict(
        unit_one=((rows // 2, D), F32),
        inverse_one=((rows // 2, 128), F32),
        unit_two=((rows // 2, D), F32),
        inverse_two=((rows // 2, 128), F32),
        hidden=((rows, units), BF),
        slope=((rows, units), BF),
    )


def forward_stages(r, who, first, second, spread):
    def project(t):
        first.give(t, dot_nt(r.mixed[who.chunk(t), :], r.attn[3]))

    def middle(t):
        rows = who.own(t) if r.residual.shape[0] == r.mixed.shape[0] else who.half(t)
        total = r.residual[rows, :].astype(F32) + first.take(t) + r.shared[0:1, :]
        unit, inverse, normed = norm_forward(total, r.shared[1:2, :], r.shared[2:3, :])
        r.unit_one[who.half(t), :] = unit
        r.inverse_one[who.half(t), :] = wide(inverse)
        r.normed[who.half(t), :] = normed
        spread.give(t, normed)

    def feed(t):
        pre = dot(spread.take(t), r.ffn[0]) + r.hidden_bias[...]
        chance = 0.5 + 0.5 * lax.erf(pre * (0.5**0.5))
        hidden = (pre * chance).astype(BF)
        r.hidden[who.chunk(t), :] = hidden
        bell = jnp.exp(-0.5 * pre * pre) * 0.3989422804014327
        r.slope[who.chunk(t), :] = (chance + pre * bell).astype(BF)
        second.give(t, dot_nt(hidden, r.ffn[1]))

    def final(t):
        total = r.normed[who.half(t), :] + second.take(t) + r.shared[3:4, :]
        unit, inverse, result = norm_forward(total, r.shared[4:5, :], r.shared[5:6, :])
        r.unit_two[who.half(t), :] = unit
        r.inverse_two[who.half(t), :] = wide(inverse)
        return unit, inverse, result

    return project, middle, feed, final


def backward_stages(r, who, ends, third, mids):
    def enter(t, grad, unit, inverse):
        grad_total = norm_back(grad, unit, inverse, r.shared[4:5, :])
        r.vectors[3:4, :] += column_sum(grad_total)
        r.vectors[4:5, :] += column_sum(grad * unit)
        r.vectors[5:6, :] += column_sum(grad)
        r.kept[who.half(t), :] = grad_total
        ends.give(t, grad_total)

    def feed_back(t):
        rows = who.chunk(t)
        grad = ends.take(t)
        hidden = r.hidden[rows, :]
        grad_pre = (dot(grad, r.ffn[1]) * r.slope[rows, :].astype(F32)).astype(BF)
        r.units[0:1, :] += column_sum(grad_pre.astype(F32))
        third.give(t, dot_nt(grad_pre, r.ffn[0]))
        r.sum_up[...] += dot_tn(r.spread_full[rows, :], grad_pre)
        r.sum_down[...] += dot_tn(grad, hidden)

    def leave(t):
        grad = r.kept[who.half(t), :] + third.take(t)
        unit = r.unit_one[who.half(t), :]
        grad_total = norm_back(grad, unit, r.inverse_one[who.half(t), 0:1], r.shared[1:2, :])
        r.vectors[0:1, :] += column_sum(grad_total)
        r.vectors[1:2, :] += column_sum(grad * unit)
        r.vectors[2:3, :] += column_sum(grad)
        r.grad_one[who.half(t), :] = grad_total
        mids.give(t, grad_total)

    def project_back(t):
        rows = who.chunk(t)
        grad = mids.take(t)
        r.grad_mixed[rows, :] = dot(grad, r.attn[3]).astype(BF)
        r.sum_out[...] += dot_tn(grad, r.mixed[rows, :])

    return enter, feed_back, leave, project_back


def clear(*refs):
    for ref in refs:
        ref[...] = jnp.zeros_like(ref)


def finish_all(count, parts):
    def step(t, carry):
        for part in parts:
            part.finish(t)
        return carry

    lax.fori_loop(0, count, step, 0)


def middle_forward(mixed, attn, ffn, residual, shared, hidden_bias, next_attn, next_bias):
    rows, width = mixed.shape
    units = ffn.shape[2]
    count = rows // CHUNK

    def body(r):
        who = Partners()
        first, second = Exchange(who, pick(r, "first")), Exchange(who, pick(r, "second"))
        spread = Gather(who, SimpleNamespace(full=r.spread_full, sent=r.spread_sent, came=r.spread_came))
        last = Gather(who, SimpleNamespace(full=r.last_full, sent=r.last_sent, came=r.last_came))
        who.meet()
        project, middle, feed, final = forward_stages(r, who, first, second, spread)

        def close(t):
            _, _, result = final(t)
            r.result[who.half(t), :] = result
            last.give(t, result)

        def next_project(t):
            low = last.take(t)
            for which in range(3):
                value = dot(low, r.next_attn[which]) + r.next_bias[which : which + 1, :]
                r.qkv[which, who.chunk(t), :] = value.astype(BF)

        run_stages(
            count,
            [
                (5, second.add),
                (1, first.add),
                (7, close),
                (3, middle),
                (8, next_project),
                (4, feed),
                (0, project),
            ],
        )
        finish_all(count, (first, second, spread, last))

    outputs = forward_refs(rows, width, units)
    outputs.update(
        spread_full=((rows, D), BF), last_full=((rows, D), BF), result=((rows // 2, D), F32), qkv=((3, rows, width), BF)
    )
    scratch = dict(normed=pltpu.VMEM((rows // 2, D), F32))
    scratch.update(prefixed("first", exchange_scratch(rows)))
    scratch.update(prefixed("second", exchange_scratch(rows)))
    for key in ("spread", "last"):
        for part in ("sent", "came"):
            scratch[key + "_" + part] = pltpu.SemaphoreType.DMA((count,))
    return run_kernel(
        body,
        "middle_forward",
        dict(
            mixed=mixed,
            attn=attn,
            ffn=ffn,
            residual=residual,
            shared=shared,
            hidden_bias=hidden_bias,
            next_attn=next_attn,
            next_bias=next_bias,
        ),
        outputs,
        scratch,
        collective=1,
        flops=2 * rows * D * (4 * width + 2 * units),
    )


def turning(mixed, attn, ffn, residual, shared, hidden_bias, cotangent, turn):
    rows, width = mixed.shape
    units = ffn.shape[2]
    count = rows // CHUNK

    def body(r):
        who = Partners()
        first, second = Exchange(who, pick(r, "first")), Exchange(who, pick(r, "second"))
        third = Exchange(who, pick(r, "third"))
        spread = Gather(who, pick(r, "spread"))
        ends, mids = Gather(who, pick(r, "ends")), Gather(who, pick(r, "mids"))
        out = Gather(who, SimpleNamespace(full=r.output, sent=r.out_sent, came=r.out_came))
        who.meet()
        clear(r.vectors, r.units, r.sum_up, r.sum_down, r.sum_out)
        project, middle, feed, final = forward_stages(r, who, first, second, spread)
        enter, feed_back, leave, project_back = backward_stages(r, who, ends, third, mids)

        def close(t):
            unit, inverse, result = final(t)
            grad = dot(r.cotangent[who.own(t), :], r.turn[...])
            enter(t, grad, unit, inverse)
            out.give(t, unturned(result, r.turn[...]))

        run_stages(
            count,
            [
                (9, third.add),
                (5, second.add),
                (1, first.add),
                (11, leave),
                (7, close),
                (3, middle),
                (12, project_back),
                (8, feed_back),
                (4, feed),
                (0, project),
            ],
        )

        def arrive(t, carry):
            out.wait(t)
            return carry

        lax.fori_loop(0, count, arrive, 0)
        finish_all(count, (first, second, third, spread, ends, mids, out))
        r.weights[:, :units] = r.sum_up[...].astype(BF)
        r.weights[:, units : 2 * units] = r.sum_down[...].astype(BF)
        r.weights[:, 2 * units :] = r.sum_out[...].astype(BF)

    outputs = dict(
        output=((rows, D), F32),
        weights=((D, 2 * units + width), BF),
        grad_one=((rows // 2, D), F32),
        grad_mixed=((rows, width), BF),
        vectors=((8, D), F32),
        units=((8, units), F32),
    )
    scratch = dict(
        normed=pltpu.VMEM((rows // 2, D), F32),
        kept=pltpu.VMEM((rows // 2, D), F32),
        sum_up=pltpu.VMEM((D, units), F32),
        sum_down=pltpu.VMEM((D, units), F32),
        sum_out=pltpu.VMEM((D, width), F32),
        out_sent=pltpu.SemaphoreType.DMA((count,)),
        out_came=pltpu.SemaphoreType.DMA((count,)),
    )
    for key, (shape, dtype) in forward_refs(rows, width, units).items():
        scratch[key] = pltpu.VMEM(shape, dtype)
    for key in ("first", "second", "third"):
        scratch.update(prefixed(key, exchange_scratch(rows)))
    for key in ("spread", "ends", "mids"):
        scratch.update(prefixed(key, gather_scratch(rows)))
    return run_kernel(
        body,
        "turning",
        dict(
            mixed=mixed,
            attn=attn,
            ffn=ffn,
            residual=residual,
            shared=shared,
            hidden_bias=hidden_bias,
            cotangent=cotangent,
            turn=turn,
        ),
        outputs,
        scratch,
        collective=2,
        flops=2 * rows * D * (3 * width + 6 * units),
    )


def projection_back_stage(r, who, exchange):
    rows, width = r.grad_query.shape
    rim = r.from_left.shape[1]

    def gather_parts():
        own = r.grad_own[...].astype(F32)
        for which in range(2):
            r.grad_pair[which] = r.grad_own[which]
            head = own[which, :rim] + r.from_left[which].astype(F32)
            r.grad_pair[which, :rim, :] = head.astype(BF)
            held = r.grad_pair[which, rows - rim :, :].astype(F32)
            r.grad_pair[which, rows - rim :, :] = (held + r.from_right[which].astype(F32)).astype(BF)

    def stage(t):
        chunk = who.chunk(t)
        parts = [r.grad_query[chunk, :], r.grad_pair[0, chunk, :], r.grad_pair[1, chunk, :]]
        low = r.low[chunk, :]
        part = sum(dot_nt(value, r.next_attn[which]) for which, value in enumerate(parts))
        exchange.give(t, part)
        for which, value in enumerate(parts):
            r.sum_three[which] += dot_tn(low, value)
        r.biases[0:1, :] += column_sum(parts[0].astype(F32))
        r.biases[1:2, :] += column_sum(parts[2].astype(F32))

    return gather_parts, stage


def middle_backward(back, from_left, from_right, next_attn, grad_above, low, saved, mixed, attn, ffn, shared):
    rows, width = mixed.shape
    units = ffn.shape[2]
    count = rows // CHUNK

    def body(r):
        who = Partners()
        zeroth, third = Exchange(who, pick(r, "zeroth")), Exchange(who, pick(r, "third"))
        ends, mids = Gather(who, pick(r, "ends")), Gather(who, pick(r, "mids"))
        who.meet()
        clear(r.vectors, r.units, r.biases, r.sum_up, r.sum_down, r.sum_out, r.sum_three)
        gather_parts, inputs_back = projection_back_stage(r, who, zeroth)
        gather_parts()
        enter, feed_back, leave, project_back = backward_stages(r, who, ends, third, mids)

        def start(t):
            half = who.half(t)
            enter(t, r.grad_above[half, :] + zeroth.take(t), r.unit_two[half, :], r.inverse_two[half, 0:1])

        run_stages(
            count,
            [
                (5, third.add),
                (1, zeroth.add),
                (7, leave),
                (3, start),
                (8, project_back),
                (4, feed_back),
                (0, inputs_back),
            ],
        )
        finish_all(count, (zeroth, third, ends, mids))
        r.weights[:, :units] = r.sum_up[...].astype(BF)
        r.weights[:, units : 2 * units] = r.sum_down[...].astype(BF)
        tail = jnp.concatenate([r.sum_three[0], r.sum_three[1], r.sum_three[2], r.sum_out[...]], axis=1)
        r.weights[:, 2 * units :] = tail.astype(BF)

    outputs = dict(
        weights=((D, 2 * units + 4 * width), BF),
        grad_one=((rows // 2, D), F32),
        grad_mixed=((rows, width), BF),
        vectors=((8, D), F32),
        units=((8, units), F32),
        biases=((8, width), F32),
    )
    scratch = dict(
        kept=pltpu.VMEM((rows // 2, D), F32),
        grad_pair=pltpu.VMEM((2, rows, width), BF),
        sum_up=pltpu.VMEM((D, units), F32),
        sum_down=pltpu.VMEM((D, units), F32),
        sum_out=pltpu.VMEM((D, width), F32),
        sum_three=pltpu.VMEM((3, D, width), F32),
    )
    for key in ("zeroth", "third"):
        scratch.update(prefixed(key, exchange_scratch(rows)))
    for key in ("ends", "mids"):
        scratch.update(prefixed(key, gather_scratch(rows)))
    return run_kernel(
        body,
        "middle_backward",
        dict(
            grad_query=back.out_query,
            grad_own=back.out_own,
            from_left=from_left,
            from_right=from_right,
            next_attn=next_attn,
            grad_above=grad_above,
            low=low,
            unit_one=saved.unit_one,
            inverse_one=saved.inverse_one,
            unit_two=saved.unit_two,
            inverse_two=saved.inverse_two,
            hidden=saved.hidden,
            slope=saved.slope,
            spread_full=saved.spread_full,
            mixed=mixed,
            attn=attn,
            ffn=ffn,
            shared=shared,
        ),
        outputs,
        scratch,
        collective=3,
        flops=2 * rows * D * (8 * width + 4 * units),
    )


def ending(back, from_left, from_right, next_attn, grad_above, low, turn):
    rows, width = back.out_query.shape
    count = rows // CHUNK

    def body(r):
        who = Partners()
        zeroth = Exchange(who, pick(r, "zeroth"))
        out = Gather(who, SimpleNamespace(full=r.output, sent=r.out_sent, came=r.out_came))
        who.meet()
        clear(r.biases, r.sum_three)
        gather_parts, inputs_back = projection_back_stage(r, who, zeroth)
        gather_parts()

        def close(t):
            out.give(t, unturned(r.grad_above[who.half(t), :] + zeroth.take(t), r.turn[...]))

        run_stages(count, [(1, zeroth.add), (3, close), (0, inputs_back)])

        def arrive(t, carry):
            out.wait(t)
            return carry

        lax.fori_loop(0, count, arrive, 0)
        finish_all(count, (zeroth, out))
        tail = jnp.concatenate([r.sum_three[0], r.sum_three[1], r.sum_three[2]], axis=1)
        r.weights[...] = tail.astype(BF)

    outputs = dict(output=((rows, D), F32), weights=((D, 3 * width), BF), biases=((8, width), F32))
    scratch = dict(
        grad_pair=pltpu.VMEM((2, rows, width), BF),
        sum_three=pltpu.VMEM((3, D, width), F32),
        out_sent=pltpu.SemaphoreType.DMA((count,)),
        out_came=pltpu.SemaphoreType.DMA((count,)),
    )
    scratch.update(prefixed("zeroth", exchange_scratch(rows)))
    return run_kernel(
        body,
        "ending",
        dict(
            grad_query=back.out_query,
            grad_own=back.out_own,
            from_left=from_left,
            from_right=from_right,
            next_attn=next_attn,
            grad_above=grad_above,
            low=low,
            turn=turn,
        ),
        outputs,
        scratch,
        collective=4,
        flops=2 * rows * D * 6 * width,
    )


def beginning(activations, turn, attn, bias):
    rows = activations.shape[0]
    width = attn.shape[2]

    def body(r):
        for start in range(0, rows, BLOCK):
            chunk = pl.ds(start, BLOCK)
            low = dot(r.activations[chunk, :], r.turn[...]).astype(BF)
            r.low[chunk, :] = low
            for which in range(3):
                value = dot(low, r.attn[which]) + r.bias[which : which + 1, :]
                r.qkv[which, chunk, :] = value.astype(BF)

    return run_kernel(
        body,
        "beginning",
        dict(activations=activations, turn=turn, attn=attn, bias=bias),
        dict(low=((rows, D), BF), qkv=((3, rows, width), BF)),
        {},
        flops=2 * rows * D * (D + 3 * width),
    )


def to_next(block):
    count = lax.axis_size("seq")
    return lax.ppermute(block, "seq", [(i, i + 1) for i in range(count - 1)])


def to_previous(block):
    count = lax.axis_size("seq")
    return lax.ppermute(block, "seq", [(i + 1, i) for i in range(count - 1)])


def rotate_update(weight, grad_now, first, second, running_average, basis, rates):
    turn = basis[:, :, 0, 0]
    turned = jnp.einsum("lmre,lmec->lmrc", grad_now, turn)
    first_new = BETA_FIRST * first + (1.0 - BETA_FIRST) * turned
    second_new = BETA_SECOND * second + (1.0 - BETA_SECOND) * turned * turned
    direction = (
        first_new
        / (1.0 - BETA_FIRST**STEP)
        / (jnp.sqrt(second_new / (1.0 - BETA_SECOND**STEP)) + ADAM_EPSILON)
    )
    back = jnp.einsum("lmrc,lmec->lmre", direction, turn)
    weight_new = weight - rates[None, :, None, None] * (back + DECAY_RATE * weight)
    average_new = AVERAGE_RATE * running_average + (1.0 - AVERAGE_RATE) * weight_new
    return (weight_new, first_new, second_new, average_new)


def vector_update(current, grad_now, first, second):
    first_new = BETA_FIRST * first + (1.0 - BETA_FIRST) * grad_now
    second_new = BETA_SECOND * second + (1.0 - BETA_SECOND) * grad_now * grad_now
    direction = (
        first_new
        / (1.0 - BETA_FIRST**STEP)
        / (jnp.sqrt(second_new / (1.0 - BETA_SECOND**STEP)) + ADAM_EPSILON)
    )
    return (current - VECTOR_RATE * direction, first_new, second_new)


def scatter_sum(grads):
    return lax.psum_scatter(grads, "seq", scatter_dimension=0, tiled=True).astype(F32)


def local(
    activations,
    cotangent,
    segments,
    dilated_heads,
    owners,
    attn_weights,
    attn_first,
    attn_second,
    attn_average,
    attn_basis,
    ffn_weights,
    ffn_first,
    ffn_second,
    ffn_average,
    ffn_basis,
    split_biases,
    split_first,
    split_second,
    shared_vectors,
    shared_first,
    shared_second,
):
    slot_count = lax.axis_size("seq")
    rows = activations.shape[0]
    width = attn_weights.shape[3]
    units = ffn_weights.shape[3]
    heads = width // DH
    attn_low, ffn_low = attn_weights.astype(BF), ffn_weights.astype(BF)
    attn, ffn = [], []
    for layer in range(2):
        attn.append(lax.all_gather(attn_low[layer], "seq", axis=1, tiled=True))
        ffn.append(lax.all_gather(ffn_low[layer], "seq", axis=1, tiled=True))
    block = D // slot_count
    place = (owners[:, None] * block + jnp.arange(block, dtype=jnp.int32)[None, :]).reshape(D)
    turn = (place[:, None] == jnp.arange(D, dtype=jnp.int32)[None, :]).astype(BF)
    turn_wide = turn.astype(F32)
    shared = jnp.dot(shared_vectors.reshape(12, D), turn_wide, precision=HIGHEST_PRECISION).reshape(2, 6, D)

    seg_pad = jnp.concatenate([to_next(segments[rows - 2 * WIN :]), segments, to_previous(segments[: 2 * WIN])])
    seg_keys = [
        seg_pad[WIN : rows + 3 * WIN][None],
        jnp.stack(
            [
                jnp.concatenate([seg_pad[WIN : rows + WIN], seg_pad[rows - WIN : 2 * rows - WIN]]),
                seg_pad.reshape(4, WIN, 2).transpose(2, 0, 1).reshape(8 * WIN),
            ]
        ),
    ]
    seg_query = [
        segments[:, None],
        jnp.stack([segments, segments.reshape(2, WIN, 2).transpose(2, 0, 1).reshape(rows)], axis=1),
    ]
    heads_here = lax.axis_index("mp") * heads + jnp.arange(heads, dtype=jnp.int32)
    flags = jnp.any(heads_here[:, None] == dilated_heads[None, :], axis=1).astype(jnp.int32)
    flag_lanes = jnp.repeat(flags, DH)[None, :]

    def biases_of(layer):
        both = split_biases[layer, 0, : 2 * width].reshape(2, width)
        return jnp.stack([both[0], jnp.zeros_like(both[0]), both[1]])

    def hidden_bias(layer):
        return split_biases[layer, :, 2 * width :]

    def halo(qkv, rim):
        return to_next(qkv[1:, rows - rim :]), to_previous(qkv[1:, :rim])

    begin = beginning(activations, turn, attn[0], biases_of(0))
    left, right = halo(begin.qkv, WIN)
    near = attend(begin.qkv, left, right, seg_query[0], seg_keys[0], flags, flag_lanes, False)
    mid = middle_forward(
        near.out, attn[0], ffn[0], begin.low, shared[0], hidden_bias(0), attn[1], biases_of(1)
    )
    left, right = halo(mid.qkv, 2 * WIN)
    far = attend(mid.qkv, left, right, seg_query[1], seg_keys[1], flags, flag_lanes, True)
    top = turning(far.out, attn[1], ffn[1], mid.result, shared[1], hidden_bias(1), cotangent, turn)
    far_back = attend_back(far, top.grad_mixed, flag_lanes, 2 * WIN, True)
    from_left, from_right = to_next(far_back.out_right), to_previous(far_back.out_left)
    low = middle_backward(
        far_back, from_left, from_right, attn[1], top.grad_one, mid.last_full, mid, near.out, attn[0], ffn[0], shared[0]
    )
    near_back = attend_back(near, low.grad_mixed, flag_lanes, WIN, False)
    from_left, from_right = to_next(near_back.out_right), to_previous(near_back.out_left)
    end = ending(near_back, from_left, from_right, attn[0], low.grad_one, begin.low, turn)

    top_sum, low_sum, end_sum = scatter_sum(top.weights), scatter_sum(low.weights), scatter_sum(end.weights)

    def columns(value, start, size, count):
        return [value[:, start + i * size : start + (i + 1) * size] for i in range(count)]

    attn_grads = jnp.stack(
        [
            jnp.stack(columns(end_sum, 0, width, 3) + columns(low_sum, 2 * units + 3 * width, width, 1)),
            jnp.stack(columns(low_sum, 2 * units, width, 3) + columns(top_sum, 2 * units, width, 1)),
        ]
    )
    ffn_grads = jnp.stack(
        [jnp.stack(columns(low_sum, 0, units, 2)), jnp.stack(columns(top_sum, 0, units, 2))]
    )
    shared_grads = lax.psum(jnp.stack([low.vectors[:6], top.vectors[:6]]), ("seq", "mp")) * 0.5
    shared_grads = jnp.dot(
        shared_grads.reshape(12, D), turn_wide.T, precision=HIGHEST_PRECISION
    ).reshape(2, 6, D)
    split_grads = lax.psum(
        jnp.stack(
            [
                jnp.concatenate([end.biases[0], end.biases[1], low.units[0]]),
                jnp.concatenate([low.biases[0], low.biases[1], top.units[0]]),
            ]
        )[:, None, :],
        "seq",
    )
    first_seq = lax.axis_index("seq") == 0
    first_both = jnp.logical_and(first_seq, lax.axis_index("mp") == 0)
    local_sum = jnp.sum(attn_grads * attn_grads) + jnp.sum(ffn_grads * ffn_grads)
    local_sum = (
        local_sum
        + jnp.where(first_seq, jnp.sum(split_grads * split_grads), 0.0)
        + jnp.where(first_both, jnp.sum(shared_grads * shared_grads), 0.0)
    )
    grad_norm = jnp.sqrt(lax.psum(local_sum, ("seq", "mp")))
    factor = CLIP_LEVEL / jnp.maximum(grad_norm, CLIP_LEVEL)
    attn_rates = jnp.array([0.5 * D ** (-0.5)] * 3 + [0.5 * (WIN / D) ** 0.5], F32)
    ffn_rates = jnp.array([0.5 * D ** (-0.5), 0.5 * FF ** (-0.5)], F32)
    attn_out = rotate_update(
        attn_weights, factor * attn_grads, attn_first, attn_second, attn_average, attn_basis, attn_rates
    )
    ffn_out = rotate_update(
        ffn_weights, factor * ffn_grads, ffn_first, ffn_second, ffn_average, ffn_basis, ffn_rates
    )
    split_out = vector_update(split_biases, factor * split_grads, split_first, split_second)
    shared_out = vector_update(shared_vectors, factor * shared_grads, shared_first, shared_second)
    return (
        top.output,
        end.output,
        attn_out[0],
        attn_out[1],
        attn_out[2][:, :3],
        attn_out[2][:, 3],
        attn_out[3],
        ffn_out[0],
        ffn_out[1],
        ffn_out[2],
        ffn_out[3],
        split_out[0],
        split_out[1],
        split_out[2],
        shared_out[0],
        shared_out[1],
        shared_out[2],
        grad_norm,
    )


def solution(mesh):
    placed = (
        P("seq", None),
        P("seq", None),
        P("seq"),
        P(),
        P(),
        P(None, None, "seq", "mp"),
        P(None, None, "seq", "mp"),
        P(None, None, "seq", "mp"),
        P(None, None, "seq", "mp"),
        P(None, None, "seq", "mp", None, None),
        P(None, None, "seq", "mp"),
        P(None, None, "seq", "mp"),
        P(None, None, "seq", "mp"),
        P(None, None, "seq", "mp"),
        P(None, None, "seq", "mp", None, None),
        P(None, "mp", None),
        P(None, "mp", None),
        P(None, "mp", None),
        P(),
        P(),
        P(),
    )
    return jax.shard_map(
        local,
        mesh=mesh,
        in_specs=placed,
        out_specs=(
            P("seq", None),
            P("seq", None),
            P(None, None, "seq", "mp"),
            P(None, None, "seq", "mp"),
            P(None, None, "seq", "mp"),
            P(None, "seq", "mp"),
            P(None, None, "seq", "mp"),
            P(None, None, "seq", "mp"),
            P(None, None, "seq", "mp"),
            P(None, None, "seq", "mp"),
            P(None, None, "seq", "mp"),
            P(None, "mp", None),
            P(None, "mp", None),
            P(None, "mp", None),
            P(),
            P(),
            P(),
            P(),
        ),
        check_vma=False,
    )
```

time: 1490 us -> 780 us (0.52)
  waiting for transfers between devices: 770 us -> 311 us
  Pallas kernels: 0 us -> 254 us
  local copies, waits for them, and re-layouts: 217 us -> 26.1 us
  matrix products: 189 us -> 15.4 us
  other arithmetic: 152 us -> 10.5 us
  loops' own time: 26.1 us -> 0 us
  blocking collectives: 78.1 us -> 104 us
    psum x8 -> x0, waiting for transfers between devices: 409 us -> none  [the longest x4 248 us: join_grads(): return lax.psum(term, 'mp')]
    pallas_call x0 -> x9, Pallas kernels: none -> 254 us  [run_kernel(): pl.pallas_call(kernel, out_shape=shapes, in_specs=[spec_of(key) for key i...]
    dot_general x55 -> x6, matrix products: 188 us -> 15.4 us  [the longest x2 7 us: rotate_update(): turned = jnp.einsum('lmre,lmec->lmrc', grad_now, turn)]
    reduce_sum x25 -> x0, other arithmetic: 56.5 us -> none  [the longest x8 19.7 us: normalize_layer(): center = values - jnp.mean(values, axis=-1, keepdims=True)]
    dynamic_update_slice x8 -> x0, local copies, waits for them, and re-layouts: 39 us -> none  [the longest x4 36.2 us: one_step(): lax.dynamic_update_slice_in_dim(carry, current + update, first_row, 0)]
    unnamed x315 -> x89, local copies, waits for them, and re-layouts: 40.7 us -> 10.4 us
    gather x6 -> x0, local copies, waits for them, and re-layouts: 29.6 us -> none  [the longest x4 20 us: to_slots(): return jnp.take(blocks, inverse, axis=1).reshape(grads.shape)]
    all_gather x2 -> x4, waiting for transfers between devices: 132 us -> 104 us  [the longest x2 53.7 us: local(): ffn.append(lax.all_gather(ffn_low[layer], 'seq', axis=1, tiled=True))]
  transfers between devices with their start and end apart: 22 -> 17, of which waited for: 16 -> 11; matrix products, arithmetic and copies ran while one was open for 7% -> 3% of each run, Pallas kernels for 0% -> 10%
where the time goes in v1:
time: 780 us; the launch traced here: 772 us
  waiting for transfers between devices  311 us (40%)
  Pallas kernels  254 us (33%)
  blocking collectives  104 us (13%)
  starting transfers between devices  31.3 us (4%)
  local copies, waits for them, and re-layouts  26.1 us (3%)
  between operations  19.8 us (3%)
  matrix products  15.4 us (2%)
  other arithmetic  10.5 us (1%)
    pallas_call x9, Pallas kernels, run_kernel(): pl.pallas_call(kernel, out_shape=shapes, in_specs=[spec_of(key) for key i...  254 us
    reduce_scatter x3, waiting for transfers between devices, scatter_sum(): lax.psum_scatter(grads, 'seq', scatter_dimension=0, tiled=True).astype(F32)  145 us
    all_gather x2, waiting for transfers between devices, local(): ffn.append(lax.all_gather(ffn_low[layer], 'seq', axis=1, tiled=True))  53.7 us
    all_gather x2, waiting for transfers between devices, local(): attn.append(lax.all_gather(attn_low[layer], 'seq', axis=1, tiled=True))  50.2 us
    ppermute x5, waiting for transfers between devices, to_next(): return lax.ppermute(block, 'seq', [(i, i + 1) for i in range(count - 1)])  47.9 us
    psum x1, blocking collectives, local(): lax.psum(jnp.stack([low.vectors[:6], top.vectors[:6]]), ('seq', 'mp')) * 0.5  42.6 us
    psum x1, blocking collectives, local(): grad_norm = jnp.sqrt(lax.psum(local_sum, ('seq', 'mp')))  40.5 us
    ppermute x5, starting transfers between devices, to_next(): return lax.ppermute(block, 'seq', [(i, i + 1) for i in range(count - 1)])  24.4 us
  transfers between devices with their start and end apart: 17, of which 11 were waited for; matrix products, arithmetic and copies ran while one was open for 3% of the time, Pallas kernels for 10%

profile of v1, /device:TPU:0, one launch (start us, length us, event | category | flops | bytes accessed | tf_op | source)
XLA Modules:
  0.0 772.4 jit_solution(14830987593362642328)
XLA Ops:
  12.6 5.5 collective-permute-start.2
  24.8 33.0 %all-gather.9.cloned.1.call-done = bf16[1,4,768,192]{3,2,1,0:T(8,128)(2,1)} async-done(((bf16[1,4,96,192]{3,2,1,0:T(8,128)(2,1)}), bf16[1,4,768,192]{3,2,1,0:T(8,128)(2,1)}) %all-gather.9.cloned.1.call-update) | async-done | bytes 1179664 | tf_op jit(solution)/shard_map/all_gather | solution.py:1011
  57.8 6.3 beginning.1
  66.5 4.6 collective-permute-start
  71.7 4.9 collective-permute-done.1.refs_2_
  76.6 4.5 collective-permute-done.refs_1_
  81.9 11.3 %attend.2 = (bf16[1024,192]{1,0:T(8,128)(2,1)}, bf16[1024,192]{1,0:T(8,128)(2,1)}, bf16[1024,192]{1,0:T(8,128)(2,1)}, bf16[1536,192]{1,0:T(8,128)(2,1)}, bf16[15...) custom-call(bf16[3,1024,192]{2,1,0:T(8,128)(2,1)} %get-tuple-element.65.refs_0_, bf16[2,256,192]{2,1,0:T(8,128)(2,1)} %copy-done.35, ...), custom_call_target="tpu_custom_call" | custom-call | flops 2415919104 | bytes 8661772 | tf_op jit(solution)/shard_map/attend/pallas_call | solution.py:69
  93.2 17.2 %all-gather.13.cloned.1.call-done = bf16[1,4,768,192]{3,2,1,0:T(8,128)(2,1)} async-done(((bf16[1,4,96,192]{3,2,1,0:T(8,128)(2,1)}), bf16[1,4,768,192]{3,2,1,0:T(8,128)(2,1)}) %all-gather.13.cloned.1.call-update) | async-done | bytes 1179664 | tf_op jit(solution)/shard_map/all_gather | solution.py:1011
  110.4 53.7 %all-gather.11.cloned.1.call-done = bf16[1,2,768,768]{3,2,1,0:T(8,128)(2,1)} async-done(((bf16[1,2,96,768]{3,2,1,0:T(8,128)(2,1)}), bf16[1,2,768,768]{3,2,1,0:T(8,128)(2,1)}) %all-gather.11.cloned.1.call-update) | async-done | bytes 2359312 | tf_op jit(solution)/shard_map/all_gather | solution.py:1012
  164.1 48.8 %middle_forward.1 = (f32[512,768]{1,0:T(8,128)}, f32[512,128]{1,0:T(8,128)}, f32[512,768]{1,0:T(8,128)}, f32[512,128]{1,0:T(8,128)}, bf16[1024,768]{1,0:T(8,128)...) custom-call(bf16[1024,192]{1,0:T(8,128)(2,1)} %get-tuple-element.66., ...), custom_call_target="tpu_custom_call" | custom-call | flops 3623878656 | bytes 19422464 | tf_op jit(solution)/shard_map/middle_forward/pallas_call | solution.py:69
  215.5 5.5 collective-permute-start.4
  223.4 7.3 collective-permute-done.5.refs_2_
  230.7 10.0 %collective-permute-done.4.refs_1_ = bf16[2,512,192]{2,1,0:T(8,128)(2,1)} collective-permute-done((bf16[2,512,192]{2,1,0:T(8,128)(2,1)S(1)}, bf16[2,512,192]{2,1,0:T(8,128)(2,1)}, u32[]{:S(2)}, u32[]{:S(2)}) %collective-permute-start.4) | collective-permute-done | bytes 393248 | tf_op jit(solution)/shard_map/ppermute | solution.py:941
  240.7 13.2 %attend.3 = (bf16[1024,192]{1,0:T(8,128)(2,1)}, bf16[1024,192]{1,0:T(8,128)(2,1)}, bf16[1024,192]{1,0:T(8,128)(2,1)}, bf16[2048,192]{1,0:T(8,128)(2,1)}, bf16[20...) custom-call(bf16[3,1024,192]{2,1,0:T(8,128)(2,1)} %get-tuple-element.68.refs_0_, ...), custom_call_target="tpu_custom_call" | custom-call | flops 2415919104 | bytes 9462540 | tf_op jit(solution)/shard_map/attend/pallas_call | solution.py:69
  253.9 68.3 %turning.1 = (f32[1024,768]{1,0:T(8,128)}, bf16[768,1728]{1,0:T(8,128)(2,1)}, f32[512,768]{1,0:T(8,128)}, bf16[1024,192]{1,0:T(8,128)(2,1)}, f32[8,768]{1,0:T(8,128)}, /*index=5*/f32[8,768]{1,0:T(8,128)}) custom-call(bf16[1024,192]{1,0:T(8,128)(2,1)} %get-tuple-element.69.refs_0_, bf16[4,768,192]{2,1,0:T(8,128)(2,1)} %bitcast.148, ...), custom_call_target="tpu_custom_call" | custom-call | flops 8153726976 | bytes 16094208 | tf_op jit(solution)/shard_map/turning/pallas_call | solution.py:69
  322.2 12.5 %attend_back.2 = (bf16[1024,192]{1,0:T(8,128)(2,1)}, bf16[2,1024,192]{2,1,0:T(8,128)(2,1)}, bf16[2,512,192]{2,1,0:T(8,128)(2,1)}, bf16[2,512,192]{2,1,0:T(8,128)(2,1)}) custom-call(bf16[1024,192]{1,0:T(8,128)(2,1)} %get-tuple-element.72.refs_0_, bf16[1024,192]{1,0:T(8,128)(2,1)} %get-tuple-element.73.refs_1_, bf16[1024,192]{1,0:T(8,128)(2,1)} %get-tuple-element.74.refs_2_, ...), custom_call_target="tpu_custom_call" | custom-call | flops 4831838208 | bytes 9437952 | tf_op jit(solution)/shard_map/attend_back/pallas_call | solution.py:69
  334.7 4.5 collective-permute-start.6
  340.7 22.2 %collective-permute-done.6.refs_2_ = bf16[2,512,192]{2,1,0:T(8,128)(2,1)S(1)} collective-permute-done((bf16[2,512,192]{2,1,0:T(8,128)(2,1)}, bf16[2,512,192]{2,1,0:T(8,128)(2,1)S(1)}, u32[]{:S(2)}, u32[]{:S(2)}) %collective-permute-start.6) | collective-permute-done | bytes 393248 | tf_op jit(solution)/shard_map/ppermute | solution.py:941
  363.9 51.8 %middle_backward.1 = (bf16[768,2304]{1,0:T(8,128)(2,1)}, f32[512,768]{1,0:T(8,128)}, bf16[1024,192]{1,0:T(8,128)(2,1)}, f32[8,768]{1,0:T(8,128)}, f32[8,768]{1,0:T(8,128)}, /*index=5*/f32[8,192]{1,0:T(8,128)}) custom-call(bf16[1024,192]{1,0:T(8,128)(2,1)} %get-tuple-element.78.refs_0_, bf16[2,1024,192]{2,1,0:T(8,128)(2,1)} %get-tuple-element.79.refs_1_, ...), custom_call_target="tpu_custom_call" | custom-call | flops 7247757312 | bytes 24190976 | tf_op jit(solution)/shard_map/middle_backward/pallas_call | solution.py:69
  415.7 10.3 %attend_back.3 = (bf16[1024,192]{1,0:T(8,128)(2,1)}, bf16[2,1024,192]{2,1,0:T(8,128)(2,1)}, bf16[2,256,192]{2,1,0:T(8,128)(2,1)}, bf16[2,256,192]{2,1,0:T(8,128)(2,1)}) custom-call(bf16[1024,192]{1,0:T(8,128)(2,1)} %get-tuple-element.91.refs_0_, bf16[1024,192]{1,0:T(8,128)(2,1)} %get-tuple-element.92.refs_1_, bf16[1024,192]{1,0:T(8,128)(2,1)} %get-tuple-element.93.refs_2_, ...), custom_call_target="tpu_custom_call" | custom-call | flops 4831838208 | bytes 8651520 | tf_op jit(solution)/shard_map/attend_back/pallas_call | solution.py:69
  426.0 4.3 collective-permute-start.8
  431.5 11.1 %collective-permute-done.8.refs_2_ = bf16[2,256,192]{2,1,0:T(8,128)(2,1)S(1)} collective-permute-done((bf16[2,256,192]{2,1,0:T(8,128)(2,1)}, bf16[2,256,192]{2,1,0:T(8,128)(2,1)S(1)}, u32[]{:S(2)}, u32[]{:S(2)}) %collective-permute-start.8) | collective-permute-done | bytes 196640 | tf_op jit(solution)/shard_map/ppermute | solution.py:941
  443.5 31.3 %ending.1 = (f32[1024,768]{1,0:T(8,128)}, bf16[768,576]{1,0:T(8,128)(2,1)}, f32[8,192]{1,0:T(8,128)}) custom-call(bf16[1024,192]{1,0:T(8,128)(2,1)} %get-tuple-element.97.refs_0_, bf16[2,1024,192]{2,1,0:T(8,128)(2,1)} %get-tuple-element.98.refs_1_, bf16[2,256,192]{2,1,0:T(8,128)(2,1)} %copy-done.15, bf16[2,256,192]{2,1,0:T(8,128)(2,1)} %copy-done.16, ...), custom_call_target="tpu_custom_call" | custom-call | flops 1811939328 | bytes 11114496 | tf_op jit(solution)/shard_map/ending/pallas_call | solution.py:69
  477.8 42.6 %psum.22 = f32[2,6,768]{2,1,0:T(8,128)S(1)} all-reduce(f32[2,6,768]{2,1,0:T(8,128)S(1)} %pad_maximum_fusion.4), channel_id=1, replica_groups=mesh['seq'=8,'mp'=4] {'seq','mp'}, use_global_device_ids=true, to_apply=%region_8.0 | all-reduce | flops 9216 | bytes 73728 | tf_op jit(solution)/shard_map/psum | solution.py:1079
  520.5 2.5 multiply_reduce_fusion.2
  525.2 21.3 %psum.21 = f32[2,1,1152]{2,1,0:T(1,128)S(1)} all-reduce(f32[2,1,1152]{2,1,0:T(1,128)S(1)} %broadcast_in_dim.22), channel_id=1, replica_groups=mesh['seq'=8,'mp'=4] {'seq'}, use_global_device_ids=true, to_apply=%region_6.0 | all-reduce | flops 2304 | bytes 18432 | tf_op jit(solution)/shard_map/psum | solution.py:1083
  548.8 64.7 %reduce-scatter.8.cloned.1.call-done = bf16[96,1728]{1,0:T(8,128)(2,1)} async-done(((bf16[768,1728]{1,0:T(8,128)(2,1)}), bf16[96,1728]{1,0:T(8,128)(2,1)}) %reduce-scatter.8.cloned.1.call-update) | async-done | bytes 331792 | tf_op jit(solution)/shard_map/reduce_scatter | solution.py:977
  615.4 80.5 %reduce-scatter.6.cloned.1.call-done = bf16[96,2304]{1,0:T(8,128)(2,1)} async-done(((bf16[768,2304]{1,0:T(8,128)(2,1)}), bf16[96,2304]{1,0:T(8,128)(2,1)}) %reduce-scatter.6.cloned.1.call-update) | async-done | bytes 442384 | tf_op jit(solution)/shard_map/reduce_scatter | solution.py:977
  700.4 40.5 %psum.23 = f32[]{:T(128)} all-reduce(f32[]{:T(128)S(6)} %add.119), channel_id=1, replica_groups=mesh['seq'=8,'mp'=4] {'seq','mp'}, use_global_device_ids=true, to_apply=%region_10.11 | all-reduce | flops 1 | bytes 8 | tf_op jit(solution)/shard_map/psum | solution.py:1100
  747.8 1.8 multiply_add_fusion.3
  749.7 5.3 multiply_add_fusion
  756.0 3.3 multiply_add_fusion.1
  (185 shorter events, 48.0 us)
Async XLA Ops:
  7.2 734.5 %copy-start = (f32[2,4,1,1,192,192]{5,4,3,2,1,0:T(8,128)S(1)}, f32[2,4,1,1,192,192]{5,4,3,2,1,0:T(8,128)}, u32[]{:S(2)}) copy-start(f32[2,4,1,1,192,192]{5,4,3,2,1,0:T(8,128)} %param.32) | copy-start | bytes 3538948
  7.2 50.6 %all-gather.9.cloned.1.call-start = ((), (), s32[]{:S(2)}) async-start(), calls=%async_computation.6 | async-start | bytes 1769472 | tf_op jit(solution)/shard_map/all_gather | solution.py:1011
  9.4 101.0 %all-gather.13.cloned.1.call-start = ((), (), s32[]{:S(2)}) async-start(), calls=%async_computation.8 | async-start | bytes 1769472 | tf_op jit(solution)/shard_map/all_gather | solution.py:1011
  10.1 154.0 %all-gather.11.cloned.1.call-start = ((), (), s32[]{:S(2)}) async-start(), calls=%async_computation.7 | async-start | bytes 2654208 | tf_op jit(solution)/shard_map/all_gather | solution.py:1012
  10.3 7.9 %copy-start.36 = (s32[8]{0:T(128)S(1)}, s32[8]{0:T(128)}, u32[]{:S(2)}) copy-start(s32[8]{0:T(128)} %param.27) | copy-start | bytes 100
  10.3 8.0 %copy-start.17 = (f32[2,6,768]{2,0,1:T(2,128)S(1)}, f32[2,6,768]{2,0,1:T(2,128)}, u32[]{:S(2)}) copy-start(f32[2,6,768]{2,0,1:T(2,128)} %param.41) | copy-start | bytes 110596
  10.3 8.1 %copy-start.21 = (f32[2,1,1152]{2,1,0:T(1,128)S(1)}, f32[2,1,1152]{2,1,0:T(1,128)}, u32[]{:S(2)}) copy-start(f32[2,1,1152]{2,1,0:T(1,128)} %param.38) | copy-start | bytes 27652
  11.2 242.7 %all-gather.15.cloned.1.call-start = ((), (), s32[]{:S(2)}) async-start(), calls=%async_computation.9 | async-start | bytes 2654208 | tf_op jit(solution)/shard_map/all_gather | solution.py:1012
  11.3 59.8 %collective-permute-start.3 = (s32[512]{0:T(512)S(1)}, s32[512]{0:T(512)S(1)}, u32[]{:S(2)}, u32[]{:S(2)}) collective-permute-start(s32[512]{0:T(512)S(1)} %get-tuple-element.228), channel_id=1, source_target_pairs={{4,0},{8,4},{12,8},{16,12},{20,16},{24,20},{28,24},{5,1},{9,5},{13... | collective-permute-start | bytes 6152 | tf_op jit(solution)/shard_map/ppermute | solution.py:946
  12.6 12.2 %collective-permute-start.2 = (s32[512]{0:T(512)S(1)}, s32[512]{0:T(512)S(1)}, u32[]{:S(2)}, u32[]{:S(2)}) collective-permute-start(s32[512]{0:T(512)S(1)} %get-tuple-element.229), channel_id=1, source_target_pairs={{0,4},{4,8},{8,12},{12,16},{16,20},{20,24},{24,28},{1,5},{5,9},{9,... | collective-permute-start | bytes 6152 | tf_op jit(solution)/shard_map/ppermute | solution.py:941
  18.1 4.4 copy-start.37
  18.1 529.7 %reduce-scatter.4.cloned.1.call-start = ((), (), s32[]{:S(2)}) async-start(), calls=%async_computation.3 | async-start | bytes 1105920 | tf_op jit(solution)/shard_map/reduce_scatter | solution.py:977
  22.9 41.2 %copy-start.31 = (s32[3]{0:T(128)}, s32[3]{0:T(128)S(1)}, u32[]{:S(2)}) copy-start(s32[3]{0:T(128)S(1)} %convert_element_type.24.refs_5_) | copy-start | bytes 40
  65.2 11.4 %collective-permute-start.1 = (bf16[2,256,192]{2,1,0:T(8,128)(2,1)S(1)}, bf16[2,256,192]{2,1,0:T(8,128)(2,1)S(1)}, u32[]{:S(2)}, u32[]{:S(2)}) collective-permute-start(bf16[2,256,192]{2,1,0:T(8,128)(2,1)S(1)} %get-tuple-element.192), channel_id=1, source_target_pairs={{4,0},{8,4},{12,8},{16,12},{20,16},{24,20},{28,24},{5,1},{9,5},{13... | collective-permute-start | bytes 589832 | tf_op jit(solution)/shard_map/ppermute | solution.py:946
  66.5 14.7 %collective-permute-start = (bf16[2,256,192]{2,1,0:T(8,128)(2,1)S(1)}, bf16[2,256,192]{2,1,0:T(8,128)(2,1)S(1)}, u32[]{:S(2)}, u32[]{:S(2)}) collective-permute-start(bf16[2,256,192]{2,1,0:T(8,128)(2,1)S(1)} %get-tuple-element.193), channel_id=1, source_target_pairs={{0,4},{4,8},{8,12},{12,16},{16,20},{20,24},{24,28},{1,5},{5,9},{9,... | collective-permute-start | bytes 589832 | tf_op jit(solution)/shard_map/ppermute | solution.py:941
  76.6 4.5 copy-start.34
  214.2 16.5 %collective-permute-start.5 = (bf16[2,512,192]{2,1,0:T(8,128)(2,1)S(1)}, bf16[2,512,192]{2,1,0:T(8,128)(2,1)}, u32[]{:S(2)}, u32[]{:S(2)}) collective-permute-start(bf16[2,512,192]{2,1,0:T(8,128)(2,1)S(1)} %get-tuple-element.190), channel_id=1, source_target_pairs={{4,0},{8,4},{12,8},{16,12},{20,16},{24,20},{28,24},{5,1},{9,5},{13... | collective-permute-start | bytes 1179656 | tf_op jit(solution)/shard_map/ppermute | solution.py:946
  215.5 25.2 %collective-permute-start.4 = (bf16[2,512,192]{2,1,0:T(8,128)(2,1)S(1)}, bf16[2,512,192]{2,1,0:T(8,128)(2,1)}, u32[]{:S(2)}, u32[]{:S(2)}) collective-permute-start(bf16[2,512,192]{2,1,0:T(8,128)(2,1)S(1)} %get-tuple-element.191), channel_id=1, source_target_pairs={{0,4},{4,8},{8,12},{12,16},{16,20},{20,24},{24,28},{1,5},{5,9},{9,... | collective-permute-start | bytes 1179656 | tf_op jit(solution)/shard_map/ppermute | solution.py:941
  334.7 28.2 %collective-permute-start.6 = (bf16[2,512,192]{2,1,0:T(8,128)(2,1)}, bf16[2,512,192]{2,1,0:T(8,128)(2,1)S(1)}, u32[]{:S(2)}, u32[]{:S(2)}) collective-permute-start(bf16[2,512,192]{2,1,0:T(8,128)(2,1)} %get-tuple-element.80), channel_id=1, source_target_pairs={{0,4},{4,8},{8,12},{12,16},{16,20},{20,24},{24,28},{1,5},{5,9},{9,... | collective-permute-start | bytes 1179656 | tf_op jit(solution)/shard_map/ppermute | solution.py:941
  339.2 23.7 %collective-permute-start.7 = (bf16[2,512,192]{2,1,0:T(8,128)(2,1)}, bf16[2,512,192]{2,1,0:T(8,128)(2,1)S(1)}, u32[]{:S(2)}, u32[]{:S(2)}) collective-permute-start(bf16[2,512,192]{2,1,0:T(8,128)(2,1)} %get-tuple-element.81), channel_id=1, source_target_pairs={{4,0},{8,4},{12,8},{16,12},{20,16},{24,20},{28,24},{5,1},{9,5},{13... | collective-permute-start | bytes 1179656 | tf_op jit(solution)/shard_map/ppermute | solution.py:946
  426.0 16.7 %collective-permute-start.8 = (bf16[2,256,192]{2,1,0:T(8,128)(2,1)}, bf16[2,256,192]{2,1,0:T(8,128)(2,1)S(1)}, u32[]{:S(2)}, u32[]{:S(2)}) collective-permute-start(bf16[2,256,192]{2,1,0:T(8,128)(2,1)} %get-tuple-element.99), channel_id=1, source_target_pairs={{0,4},{4,8},{8,12},{12,16},{16,20},{20,24},{24,28},{1,5},{5,9},{9,... | collective-permute-start | bytes 589832 | tf_op jit(solution)/shard_map/ppermute | solution.py:941
  430.2 12.4 %collective-permute-start.9 = (bf16[2,256,192]{2,1,0:T(8,128)(2,1)}, bf16[2,256,192]{2,1,0:T(8,128)(2,1)S(1)}, u32[]{:S(2)}, u32[]{:S(2)}) collective-permute-start(bf16[2,256,192]{2,1,0:T(8,128)(2,1)} %get-tuple-element.100), channel_id=1, source_target_pairs={{4,0},{8,4},{12,8},{16,12},{20,16},{24,20},{28,24},{5,1},{9,5},{13... | collective-permute-start | bytes 589832 | tf_op jit(solution)/shard_map/ppermute | solution.py:946
  474.8 138.7 %reduce-scatter.8.cloned.1.call-start = ((), (), s32[]{:S(2)}) async-start(), calls=%async_computation.5 | async-start | bytes 3096576 | tf_op jit(solution)/shard_map/reduce_scatter | solution.py:977
  475.4 220.4 %reduce-scatter.6.cloned.1.call-start = ((), (), s32[]{:S(2)}) async-start(), calls=%async_computation.4 | async-start | bytes 3981312 | tf_op jit(solution)/shard_map/reduce_scatter | solution.py:977
  743.5 6.1 copy-start.8
  745.2 4.4 copy-start.10
  747.8 7.2 slice-start
  749.6 5.5 slice-start.1
  749.6 5.7 slice-start.2
  749.6 6.0 copy-start.4
  749.6 6.3 copy-start.11
  749.7 6.3 copy-start.29
  (26 other events, 67.8 us)
Sparse Core Ops, SparseCore 0:
  10.8 46.9 all-gather.8
  60.5 49.8 all-gather.12
  113.2 50.8 all-gather.10
  166.2 50.6 all-gather.14
  474.9 65.1 reduce-scatter.3
  543.9 69.4 reduce-scatter.7
  617.5 78.2 reduce-scatter.5

commit v2 on v0

v2 whole, which is shorter than its diff:
```python
from types import SimpleNamespace

import jax
import jax.numpy as jnp
from jax import lax
from jax.experimental import pallas as pl
from jax.experimental.pallas import tpu as pltpu
from jax.sharding import PartitionSpec as P

D = 768
DH = 64
FF = 3072
WIN = 256
STEP = 10

HIGHEST_PRECISION = lax.Precision.HIGHEST
NORM_EPSILON = 1e-05
MASK_FILL = -1e30
CLIP_LEVEL = 1.0
BETA_FIRST = 0.5
BETA_SECOND = 0.5
ADAM_EPSILON = 1e-08
DECAY_RATE = 0.01
AVERAGE_RATE = 0.7
VECTOR_RATE = 0.3

BF = jnp.bfloat16
SEQ, MP = "seq", "mp"
F32 = jnp.float32
MESH = pl.DeviceIdType.MESH
BLOCK = 256
CHUNK = 128
HALF = 64
VMEM_LIMIT = 56 * 1024 * 1024
SCORE_SCALE = DH ** (-0.5)

GATHER_TIMES = ((2, 4, 5), (3, 5), (6, 7, 9), (7, 10, 13, 16))
BACK_TIMES = ((1, 4, 7, 10, 12), (6, 8, 10, 12), (10, 13, 15, 17))
END_TIMES = ((1, 4, 7, 10, 13), (5, 8, 10, 12), (11, 14, 15, 16))


def dot(left, right):
    return jnp.dot(left, right, preferred_element_type=F32)


def dot_nt(left, right):
    return lax.dot_general(left, right, (((1,), (1,)), ((), ())), preferred_element_type=F32)


def dot_tn(left, right):
    return lax.dot_general(left, right, (((0,), (0,)), ((), ())), preferred_element_type=F32)


class Flush:
    def __init__(self, held, out, sems):
        self.held, self.out, self.sems = held, out, sems

    def copy(self, rows, t):
        return pltpu.make_async_copy(self.held.at[rows, :], self.out.at[rows, :], self.sems.at[t])


def run_kernel(
    body,
    name,
    inputs,
    outputs,
    scratch,
    collective=None,
    flops=0,
    grid=None,
    specs=None,
    in_smem=(),
    in_hbm=(),
    late=None,
    flushed=None,
    pieces=0,
):
    specs, late, flushed = specs or {}, late or {}, flushed or {}

    def kernel(*refs):
        refs = list(refs)

        def take(keys):
            got = refs[: len(keys)]
            del refs[: len(keys)]
            return dict(zip(keys, got))

        given, distant, made, written, held = (take(keys) for keys in (inputs, late, outputs, flushed, scratch))
        fetched, fetched_sems, filled, filled_sems = (take(keys) for keys in (late, late, flushed, flushed))
        r = SimpleNamespace(**given, **made, **held, **fetched, **filled)
        r.late = SimpleNamespace(
            **{key: pltpu.make_async_copy(distant[key], fetched[key], fetched_sems[key]) for key in late}
        )
        r.flush = SimpleNamespace(**{key: Flush(filled[key], written[key], filled_sems[key]) for key in flushed})
        for copy in vars(r.late).values():
            copy.start()
        body(r)

    def spec_of(key):
        if key in specs:
            return specs[key]
        if key in in_hbm or key in late or key in flushed:
            return pl.BlockSpec(memory_space=pl.ANY)
        return pl.BlockSpec(memory_space=pltpu.SMEM if key in in_smem else pltpu.VMEM)

    arguments = {**inputs, **late}
    gives = {**outputs, **flushed}
    shapes = [jax.ShapeDtypeStruct(shape, dtype) for shape, dtype in gives.values()]
    moved = sum(v.size * v.dtype.itemsize for v in arguments.values())
    moved += sum(v.size * v.dtype.itemsize for v in shapes)
    extra = {} if grid is None else dict(grid=grid)
    params = dict(vmem_limit_bytes=VMEM_LIMIT)
    if collective is not None:
        params.update(collective_id=collective, has_side_effects=True)
    results = pl.pallas_call(
        kernel,
        out_shape=shapes,
        in_specs=[spec_of(key) for key in arguments],
        out_specs=[spec_of(key) for key in gives],
        scratch_shapes=list(scratch.values())
        + [pltpu.VMEM(v.shape, v.dtype) for v in late.values()]
        + [pltpu.SemaphoreType.DMA for _ in late]
        + [pltpu.VMEM(shape, dtype) for shape, dtype in flushed.values()]
        + [pltpu.SemaphoreType.DMA((pieces,)) for _ in flushed],
        compiler_params=pltpu.CompilerParams(**params),
        cost_estimate=pl.CostEstimate(flops=int(flops), bytes_accessed=int(moved), transcendentals=0),
        name=name,
        **extra,
    )(*arguments.values())
    return SimpleNamespace(**dict(zip(gives, results)))


def parity_matrix():
    row = lax.broadcasted_iota(jnp.int32, (2 * BLOCK, 2 * BLOCK), 0)
    col = lax.broadcasted_iota(jnp.int32, (2 * BLOCK, 2 * BLOCK), 1)
    source = 2 * (row % BLOCK) + row // BLOCK
    return jnp.where(col == source, 1.0, 0.0).astype(BF)


def head_lanes(count):
    lane = lax.broadcasted_iota(jnp.int32, (1, count * DH), 1)
    return [lane // DH == head for head in range(count)]


def head_flags(dilated, count):
    first = lax.axis_index(MP) * count
    return [jnp.logical_or(dilated[0] == first + head, dilated[1] == first + head) for head in range(count)]


def marked_lanes(dilated, count):
    marked = jnp.zeros((1, count * DH), jnp.int32)
    for flag, lanes in zip(head_flags(dilated, count), head_lanes(count)):
        marked = jnp.where(lanes, flag.astype(jnp.int32), marked)
    return marked > 0


def arrange_rows(natural, sort):
    groups = natural.shape[0] // (2 * BLOCK)
    parts = [
        dot(sort, natural[g * 2 * BLOCK : (g + 1) * 2 * BLOCK]).astype(BF) for g in range(groups)
    ]
    return jnp.concatenate([p[:BLOCK] for p in parts] + [p[BLOCK:] for p in parts], axis=0)


def restore_rows(arranged, sort):
    groups = arranged.shape[0] // (2 * BLOCK)
    half = groups * BLOCK
    parts = []
    for g in range(groups):
        pair = jnp.concatenate(
            [
                arranged[g * BLOCK : (g + 1) * BLOCK],
                arranged[half + g * BLOCK : half + (g + 1) * BLOCK],
            ],
            axis=0,
        )
        parts.append(dot_tn(sort, pair))
    return jnp.concatenate(parts, axis=0)


def soft_weights(query_block, key_block, lanes, allowed):
    raw = dot_nt(jnp.where(lanes, query_block, 0.0).astype(BF), key_block)
    scores = jnp.where(allowed, raw, MASK_FILL)
    top = jnp.max(scores, axis=1, keepdims=True)
    exponent = jnp.exp(scores - top)
    total = jnp.sum(exponent, axis=1, keepdims=True)
    return (exponent * (1.0 / total)).astype(BF)


def window_mask():
    row = lax.broadcasted_iota(jnp.int32, (BLOCK, 3 * BLOCK), 0)
    col = lax.broadcasted_iota(jnp.int32, (BLOCK, 3 * BLOCK), 1)
    return jnp.abs(row - col + BLOCK) <= WIN


def attend(query, pair, left, right, seg_query, seg_keys, dilated):
    rows, width = query.shape
    heads = width // DH
    blocks = rows // BLOCK
    keys = 3 * BLOCK
    slots = 2 * blocks

    def body(r):
        step = pl.program_id(0)

        @pl.when(step == 0)
        def _():
            marked = marked_lanes(r.dilated, heads)
            sort = parity_matrix()
            for which, held in ((0, r.keys), (1, r.values)):
                lanes = slice(which * width, (which + 1) * width)
                padded = jnp.concatenate([r.left[:, lanes], r.pair[:, lanes], r.right[:, lanes]], axis=0)
                middle = jnp.concatenate(
                    [
                        padded[BLOCK : (blocks + 1) * BLOCK],
                        padded[(blocks - 1) * BLOCK : (2 * blocks - 1) * BLOCK],
                    ],
                    axis=0,
                )
                held[...] = jnp.where(marked, arrange_rows(padded, sort), middle)
            scaled = (r.asked[...].astype(F32) * SCORE_SCALE).astype(BF)
            r.query[...] = jnp.where(marked, arrange_rows(scaled, sort), scaled)

        window = window_mask()
        first = step + 2 * (step >= blocks // 2)
        own = pl.ds(pl.multiple_of(step * BLOCK, BLOCK), BLOCK)
        near = pl.ds(pl.multiple_of(first * BLOCK, BLOCK), keys)
        key_block = r.keys[near, :]
        value_block = r.values[near, :]
        query_block = r.query[own, :]
        gathered = jnp.zeros((BLOCK, width), F32)
        flags = head_flags(r.dilated, heads)
        for head, lanes in enumerate(head_lanes(heads)):
            mine = jnp.where(flags[head], r.seg_query[own, 1:2], r.seg_query[own, 0:1])
            theirs = jnp.where(flags[head], r.seg_keys[1:2, near], r.seg_keys[0:1, near])
            soft = soft_weights(query_block, key_block, lanes, jnp.logical_and(window, mine == theirs))
            r.soft[head] = soft
            gathered = jnp.where(lanes, dot(soft, value_block), gathered)
        r.arranged[own, :] = gathered.astype(BF)

        @pl.when(step == blocks - 1)
        def _():
            arranged = r.arranged[...]
            natural = restore_rows(arranged, parity_matrix()).astype(BF)
            r.out[...] = jnp.where(marked_lanes(r.dilated, heads), natural, arranged)

    return run_kernel(
        body,
        "attend",
        dict(
            asked=query,
            pair=pair,
            left=left,
            right=right,
            seg_query=seg_query,
            seg_keys=seg_keys,
            dilated=dilated,
        ),
        dict(
            out=((rows, width), BF),
            arranged=((rows, width), BF),
            query=((rows, width), BF),
            keys=((slots * BLOCK, width), BF),
            values=((slots * BLOCK, width), BF),
            soft=((heads, rows, keys), BF),
        ),
        {},
        flops=4 * rows * keys * 256 * heads,
        grid=(blocks,),
        specs=dict(soft=pl.BlockSpec((heads, BLOCK, keys), lambda i: (0, i, 0))),
        in_smem=("dilated",),
    )


def attend_back(saved, grad_out, dilated, rim, mixed, count, collective):
    rows, width = grad_out.shape
    heads = width // DH
    blocks = rows // BLOCK
    keys = 3 * BLOCK
    slots = 2 * blocks if mixed else blocks + 2
    half = blocks // 2

    def order(i):
        return (i % 2) * half + i // 2

    def body(r):
        turn = pl.program_id(0)
        step = order(turn) if mixed else turn
        column = Column(count)
        first, last = column.index == 0, column.index == count - 1
        before = (lax.rem(column.index + count - 1, count), column.here)
        after = (lax.rem(column.index + 1, count), column.here)
        copy = copy_to(r.ready_left, r.from_right, r.sent.at[0], r.came.at[0], before)

        @pl.when(turn == 0)
        def _():
            barrier = pltpu.get_barrier_semaphore()

            @pl.when(jnp.logical_not(last))
            def _():
                pl.semaphore_signal(barrier, inc=1, device_id=after, device_id_type=MESH)

            grad = r.grad_out[...]
            if mixed:
                grad = jnp.where(marked_lanes(r.dilated, heads), arrange_rows(grad, parity_matrix()), grad)
            r.grad[...] = grad
            r.grad_keys[...] = jnp.zeros_like(r.grad_keys)
            r.grad_values[...] = jnp.zeros_like(r.grad_values)

            @pl.when(jnp.logical_not(first))
            def _():
                pl.semaphore_wait(barrier, 1)

        start = step + 2 * (step >= half) if mixed else step
        own = pl.ds(pl.multiple_of(step * BLOCK, BLOCK), BLOCK)
        near = pl.ds(pl.multiple_of(start * BLOCK, BLOCK), keys)
        key_block = r.keys[near, :]
        value_block = r.values[near, :]
        query_block = r.query[own, :]
        grad_block = r.grad[own, :]
        product = grad_block.astype(F32) * r.arranged[own, :].astype(F32)
        grad_query = jnp.zeros((BLOCK, width), F32)
        grad_key = jnp.zeros((keys, width), F32)
        grad_value = jnp.zeros((keys, width), F32)
        for head, lanes in enumerate(head_lanes(heads)):
            soft = r.soft[head]
            grad_head = jnp.where(lanes, grad_block, 0.0).astype(BF)
            row_dot = jnp.sum(jnp.where(lanes, product, 0.0), axis=1, keepdims=True)
            grad_soft = dot_nt(grad_head, value_block)
            grad_scores = (soft.astype(F32) * (grad_soft - row_dot)).astype(BF)
            grad_value += dot_tn(soft, grad_head)
            grad_key += dot_tn(grad_scores, jnp.where(lanes, query_block, 0.0).astype(BF))
            grad_query = jnp.where(lanes, dot(grad_scores, key_block), grad_query)
        r.grad_query[own, :] = (grad_query * SCORE_SCALE).astype(BF)
        r.grad_keys[near, :] += grad_key
        r.grad_values[near, :] += grad_value

        def natural_group(g, middle):
            both = []
            for held in (r.grad_keys, r.grad_values):
                plain = middle(held)
                pair = jnp.concatenate(
                    [
                        held[g * BLOCK : (g + 1) * BLOCK, :],
                        held[(blocks + g) * BLOCK : (blocks + g + 1) * BLOCK, :],
                    ],
                    axis=0,
                ).astype(BF)
                marked = marked_lanes(r.dilated, heads)
                both.append(jnp.where(marked, dot_tn(parity_matrix(), pair), plain).astype(BF))
            return jnp.concatenate(both, axis=1)

        edge = jnp.zeros((BLOCK, width), F32)

        @pl.when(turn == (1 if mixed else 0))
        def _():
            if mixed:
                r.ready_left[...] = natural_group(0, lambda held: jnp.concatenate([edge, held[:BLOCK, :]], axis=0))
            else:
                r.ready_left[...] = jnp.concatenate(
                    [r.grad_keys[:rim, :], r.grad_values[:rim, :]], axis=1
                ).astype(BF)

            @pl.when(jnp.logical_not(first))
            def _():
                copy.start()

        @pl.when(turn == blocks - 1)
        def _():
            if mixed:
                arranged = r.grad_query[...]
                natural = restore_rows(arranged, parity_matrix()).astype(BF)
                r.out_query[...] = jnp.where(marked_lanes(r.dilated, heads), natural, arranged)
                lap = 2 * BLOCK
                middle = blocks * BLOCK
                r.out_own[:lap, :] = natural_group(
                    1, lambda held: jnp.concatenate([held[BLOCK:lap, :], held[lap : lap + BLOCK, :] + held[middle : middle + BLOCK, :]], axis=0)
                )
                r.out_own[lap:, :] = natural_group(
                    2,
                    lambda held: jnp.concatenate(
                        [
                            held[lap + BLOCK : middle, :] + held[middle + BLOCK : middle + lap, :],
                            held[middle + lap : middle + lap + BLOCK, :],
                        ],
                        axis=0,
                    ),
                )
                r.out_right[...] = natural_group(
                    3, lambda held: jnp.concatenate([held[middle + lap + BLOCK :, :], edge], axis=0)
                )
            else:
                r.out_query[...] = r.grad_query[...]
                both = jnp.concatenate([r.grad_keys[rim:, :], r.grad_values[rim:, :]], axis=1).astype(BF)
                r.out_own[...] = both[:rows]
                r.out_right[...] = both[rows:]

            @pl.when(jnp.logical_not(last))
            def _():
                copy.wait_recv()
                tail = pl.ds(rows - rim, rim)
                r.out_own[tail, :] = (r.out_own[tail, :].astype(F32) + r.from_right[...].astype(F32)).astype(BF)

            @pl.when(jnp.logical_not(first))
            def _():
                copy.wait_send()

    soft_index = (lambda i: (0, order(i), 0)) if mixed else (lambda i: (0, i, 0))
    return run_kernel(
        body,
        "attend_back",
        dict(
            grad_out=grad_out,
            arranged=saved.arranged,
            query=saved.query,
            keys=saved.keys,
            values=saved.values,
            soft=saved.soft,
            dilated=dilated,
        ),
        dict(
            out_query=((rows, width), BF),
            out_own=((rows, 2 * width), BF),
            out_right=((rim, 2 * width), BF),
        ),
        dict(
            grad=pltpu.VMEM((rows, width), BF),
            grad_query=pltpu.VMEM((rows, width), BF),
            grad_keys=pltpu.VMEM((slots * BLOCK, width), F32),
            grad_values=pltpu.VMEM((slots * BLOCK, width), F32),
            ready_left=pltpu.VMEM((rim, 2 * width), BF),
            from_right=pltpu.VMEM((rim, 2 * width), BF),
            sent=pltpu.SemaphoreType.DMA((1,)),
            came=pltpu.SemaphoreType.DMA((1,)),
        ),
        collective=collective,
        flops=8 * rows * keys * 256 * heads,
        grid=(blocks,),
        specs=dict(soft=pl.BlockSpec((heads, BLOCK, keys), soft_index)),
        in_smem=("dilated",),
    )


class Partners:
    def __init__(self, count=0, shift=0):
        seq = lax.axis_index(SEQ)
        here = lax.axis_index(MP)
        self.core = lax.rem(here, 2)
        self.sibling = (seq, here + 1 - 2 * self.core)
        self.across = (seq, lax.rem(here + 2, 4))
        self.diagonal = (seq, lax.rem(here + 3 - 2 * self.core, 4))
        self.count, self.shift = count, shift

    def meet(self, column=None):
        barrier = pltpu.get_barrier_semaphore()
        others = [self.sibling, self.across, self.diagonal]
        if column is not None:
            others += [column.peer(k) for k in range(1, column.count)]
        for other in others:
            pl.semaphore_signal(barrier, inc=1, device_id=other, device_id_type=MESH)
        pl.semaphore_wait(barrier, len(others))

    def place(self, t):
        return lax.rem(t + self.shift, self.count) if self.shift else t

    def chunk(self, t):
        return pl.ds(pl.multiple_of(self.place(t) * CHUNK, CHUNK), CHUNK)

    def two_chunks(self, t):
        return pl.ds(pl.multiple_of(self.place(t - 1) * CHUNK, 2 * CHUNK), 2 * CHUNK)

    def own(self, t):
        return pl.ds(pl.multiple_of(self.place(t) * CHUNK + self.core * HALF, HALF), HALF)

    def other(self, t):
        return pl.ds(pl.multiple_of(self.place(t) * CHUNK + (1 - self.core) * HALF, HALF), HALF)

    def half(self, t):
        return pl.ds(pl.multiple_of(self.place(t) * HALF, HALF), HALF)


def copy_to(source, target, sent, arrived, device):
    return pltpu.make_async_remote_copy(
        src_ref=source, dst_ref=target, send_sem=sent, recv_sem=arrived, device_id=device, device_id_type=MESH
    )


def exchange_scratch(rows):
    count = rows // CHUNK
    return dict(
        part=pltpu.VMEM((rows, D), BF),
        near=pltpu.VMEM((rows // 2, D), BF),
        far=pltpu.VMEM((rows // 2, D), BF),
        core_sent=pltpu.SemaphoreType.DMA((count,)),
        core_came=pltpu.SemaphoreType.DMA((count,)),
        far_sent=pltpu.SemaphoreType.DMA((count,)),
        far_came=pltpu.SemaphoreType.DMA((count,)),
    )


def gather_scratch(rows, width=D, dtype=BF):
    count = rows // CHUNK
    return dict(
        full=pltpu.VMEM((rows, width), dtype),
        sent=pltpu.SemaphoreType.DMA((count,)),
        came=pltpu.SemaphoreType.DMA((count,)),
    )


class Exchange:
    def __init__(self, who, refs):
        self.who, self.r = who, refs

    def core_copy(self, t):
        who, r = self.who, self.r
        return copy_to(
            r.part.at[who.other(t), :], r.near.at[who.half(t), :], r.core_sent.at[t], r.core_came.at[t], who.sibling
        )

    def far_copy(self, t):
        who, r = self.who, self.r
        rows = who.half(t)
        return copy_to(r.near.at[rows, :], r.far.at[rows, :], r.far_sent.at[t], r.far_came.at[t], who.across)

    def give(self, t, part):
        self.r.part[self.who.chunk(t), :] = part.astype(BF)
        self.core_copy(t).start()

    def add(self, t):
        who, r = self.who, self.r
        self.core_copy(t).wait_recv()
        pair = r.part[who.own(t), :].astype(F32) + r.near[who.half(t), :].astype(F32)
        r.near[who.half(t), :] = pair.astype(BF)
        self.far_copy(t).start()

    def take(self, t):
        who, r = self.who, self.r
        self.far_copy(t).wait_recv()
        return r.near[who.half(t), :].astype(F32) + r.far[who.half(t), :].astype(F32)

    def finish(self, t):
        self.core_copy(t).wait_send()
        self.far_copy(t).wait_send()


class Gather:
    def __init__(self, who, refs):
        self.who, self.r = who, refs

    def copy(self, rows, t):
        r = self.r
        return copy_to(r.full.at[rows, :], r.full.at[rows, :], r.sent.at[t], r.came.at[t], self.who.sibling)

    def give(self, t, value):
        rows = self.who.own(t)
        self.r.full[rows, :] = value.astype(self.r.full.dtype)
        self.copy(rows, t).start()

    def take(self, t):
        self.wait(t)
        return self.r.full[self.who.chunk(t), :]

    def wait(self, t):
        self.copy(self.who.other(t), t).wait_recv()

    def finish(self, t):
        self.copy(self.who.own(t), t).wait_send()


class Column:
    def __init__(self, count):
        self.count = count
        self.lines = count // 2
        self.here = lax.axis_index(MP)
        self.index = lax.axis_index(SEQ)
        self.inner = lax.rem(self.index, 2)
        self.outer = lax.div(self.index, 2)

    def peer(self, k):
        return (lax.rem(self.index + k, self.count), self.here)

    def at(self, outer, inner):
        return (2 * outer + inner, self.here)

    def turn(self, k):
        return lax.rem(self.outer + k, self.lines)


def gather_sems(lines):
    return {
        key: pltpu.SemaphoreType.DMA((lines,)) for key in ("pair_sent", "pair_came", "up_sent", "down_sent", "line_came")
    }


class GatherBlocks:
    def __init__(self, column, refs):
        self.c, self.r = column, refs
        self.above = column.outer < column.lines - 1
        self.below = column.outer > 0

    def line_copy(self, source, step):
        c, r = self.c, self.r
        block = 2 * source + c.inner
        sent = r.up_sent if step > 0 else r.down_sent
        return copy_to(
            r.full.at[block], r.full.at[block], sent.at[source], r.line_came.at[source], c.at(c.outer + step, c.inner)
        )

    def pair_copy(self, source, inner):
        c, r = self.c, self.r
        block = 2 * source + inner
        return copy_to(
            r.full.at[block],
            r.full.at[block],
            r.pair_sent.at[source],
            r.pair_came.at[source],
            c.at(c.outer, 1 - c.inner),
        )

    def put(self, value):
        self.r.full[self.c.index] = value

    def start_line(self):
        c = self.c

        @pl.when(self.above)
        def _():
            self.line_copy(c.outer, 1).start()

        @pl.when(self.below)
        def _():
            self.line_copy(c.outer, -1).start()

    def start_pair(self):
        self.pair_copy(self.c.outer, self.c.inner).start()

    def relay(self, k):
        c = self.c

        @pl.when(c.outer >= k)
        def _():
            source = c.outer - k
            self.line_copy(source, 1).wait_recv()

            @pl.when(self.above)
            def _():
                self.line_copy(source, 1).start()

            self.hand_on(source)

        @pl.when(c.outer + k < c.lines)
        def _():
            source = c.outer + k
            self.line_copy(source, -1).wait_recv()

            @pl.when(self.below)
            def _():
                self.line_copy(source, -1).start()

            self.hand_on(source)

    def hand_on(self, source):
        self.pair_copy(source, self.c.inner).start()

    def arrive(self):
        for k in range(self.c.lines):
            self.pair_copy(k, 1 - self.c.inner).wait_recv()

    def finish(self):
        for k in range(self.c.lines):
            self.pair_copy(k, self.c.inner).wait_send()
        self.finish_line()

    def finish_line(self):
        c = self.c
        for k in range(c.lines):

            @pl.when(jnp.logical_and(self.above, c.outer >= k))
            def _(k=k):
                self.line_copy(k, 1).wait_send()

            @pl.when(jnp.logical_and(self.below, c.outer <= k))
            def _(k=k):
                self.line_copy(k, -1).wait_send()


class GatherPairs(GatherBlocks):
    def line_copy(self, source, step):
        c, r = self.c, self.r
        blocks = pl.ds(2 * source, 2)
        sent = r.up_sent if step > 0 else r.down_sent
        return copy_to(
            r.full.at[blocks], r.full.at[blocks], sent.at[source], r.line_came.at[source], c.at(c.outer + step, c.inner)
        )

    def begin(self):
        self.pair_copy(self.c.outer, 1 - self.c.inner).wait_recv()
        self.start_line()

    def hand_on(self, source):
        pass

    def finish(self):
        self.pair_copy(self.c.outer, self.c.inner).wait_send()
        self.finish_line()


def scatter_scratch(lines, block, size, held=True):
    scratch = {
        key: pltpu.SemaphoreType.DMA((lines + 1,))
        for key in ("pair_sent", "pair_came", "line_sent", "line_came", "own_came")
    }
    scratch.update(near=pltpu.VMEM((lines, block, size), BF), far=pltpu.VMEM((lines + 1, block, size), BF))
    if held:
        scratch["own"] = pltpu.VMEM((lines, block, size), BF)
    return scratch


class ScatterBlocks:
    def __init__(self, column, refs, total):
        self.c, self.r, self.total = column, refs, total
        self.above = column.outer < column.lines - 1
        self.below = column.outer > 0
        self.fetched = hasattr(refs, "own")
        order = []
        for k in range(column.lines // 2):
            order += [column.lines - 1 - k, k]
        self.order = order

    def pair_copy(self, outer):
        c, r = self.c, self.r
        return copy_to(
            r.grads.at[2 * outer + 1 - c.inner],
            r.near.at[outer],
            r.pair_sent.at[outer],
            r.pair_came.at[outer],
            c.at(c.outer, 1 - c.inner),
        )

    def own_copy(self, outer):
        c, r = self.c, self.r
        return pltpu.make_async_copy(r.grads.at[2 * outer + c.inner], r.own.at[outer], r.own_came.at[outer])

    def line_copy(self, target, step):
        c, r = self.c, self.r
        slot = target if step > 0 else jnp.where(c.outer - 1 == target, c.lines, target)
        return copy_to(
            r.near.at[target],
            r.far.at[slot],
            r.line_sent.at[target],
            r.line_came.at[slot],
            c.at(c.outer + step, c.inner),
        )

    def landing(self, slot, step):
        c, r = self.c, self.r
        return copy_to(
            r.near.at[c.outer], r.far.at[slot], r.line_sent.at[c.outer], r.line_came.at[slot], c.at(c.outer + step, c.inner)
        )

    def start(self):
        for outer in self.order:
            self.pair_copy(outer).start()
            if self.fetched:
                self.own_copy(outer).start()

    def pair_step(self, k):
        c, r = self.c, self.r
        for outer in self.order[2 * k : 2 * k + 2]:
            self.pair_copy(outer).wait_recv()
            if self.fetched:
                self.own_copy(outer).wait()
                own = r.own[outer]
            else:
                own = r.grads[2 * outer + c.inner]
            r.near[outer] = (own.astype(F32) + r.near[outer].astype(F32)).astype(BF)

    def line_step(self, wave):
        c, r = self.c, self.r
        from_top = c.lines - 1 - c.outer

        def pass_on(target, step, behind):
            @pl.when(behind)
            def _():
                self.landing(target, step).wait_recv()
                r.near[target] = (r.near[target].astype(F32) + r.far[target].astype(F32)).astype(BF)

            self.line_copy(target, step).start()

        @pl.when(c.outer <= wave)
        def _():
            pass_on(from_top + c.outer - wave + c.outer, 1, self.below)

        @pl.when(from_top <= wave)
        def _():
            pass_on(wave - from_top, -1, self.above)

    def close(self):
        c, r = self.c, self.r
        self.total[...] = r.near[c.outer].astype(F32)

        @pl.when(self.below)
        def _():
            self.landing(c.outer, 1).wait_recv()
            self.total[...] += r.far[c.outer].astype(F32)

        @pl.when(self.above)
        def _():
            self.landing(c.lines, -1).wait_recv()
            self.total[...] += r.far[c.lines].astype(F32)

    def finish(self):
        c = self.c
        for outer in self.order:
            self.pair_copy(outer).wait_send()
        for target in range(c.lines):

            @pl.when(c.outer < target)
            def _(target=target):
                self.line_copy(target, 1).wait_send()

            @pl.when(c.outer > target)
            def _(target=target):
                self.line_copy(target, -1).wait_send()

    def ticks(self, times):
        steps = [(times[0], lambda: self.pair_step(0)), (times[0], lambda: self.line_step(0))]
        steps += [(times[1], lambda: self.pair_step(1))]
        steps += [(times[k], lambda k=k: self.line_step(k)) for k in range(1, self.c.lines - 1)]
        steps += [(times[self.c.lines - 1], self.close)]
        return steps


def scatter_pairs_scratch(lines, block, size):
    scratch = {key: pltpu.SemaphoreType.DMA((lines + 1,)) for key in ("pair_sent", "pair_came", "line_sent", "line_came")}
    scratch.update(
        sums=pltpu.VMEM((2 * lines, block, size), BF),
        far=pltpu.VMEM((2 * lines + 2, block, size), BF),
        give=pltpu.VMEM((block, size), BF),
        get=pltpu.VMEM((block, size), BF),
        held=pltpu.SemaphoreType.DMA,
    )
    return scratch


class ScatterPairs:
    def __init__(self, column, refs, total):
        self.c, self.r, self.total = column, refs, total
        self.above = column.outer < column.lines - 1
        self.below = column.outer > 0
        self.fetch = pltpu.make_async_copy(refs.grads, refs.sums, refs.held)

    def line_copy(self, target, step):
        c, r = self.c, self.r
        slot = target if step > 0 else jnp.where(c.outer - 1 == target, c.lines, target)
        return copy_to(
            r.sums.at[pl.ds(2 * target, 2)],
            r.far.at[pl.ds(2 * slot, 2)],
            r.line_sent.at[target],
            r.line_came.at[slot],
            c.at(c.outer + step, c.inner),
        )

    def landing(self, slot, step):
        c, r = self.c, self.r
        return copy_to(
            r.sums.at[pl.ds(2 * c.outer, 2)],
            r.far.at[pl.ds(2 * slot, 2)],
            r.line_sent.at[c.outer],
            r.line_came.at[slot],
            c.at(c.outer + step, c.inner),
        )

    def pair_copy(self):
        c, r = self.c, self.r
        return copy_to(r.give, r.get, r.pair_sent.at[0], r.pair_came.at[0], c.at(c.outer, 1 - c.inner))

    def start(self):
        self.fetch.start()

    def line_step(self, wave):
        c, r = self.c, self.r
        from_top = c.lines - 1 - c.outer
        if wave == 0:
            self.fetch.wait()

        def pass_on(target, step, behind):
            @pl.when(behind)
            def _():
                self.landing(target, step).wait_recv()
                for k in range(2):
                    block = 2 * target + k
                    r.sums[block] = (r.sums[block].astype(F32) + r.far[block].astype(F32)).astype(BF)

            self.line_copy(target, step).start()

        @pl.when(c.outer <= wave)
        def _():
            pass_on(from_top + c.outer - wave + c.outer, 1, self.below)

        @pl.when(from_top <= wave)
        def _():
            pass_on(wave - from_top, -1, self.above)

    def close_line(self):
        c, r = self.c, self.r
        mine, other = 2 * c.outer + c.inner, 2 * c.outer + 1 - c.inner
        self.total[...] = r.sums[mine].astype(F32)

        @pl.when(self.below)
        def _():
            self.landing(c.outer, 1).wait_recv()
            self.total[...] += r.far[mine].astype(F32)
            r.sums[other] = (r.sums[other].astype(F32) + r.far[other].astype(F32)).astype(BF)

        @pl.when(self.above)
        def _():
            self.landing(c.lines, -1).wait_recv()
            self.total[...] += r.far[2 * c.lines + c.inner].astype(F32)
            r.sums[other] = (r.sums[other].astype(F32) + r.far[2 * c.lines + 1 - c.inner].astype(F32)).astype(BF)

        r.give[...] = r.sums[other]
        self.pair_copy().start()

    def close(self):
        self.pair_copy().wait_recv()
        self.total[...] += self.r.get[...].astype(F32)

    def finish(self):
        c = self.c
        self.pair_copy().wait_send()
        for target in range(c.lines):

            @pl.when(c.outer < target)
            def _(target=target):
                self.line_copy(target, 1).wait_send()

            @pl.when(c.outer > target)
            def _(target=target):
                self.line_copy(target, -1).wait_send()

    def ticks(self, times):
        steps = [(times[k], lambda k=k: self.line_step(k)) for k in range(self.c.lines - 1)]
        return steps + [(times[self.c.lines - 1], self.close_line), (times[self.c.lines], self.close)]


class Halo:
    def __init__(self, column, refs, source, rim, size):
        self.c, self.r, self.source, self.rim, self.size = column, refs, source, rim, size
        self.rows = source.shape[0]
        self.before = lax.rem(column.index + column.count - 1, column.count), column.here
        self.after = lax.rem(column.index + 1, column.count), column.here
        self.first, self.last = column.index == 0, column.index == column.count - 1

    def clear(self):
        @pl.when(self.first)
        def _():
            self.r.left[...] = jnp.zeros_like(self.r.left)

        @pl.when(self.last)
        def _():
            self.r.right[...] = jnp.zeros_like(self.r.right)

    def back_copy(self, t):
        rows = pl.ds(pl.multiple_of(t * self.size, self.size), self.size)
        return copy_to(
            self.source.at[rows, :], self.r.right.at[rows, :], self.r.back_sent.at[t], self.r.back_came.at[t], self.before
        )

    def ahead_copy(self, t):
        from_rows = pl.ds(pl.multiple_of(self.rows - self.rim + t * self.size, self.size), self.size)
        rows = pl.ds(pl.multiple_of(t * self.size, self.size), self.size)
        return copy_to(
            self.source.at[from_rows, :],
            self.r.left.at[rows, :],
            self.r.ahead_sent.at[t],
            self.r.ahead_came.at[t],
            self.after,
        )

    def send(self, t):
        count = self.rim // self.size
        offset = (self.rows - self.rim) // self.size

        @pl.when(jnp.logical_and(t < count, jnp.logical_not(self.first)))
        def _():
            self.back_copy(t).start()

        @pl.when(jnp.logical_and(t >= offset, jnp.logical_not(self.last)))
        def _():
            self.ahead_copy(t - offset).start()

    def arrive(self):
        for t in range(self.rim // self.size):

            @pl.when(jnp.logical_not(self.last))
            def _():
                self.back_copy(t).wait_recv()

            @pl.when(jnp.logical_not(self.first))
            def _():
                self.ahead_copy(t).wait_recv()

    def finish(self):
        for t in range(self.rim // self.size):

            @pl.when(jnp.logical_not(self.first))
            def _():
                self.back_copy(t).wait_send()

            @pl.when(jnp.logical_not(self.last))
            def _():
                self.ahead_copy(t).wait_send()


def halo_scratch(count):
    return {
        key: pltpu.SemaphoreType.DMA((count,)) for key in ("back_sent", "back_came", "ahead_sent", "ahead_came")
    }


def pick(r, prefix):
    start = prefix + "_"
    return SimpleNamespace(
        **{key[len(start) :]: value for key, value in vars(r).items() if key.startswith(start)}
    )


def prefixed(prefix, entries):
    return {prefix + "_" + key: value for key, value in entries.items()}


def run_stages(count, stages, ticks=()):
    last = max(delay for delay, _ in stages)

    def step(i, carry):
        for when in sorted({when for when, _ in ticks if when < count + last}):

            @pl.when(i == when)
            def _(when=when):
                for other, tick in ticks:
                    if other == when:
                        tick()

        for delay, stage in stages:

            @pl.when(jnp.logical_and(i >= delay, i < count + delay))
            def _(delay=delay, stage=stage):
                stage(i - delay)

        return carry

    lax.fori_loop(0, count + last, step, 0)
    for when, tick in sorted(ticks, key=lambda entry: entry[0]):
        if when >= count + last:
            tick()


def norm_forward(total, gain, shift):
    center = total - jnp.mean(total, axis=1, keepdims=True)
    spread = jnp.mean(center * center, axis=1, keepdims=True)
    inverse = lax.rsqrt(spread + NORM_EPSILON)
    unit = center * inverse
    return unit, inverse, unit * gain + shift


def norm_back(grad, unit, inverse, gain):
    grad_unit = grad * gain
    first = jnp.mean(grad_unit, axis=1, keepdims=True)
    second = jnp.mean(grad_unit * unit, axis=1, keepdims=True)
    return inverse * (grad_unit - first - unit * second)


def column_sum(value):
    return jnp.sum(value, axis=0, keepdims=True)


def split_two(value):
    high = value.astype(BF)
    return high, (value - high.astype(F32)).astype(BF)


def exact(value, product):
    high, rest = split_two(value)
    low = (value - high.astype(F32) - rest.astype(F32)).astype(BF)
    return product(high) + product(rest) + product(low)


def unturned(value, turn):
    high, rest = split_two(value)
    return dot_nt(high, turn) + dot_nt(rest, turn)


def wide(column):
    return jnp.broadcast_to(column, (column.shape[0], 128))


def forward_refs(rows, width, units):
    return dict(
        unit_one=((rows // 2, D), F32),
        unit_two=((rows // 2, D), F32),
        hidden=((rows, units), BF),
        slope=((rows, units), BF),
    )


def forward_small(rows):
    return dict(inverse_one=((rows // 2, 128), F32), inverse_two=((rows // 2, 128), F32))


def forward_stages(r, who, first, second, spread):
    def project(t):
        first.give(t, dot_nt(r.mixed[who.chunk(t), :], r.out_proj[...]))

    def middle(t):
        rows = who.own(t) if r.residual.shape[0] == r.mixed.shape[0] else who.half(t)
        total = r.residual[rows, :].astype(F32) + first.take(t) + r.shared[r.base + 0 : r.base + 1, :]
        unit, inverse, normed = norm_forward(total, r.shared[r.base + 1 : r.base + 2, :], r.shared[r.base + 2 : r.base + 3, :])
        r.unit_one[who.half(t), :] = unit
        r.inverse_one[who.half(t), :] = wide(inverse)
        r.normed[who.half(t), :] = normed
        spread.give(t, normed)

    def feed(t):
        pre = dot(spread.take(t), r.ffn_up[...]) + r.hidden_bias
        chance = 0.5 + 0.5 * lax.erf(pre * (0.5**0.5))
        hidden = (pre * chance).astype(BF)
        r.hidden[who.chunk(t), :] = hidden
        bell = jnp.exp(-0.5 * pre * pre) * 0.3989422804014327
        r.slope[who.chunk(t), :] = (chance + pre * bell).astype(BF)
        second.give(t, dot_nt(hidden, r.ffn_down[...]))

    def final(t):
        total = r.normed[who.half(t), :] + second.take(t) + r.shared[r.base + 3 : r.base + 4, :]
        unit, inverse, result = norm_forward(total, r.shared[r.base + 4 : r.base + 5, :], r.shared[r.base + 5 : r.base + 6, :])
        r.unit_two[who.half(t), :] = unit
        r.inverse_two[who.half(t), :] = wide(inverse)
        return unit, inverse, result

    return project, middle, feed, final


def backward_stages(r, who, ends, third, mids):
    def enter(t, grad, unit, inverse):
        grad_total = norm_back(grad, unit, inverse, r.shared[r.base + 4 : r.base + 5, :])
        r.vectors[3:4, :] += column_sum(grad_total)
        r.vectors[4:5, :] += column_sum(grad * unit)
        r.vectors[5:6, :] += column_sum(grad)
        r.kept[who.half(t), :] = grad_total
        ends.give(t, grad_total)

    def feed_back(t):
        rows = who.chunk(t)
        grad = ends.take(t)
        grad_pre = (dot(grad, r.ffn_down[...]) * r.slope[rows, :].astype(F32)).astype(BF)
        r.units[0:1, :] += column_sum(grad_pre.astype(F32))
        third.give(t, dot_nt(grad_pre, r.ffn_up[...]))
        r.grad_pre[pl.ds(pl.multiple_of(lax.rem(t, 2) * CHUNK, CHUNK), CHUNK), :] = grad_pre

        @pl.when(lax.rem(t, 2) == 1)
        def _():
            both = who.two_chunks(t)
            r.sum_up[...] += dot_tn(r.spread_full[both, :], r.grad_pre[...])
            r.sum_down[...] += dot_tn(ends.r.full[both, :], r.hidden[both, :])

    def leave(t):
        grad = r.kept[who.half(t), :] + third.take(t)
        unit = r.unit_one[who.half(t), :]
        grad_total = norm_back(grad, unit, r.inverse_one[who.half(t), 0:1], r.shared[r.base + 1 : r.base + 2, :])
        r.vectors[0:1, :] += column_sum(grad_total)
        r.vectors[1:2, :] += column_sum(grad * unit)
        r.vectors[2:3, :] += column_sum(grad)
        r.grad_one[who.half(t), :] = grad_total
        mids.give(t, grad_total)

    def project_back(t):
        rows = who.chunk(t)
        grad = mids.take(t)
        r.grad_mixed[rows, :] = dot(grad, r.out_proj[...]).astype(BF)

        @pl.when(lax.rem(t, 2) == 1)
        def _():
            both = who.two_chunks(t)
            r.sum_out[...] += dot_tn(mids.r.full[both, :], r.mixed[both, :])

    return enter, feed_back, leave, project_back


def clear(*refs):
    for ref in refs:
        ref[...] = jnp.zeros_like(ref)


def finish_all(count, parts):
    def step(t, carry):
        for part in parts:
            part.finish(t)
        return carry

    lax.fori_loop(0, count, step, 0)


def packed(ref):
    return jnp.concatenate([ref[k].astype(BF) for k in range(ref.shape[0])], axis=1)


def projection_bias(split, width):
    return jnp.concatenate([split[:, :width], jnp.zeros((1, width), F32), split[:, width : 2 * width]], axis=1)


def opening(activations, segments, owners, attn_weights, ffn_weights, split_biases, shared_vectors, count):
    rows = activations.shape[0]
    width, units = attn_weights.shape[3], ffn_weights.shape[3]
    heads = width // DH
    blocks = rows // BLOCK
    lines = count // 2
    block = D // count
    layers = split_biases.shape[0]

    def body(r):
        who = Partners()
        column = Column(count)
        who.meet(column)
        wide_attn = GatherBlocks(column, SimpleNamespace(full=r.full_attn, **vars(pick(r, "ga"))))
        wide_up = GatherBlocks(column, SimpleNamespace(full=r.full_up, **vars(pick(r, "gu"))))
        wide_down = GatherPairs(column, SimpleNamespace(full=r.full_down, **vars(pick(r, "gd"))))
        halo = Halo(column, SimpleNamespace(left=r.left, right=r.right, **vars(pick(r, "halo"))), r.pair, WIN, BLOCK)
        first, last = column.index == 0, column.index == count - 1
        to_before = copy_to(r.ids, r.ids_right, r.ids_sent.at[0], r.ids_came.at[0], halo.before)
        to_after = copy_to(r.ids, r.ids_left, r.ids_sent.at[1], r.ids_came.at[1], halo.after)
        wide_attn.put(packed(r.attn.at[0]))
        wide_attn.start_line()
        wide_attn.start_pair()
        r.ids[...] = r.segments[...].astype(F32)

        @pl.when(first)
        def _():
            r.ids_left[...] = jnp.zeros_like(r.ids_left)

        @pl.when(last)
        def _():
            r.ids_right[...] = jnp.zeros_like(r.ids_right)

        @pl.when(jnp.logical_not(first))
        def _():
            to_before.start()

        @pl.when(jnp.logical_not(last))
        def _():
            to_after.start()

        halo.clear()
        wide_down.put(r.ffn[0, 1].astype(BF))
        wide_down.start_pair()
        wide_up.put(r.ffn[0, 0].astype(BF))
        for slot in range(count):
            row = lax.broadcasted_iota(jnp.int32, (block, D), 0)
            col = lax.broadcasted_iota(jnp.int32, (block, D), 1)
            target = r.owners[slot] * block + row
            r.turn[slot * block : (slot + 1) * block, :] = jnp.where(col == target, 1.0, 0.0).astype(BF)

        def sort_chunk(t, carry):
            chunk = pl.ds(pl.multiple_of(t * BLOCK, BLOCK), BLOCK)
            r.low[chunk, :] = dot(r.activations[chunk, :], r.turn[...]).astype(BF)
            return carry

        lax.fori_loop(0, blocks, sort_chunk, 0)
        wide_attn.relay(1)
        padding = jnp.zeros((16 - 6 * layers, D), F32)
        stacked = [r.shared_vectors[k, layer : layer + 1, :] for layer in range(layers) for k in range(6)]
        stacked = jnp.concatenate(stacked + [padding], axis=0)
        r.shared[...] = exact(stacked, lambda part: dot(part, r.turn[...]))
        wide_attn.relay(2)
        wide_up.start_line()

        @pl.when(jnp.logical_not(last))
        def _():
            to_before.wait_recv()

        @pl.when(jnp.logical_not(first))
        def _():
            to_after.wait_recv()

        def flat(ref):
            return jnp.concatenate([ref[k : k + 1, :] for k in range(ref.shape[0])], axis=1)

        own_ids = flat(r.ids)
        padded = jnp.concatenate([flat(r.ids_left)[:, rows - 2 * WIN :], own_ids, flat(r.ids_right)[:, : 2 * WIN]], axis=1)
        r.id_row[...] = jnp.broadcast_to(padded, r.id_row.shape)
        sort = parity_matrix()
        lap = 2 * BLOCK
        sorted_ids = [
            dot_nt(r.id_row[:, g * lap : (g + 1) * lap].astype(BF), sort) for g in range(2 * blocks // 2)
        ]
        natural = jnp.concatenate(
            [padded[:, WIN : rows + WIN], padded[:, rows - WIN : 2 * rows - WIN]], axis=1
        )
        arranged = jnp.concatenate(
            [part[0:1, :BLOCK] for part in sorted_ids] + [part[0:1, BLOCK:] for part in sorted_ids], axis=1
        )
        r.seg_keys[0:1, :] = natural
        r.seg_keys[1:2, :] = arranged
        middle = sorted_ids[1:-1]
        own_arranged = jnp.concatenate(
            [part[0:1, :BLOCK] for part in middle] + [part[0:1, BLOCK:] for part in middle], axis=1
        )
        for which, row in ((0, own_ids), (1, own_arranged)):
            for k in range(rows // 128):
                square = jnp.broadcast_to(row[:, k * 128 : (k + 1) * 128], (128, 128))
                r.seg_query[k * 128 : (k + 1) * 128, which : which + 1] = square.T[:, 0:1]

        for k in range(3, lines):
            wide_attn.relay(k)
        wide_up.start_pair()
        wide_up.relay(1)
        wide_attn.arrive()
        r.proj[...] = r.full_attn[...].reshape(D, 4 * width)[:, : 3 * width]
        bias = projection_bias(r.split[0], width)

        def project(t):
            chunk = pl.ds(pl.multiple_of(t * BLOCK, BLOCK), BLOCK)
            value = dot(r.low[chunk, :], r.proj[...]) + bias
            r.query[chunk, :] = (value[:, :width].astype(BF).astype(F32) * SCORE_SCALE).astype(BF)
            pair = value[:, width:].astype(BF)
            r.pair[chunk, :] = pair
            inner = pl.ds(pl.multiple_of((t + 1) * BLOCK, BLOCK), BLOCK)
            r.keys[inner, :] = pair[:, :width]
            r.values[inner, :] = pair[:, width:]

        def outer_project(i, carry):
            t = i * (blocks - 1)
            project(t)
            halo.send(t)
            return carry

        def inner_project(i, carry):
            project(i)
            return carry

        lax.fori_loop(0, 2, outer_project, 0)
        wide_up.relay(2)
        wide_down.begin()
        lax.fori_loop(1, blocks - 1, inner_project, 0)
        for k in range(3, lines):
            wide_up.relay(k)

        def attend_block(step):
            own = pl.ds(pl.multiple_of(step * BLOCK, BLOCK), BLOCK)
            near = pl.ds(pl.multiple_of(step * BLOCK, BLOCK), 3 * BLOCK)
            key_block, value_block, query_block = r.keys[near, :], r.values[near, :], r.query[own, :]
            mine = r.seg_query[own, 0:1]
            theirs = r.id_row[0:1, pl.ds(pl.multiple_of(step * BLOCK + BLOCK, BLOCK), 3 * BLOCK)]
            allowed = jnp.logical_and(window_mask(), mine == theirs)
            gathered = jnp.zeros((BLOCK, width), F32)
            for head, lanes in enumerate(head_lanes(heads)):
                soft = soft_weights(query_block, key_block, lanes, allowed)
                r.soft[head, own, :] = soft
                gathered = jnp.where(lanes, dot(soft, value_block), gathered)
            r.out[own, :] = gathered.astype(BF)

        def inner_attend(i, carry):
            attend_block(i)
            return carry

        def outer_attend(i, carry):
            attend_block(i * (blocks - 1))
            return carry

        lax.fori_loop(1, blocks - 1, inner_attend, 0)
        wide_down.relay(1)
        halo.arrive()
        for part, start in ((r.left, 0), (r.right, (blocks + 1) * BLOCK)):
            r.keys[pl.ds(start, BLOCK), :] = part[:, :width]
            r.values[pl.ds(start, BLOCK), :] = part[:, width:]
        lax.fori_loop(0, 2, outer_attend, 0)
        for k in range(2, lines):
            wide_down.relay(k)
        wide_up.arrive()
        halo.finish()
        for engine in (wide_attn, wide_up, wide_down):
            engine.finish()

        @pl.when(jnp.logical_not(first))
        def _():
            to_before.wait_send()

        @pl.when(jnp.logical_not(last))
        def _():
            to_after.wait_send()

    scratch = dict(
        proj=pltpu.VMEM((D, 3 * width), BF),
        pair=pltpu.VMEM((rows, 2 * width), BF),
        left=pltpu.VMEM((WIN, 2 * width), BF),
        right=pltpu.VMEM((WIN, 2 * width), BF),
        ids=pltpu.VMEM((rows // 128, 128), F32),
        ids_left=pltpu.VMEM((rows // 128, 128), F32),
        ids_right=pltpu.VMEM((rows // 128, 128), F32),
        ids_sent=pltpu.SemaphoreType.DMA((2,)),
        ids_came=pltpu.SemaphoreType.DMA((2,)),
        id_row=pltpu.VMEM((8, rows + 4 * WIN), F32),
    )
    scratch.update(prefixed("ga", gather_sems(lines)))
    scratch.update(prefixed("gu", gather_sems(lines)))
    scratch.update(prefixed("gd", gather_sems(lines)))
    scratch.update(prefixed("halo", halo_scratch(1)))
    return run_kernel(
        body,
        "opening",
        dict(
            activations=activations,
            segments=segments.reshape(rows // 128, 128),
            owners=owners,
            attn=attn_weights,
            ffn=ffn_weights,
            split=split_biases,
            shared_vectors=shared_vectors.transpose(1, 0, 2),
        ),
        dict(
            full_attn=((count, block, 4 * width), BF),
            full_up=((count, block, units), BF),
            full_down=((count, block, units), BF),
            low=((rows, D), BF),
            turn=((D, D), BF),
            shared=((16, D), F32),
            seg_query=((rows, 2), F32),
            seg_keys=((8, 2 * rows), F32),
            out=((rows, width), BF),
            query=((rows, width), BF),
            keys=((rows + 2 * BLOCK, width), BF),
            values=((rows + 2 * BLOCK, width), BF),
            soft=((heads, rows, 3 * BLOCK), BF),
        ),
        scratch,
        collective=5,
        flops=2 * rows * D * (D + 3 * width),
        in_smem=("owners",),
    )


def middle_forward(mixed, attn, ffn_up, ffn_down, residual, shared, split_biases, attn_weights, ffn_weights, count):
    rows, width = mixed.shape
    units = ffn_up.shape[1]
    chunks = rows // CHUNK
    lines = count // 2
    block = D // count

    def body(r):
        who = Partners()
        r.base = 0
        first, second = Exchange(who, pick(r, "first")), Exchange(who, pick(r, "second"))
        spread = Gather(who, SimpleNamespace(full=r.spread_full, sent=r.spread_sent, came=r.spread_came))
        last = Gather(who, SimpleNamespace(full=r.last_full, sent=r.last_sent, came=r.last_came))
        column = Column(count)
        who.meet(column)
        wide_attn = GatherBlocks(column, SimpleNamespace(full=r.full_attn, **vars(pick(r, "ga"))))
        wide_up = GatherBlocks(column, SimpleNamespace(full=r.full_up, **vars(pick(r, "gu"))))
        wide_down = GatherPairs(column, SimpleNamespace(full=r.full_down, **vars(pick(r, "gd"))))
        halo = Halo(column, SimpleNamespace(left=r.left, right=r.right, **vars(pick(r, "halo"))), r.pair, 2 * WIN, CHUNK)
        wide_attn.put(packed(r.next_attn.at[1]))
        wide_attn.start_line()
        wide_attn.start_pair()
        wide_down.put(r.next_ffn[1, 1].astype(BF))
        wide_down.start_pair()
        wide_up.put(r.next_ffn[1, 0].astype(BF))
        halo.clear()
        r.out_proj[...] = r.attn[:, 3 * width :]
        r.hidden_bias = r.split[0][:, 2 * width :]
        next_bias = projection_bias(r.split[1], width)

        def unpack():
            wide_attn.arrive()
            r.next_proj[...] = r.full_attn[...].reshape(D, 4 * width)[:, : 3 * width]

        ticks = [(3, r.late.residual.wait), (4, r.late.ffn_up.wait), (4, r.late.ffn_down.wait), (chunks, unpack)]
        ticks += [(when, lambda k=k: wide_attn.relay(k + 1)) for k, when in enumerate(GATHER_TIMES[0])]
        ticks += [(GATHER_TIMES[1][0], wide_up.start_line), (GATHER_TIMES[1][1], wide_up.start_pair)]
        ticks += [(when, lambda k=k: wide_up.relay(k + 1)) for k, when in enumerate(GATHER_TIMES[2])]
        ticks += [(GATHER_TIMES[3][0], wide_down.begin)]
        ticks += [(when, lambda k=k: wide_down.relay(k + 1)) for k, when in enumerate(GATHER_TIMES[3][1:])]
        project, middle, feed, final = forward_stages(r, who, first, second, spread)

        def middle_out(t):
            middle(t)
            r.flush.unit_one.copy(who.half(t), t).start()

        def feed_out(t):
            feed(t)
            for flush in (r.flush.hidden, r.flush.slope, r.flush.spread_full):
                flush.copy(who.chunk(t), t).start()

        def close(t):
            _, _, result = final(t)
            r.result[who.half(t), :] = result
            for flush in (r.flush.unit_two, r.flush.result):
                flush.copy(who.half(t), t).start()
            last.give(t, result)

        def next_project(t):
            value = (dot(last.take(t), r.next_proj[...]) + next_bias).astype(BF)
            r.query[who.chunk(t), :] = value[:, :width]
            r.pair[who.chunk(t), :] = value[:, width:]
            halo.send(t)
            r.flush.last_full.copy(who.chunk(t), t).start()

        run_stages(
            chunks,
            [
                (5, second.add),
                (1, first.add),
                (7, close),
                (3, middle_out),
                (8, next_project),
                (4, feed_out),
                (0, project),
            ],
            ticks,
        )
        finish_all(chunks, (first, second, spread, last))
        halo.arrive()
        wide_up.arrive()
        halo.finish()
        for engine in (wide_attn, wide_up, wide_down):
            engine.finish()

        def written(t, carry):
            for flush in (r.flush.hidden, r.flush.slope, r.flush.spread_full, r.flush.last_full):
                flush.copy(who.chunk(t), t).wait()
            for flush in (r.flush.unit_one, r.flush.unit_two, r.flush.result):
                flush.copy(who.half(t), t).wait()
            return carry

        lax.fori_loop(0, chunks, written, 0)

    outputs = forward_small(rows)
    outputs.update(
        query=((rows, width), BF),
        pair=((rows, 2 * width), BF),
        full_attn=((count, block, 4 * width), BF),
        full_up=((count, block, units), BF),
        full_down=((count, block, units), BF),
        left=((2 * WIN, 2 * width), BF),
        right=((2 * WIN, 2 * width), BF),
    )
    flushed = forward_refs(rows, width, units)
    flushed.update(spread_full=((rows, D), BF), last_full=((rows, D), BF), result=((rows // 2, D), F32))
    scratch = dict(
        normed=pltpu.VMEM((rows // 2, D), F32),
        out_proj=pltpu.VMEM((D, width), BF),
        next_proj=pltpu.VMEM((D, 3 * width), BF),
    )
    scratch.update(prefixed("first", exchange_scratch(rows)))
    scratch.update(prefixed("second", exchange_scratch(rows)))
    for key in ("spread", "last"):
        for part in ("sent", "came"):
            scratch[key + "_" + part] = pltpu.SemaphoreType.DMA((chunks,))
    for key in ("ga", "gu", "gd"):
        scratch.update(prefixed(key, gather_sems(lines)))
    scratch.update(prefixed("halo", halo_scratch(2 * WIN // CHUNK)))
    return run_kernel(
        body,
        "middle_forward",
        dict(
            mixed=mixed,
            attn=attn,
            shared=shared,
            split=split_biases,
            next_attn=attn_weights,
            next_ffn=ffn_weights,
        ),
        outputs,
        scratch,
        collective=1,
        flops=2 * rows * D * (4 * width + 2 * units),
        late=dict(residual=residual, ffn_up=ffn_up, ffn_down=ffn_down),
        flushed=flushed,
        pieces=chunks,
    )


def turning(mixed, attn, ffn_up, ffn_down, residual, shared, split_biases, cotangent, turn):
    rows, width = mixed.shape
    units = ffn_up.shape[1]
    chunks = rows // CHUNK

    def body(r):
        who = Partners()
        r.base = 6
        first, second = Exchange(who, pick(r, "first")), Exchange(who, pick(r, "second"))
        third = Exchange(who, pick(r, "third"))
        spread = Gather(who, pick(r, "spread"))
        ends, mids = Gather(who, pick(r, "ends")), Gather(who, pick(r, "mids"))
        out = Gather(who, SimpleNamespace(full=r.output, sent=r.out_sent, came=r.out_came))
        who.meet()
        r.out_proj[...] = r.attn[:, 3 * width :]
        r.hidden_bias = r.split[1][:, 2 * width :]
        clear(r.vectors, r.units, r.sum_up, r.sum_down, r.sum_out)
        project, middle, feed, final = forward_stages(r, who, first, second, spread)
        enter, feed_back, leave, project_back = backward_stages(r, who, ends, third, mids)

        ticks = [(3, r.late.residual.wait), (4, r.late.ffn_up.wait), (4, r.late.ffn_down.wait)]
        ticks += [(7, r.late.cotangent.wait), (7, r.late.turn.wait)]

        def close(t):
            unit, inverse, result = final(t)
            grad = dot(r.cotangent[who.own(t), :], r.turn[...])
            enter(t, grad, unit, inverse)
            out.give(t, unturned(result, r.turn[...]))

        run_stages(
            chunks,
            [
                (9, third.add),
                (5, second.add),
                (1, first.add),
                (11, leave),
                (7, close),
                (3, middle),
                (12, project_back),
                (8, feed_back),
                (4, feed),
                (0, project),
            ],
            ticks,
        )

        def arrive(t, carry):
            out.wait(t)
            return carry

        lax.fori_loop(0, chunks, arrive, 0)
        finish_all(chunks, (first, second, third, spread, ends, mids, out))
        r.up[...] = r.sum_up[...].astype(BF)
        r.down[...] = r.sum_down[...].astype(BF)
        r.proj[...] = r.sum_out[...].astype(BF)

    outputs = dict(
        output=((rows, D), F32),
        up=((D, units), BF),
        down=((D, units), BF),
        proj=((D, width), BF),
        grad_one=((rows // 2, D), F32),
        grad_mixed=((rows, width), BF),
        vectors=((8, D), F32),
        units=((8, units), F32),
    )
    scratch = dict(
        normed=pltpu.VMEM((rows // 2, D), F32),
        kept=pltpu.VMEM((rows // 2, D), F32),
        grad_pre=pltpu.VMEM((2 * CHUNK, units), BF),
        out_proj=pltpu.VMEM((D, width), BF),
        sum_up=pltpu.VMEM((D, units), F32),
        sum_down=pltpu.VMEM((D, units), F32),
        sum_out=pltpu.VMEM((D, width), F32),
        out_sent=pltpu.SemaphoreType.DMA((chunks,)),
        out_came=pltpu.SemaphoreType.DMA((chunks,)),
    )
    for key, (shape, dtype) in {**forward_refs(rows, width, units), **forward_small(rows)}.items():
        scratch[key] = pltpu.VMEM(shape, dtype)
    for key in ("first", "second", "third"):
        scratch.update(prefixed(key, exchange_scratch(rows)))
    for key in ("spread", "ends", "mids"):
        scratch.update(prefixed(key, gather_scratch(rows)))
    return run_kernel(
        body,
        "turning",
        dict(
            mixed=mixed,
            attn=attn,
            shared=shared,
            split=split_biases,
        ),
        outputs,
        scratch,
        collective=2,
        flops=2 * rows * D * (3 * width + 6 * units),
        late=dict(residual=residual, ffn_up=ffn_up, ffn_down=ffn_down, cotangent=cotangent, turn=turn),
    )


def projection_back_stage(r, who, column, exchange):
    rows, width = r.grad_query.shape
    rim = r.out_right.shape[0]
    first, last = column.index == 0, column.index == column.count - 1
    after = (lax.rem(column.index + 1, column.count), column.here)
    copy = copy_to(r.out_right, r.from_left, r.halo_sent.at[0], r.halo_came.at[0], after)

    def begin():
        r.grad_pair[...] = r.grad_own[...]

        @pl.when(jnp.logical_not(last))
        def _():
            copy.start()

    def absorb():
        @pl.when(jnp.logical_not(first))
        def _():
            copy.wait_recv()
            where = pl.ds(0, rim)
            total = r.grad_pair[where, :].astype(F32) + r.from_left[...].astype(F32)
            r.grad_pair[where, :] = total.astype(BF)

    def end():
        @pl.when(jnp.logical_not(last))
        def _():
            copy.wait_send()

    def stage(k):
        both = who.two_chunks(2 * k + 1)
        parts = jnp.concatenate([r.grad_query[both, :], r.grad_pair[both, :]], axis=1)
        exchange.r.part[both, :] = dot_nt(parts, r.next_attn[:, : 3 * width]).astype(BF)
        for t in (2 * k, 2 * k + 1):
            exchange.core_copy(t).start()
        r.sum_three[...] += dot_tn(r.low[both, :], parts)
        r.biases[0:1, :] += column_sum(parts.astype(F32))

    half = rows // CHUNK // 2
    steps = [(0 if k < half // 2 else half, k) for k in range(half)]
    ticks = [(half, absorb)] + [(first_time + k % (half // 2), lambda k=k: stage(k)) for first_time, k in steps]
    return begin, end, ticks


def projection_back_scratch(rows, rim, width):
    return dict(
        grad_pair=pltpu.VMEM((rows, 2 * width), BF),
        from_left=pltpu.VMEM((rim, 2 * width), BF),
        halo_sent=pltpu.SemaphoreType.DMA((1,)),
        halo_came=pltpu.SemaphoreType.DMA((1,)),
        sum_three=pltpu.VMEM((D, 3 * width), F32),
    )


def scatter_three(column, r, totals):
    return (
        ScatterPairs(column, SimpleNamespace(grads=r.above_up, **vars(pick(r, "ru"))), totals[0]),
        ScatterBlocks(column, SimpleNamespace(grads=r.above_down, **vars(pick(r, "rd"))), totals[1]),
        ScatterBlocks(column, SimpleNamespace(grads=r.packed, **vars(pick(r, "ra"))), totals[2]),
    )


def scatter_three_scratch(count, width, units):
    lines, block = count // 2, D // count
    scratch = dict(packed=pltpu.VMEM((count, block, 4 * width), BF))
    scratch.update(prefixed("ru", scatter_pairs_scratch(lines, block, units)))
    scratch.update(prefixed("rd", scatter_scratch(lines, block, units)))
    scratch.update(prefixed("ra", scatter_scratch(lines, block, 4 * width, held=False)))
    return scratch


def pack_attention(r):
    both = jnp.concatenate([r.sum_three[...].astype(BF), r.above_proj[...]], axis=1)
    r.packed[...] = both.reshape(r.packed.shape)


def middle_backward(back, next_attn, grad_above, low, saved, mixed, attn, ffn_up, ffn_down, shared, above, count):
    rows, width = mixed.shape
    units = ffn_up.shape[1]
    chunks = rows // CHUNK
    block = D // count
    rim = back.out_right.shape[0]

    def body(r):
        who = Partners(chunks, chunks // 2)
        r.base = 0
        zeroth, third = Exchange(who, pick(r, "zeroth")), Exchange(who, pick(r, "third"))
        ends, mids = Gather(who, pick(r, "ends")), Gather(who, pick(r, "mids"))
        column = Column(count)
        who.meet(column)
        up, down, three = scatter_three(column, r, (r.up_total, r.down_total, r.attn_total))
        begin, end, back_ticks = projection_back_stage(r, who, column, zeroth)
        begin()
        up.start()
        down.start()

        def start_three():
            pack_attention(r)
            three.start()

        ticks = [tick for engine, times in zip((up, down, three), BACK_TIMES) for tick in engine.ticks(times)]
        ticks += [(chunks // 2 + 2, start_three)]
        ticks += [(3, r.late.unit_two.wait), (3, r.late.grad_above.wait), (4, r.late.ffn_up.wait)]
        ticks += [(4, r.late.ffn_down.wait), (4, r.late.slope.wait), (4, r.late.hidden.wait)]
        ticks += [(4, r.late.spread_full.wait), (7, r.late.unit_one.wait), (8, r.late.mixed.wait)]
        ticks = back_ticks + ticks
        r.out_proj[...] = r.attn[:, 3 * width :]
        clear(r.vectors, r.units, r.biases, r.sum_up, r.sum_down, r.sum_out, r.sum_three)
        enter, feed_back, leave, project_back = backward_stages(r, who, ends, third, mids)

        def start(t):
            half = who.half(t)
            enter(t, r.grad_above[half, :] + zeroth.take(t), r.unit_two[half, :], r.inverse_two[half, 0:1])

        run_stages(
            chunks,
            [
                (5, third.add),
                (1, zeroth.add),
                (7, leave),
                (3, start),
                (8, project_back),
                (4, feed_back),
            ],
            ticks,
        )
        finish_all(chunks, (zeroth, third, ends, mids))
        end()
        r.up[...] = r.sum_up[...].astype(BF)
        r.down[...] = r.sum_down[...].astype(BF)
        r.proj[...] = r.sum_out[...].astype(BF)
        for engine in (up, down, three):
            engine.finish()

    outputs = dict(
        up=((D, units), BF),
        down=((D, units), BF),
        proj=((D, width), BF),
        grad_one=((rows // 2, D), F32),
        grad_mixed=((rows, width), BF),
        vectors=((8, D), F32),
        units=((8, units), F32),
        biases=((8, 3 * width), F32),
        up_total=((block, units), F32),
        down_total=((block, units), F32),
        attn_total=((block, 4 * width), F32),
    )
    scratch = dict(
        kept=pltpu.VMEM((rows // 2, D), F32),
        grad_pre=pltpu.VMEM((2 * CHUNK, units), BF),
        out_proj=pltpu.VMEM((D, width), BF),
        sum_up=pltpu.VMEM((D, units), F32),
        sum_down=pltpu.VMEM((D, units), F32),
        sum_out=pltpu.VMEM((D, width), F32),
    )
    scratch.update(projection_back_scratch(rows, rim, width))
    scratch.update(scatter_three_scratch(count, width, units))
    for key in ("zeroth", "third"):
        scratch.update(prefixed(key, exchange_scratch(rows)))
    for key in ("ends", "mids"):
        scratch.update(prefixed(key, gather_scratch(rows)))
    return run_kernel(
        body,
        "middle_backward",
        dict(
            grad_query=back.out_query,
            grad_own=back.out_own,
            out_right=back.out_right,
            next_attn=next_attn,
            low=low,
            inverse_one=saved.inverse_one,
            inverse_two=saved.inverse_two,
            attn=attn,
            shared=shared,
            above_up=above.up.reshape(count, block, units),
            above_down=above.down.reshape(count, block, units),
            above_proj=above.proj,
        ),
        outputs,
        scratch,
        collective=3,
        flops=2 * rows * D * (8 * width + 4 * units),
        in_hbm=("above_up", "above_down"),
        late=dict(
            unit_two=saved.unit_two,
            grad_above=grad_above,
            ffn_down=ffn_down,
            slope=saved.slope,
            ffn_up=ffn_up,
            hidden=saved.hidden,
            spread_full=saved.spread_full,
            unit_one=saved.unit_one,
            mixed=mixed,
        ),
    )


class SmallSum:
    def __init__(self, who, column, refs):
        self.who, self.c, self.r = who, column, refs

    def copy(self, slot, source, device):
        r = self.r
        return copy_to(r.kept.at[source], r.came.at[slot], r.sent_sem.at[slot], r.came_sem.at[slot], device)

    def core_copy(self):
        return self.copy(0, 0, self.who.sibling)

    def pair_copy(self):
        return self.copy(1, 1, self.c.at(self.c.outer, 1 - self.c.inner))

    def line_copy(self, target, slot):
        c, r = self.c, self.r
        return copy_to(
            r.kept.at[2], r.came.at[2 + slot], r.sent_sem.at[2 + target], r.came_sem.at[2 + slot], c.at(target, c.inner)
        )

    def second(self, both):
        r = self.r
        self.core_copy().wait_recv()
        row = lax.broadcasted_iota(jnp.int32, r.kept.shape[1:], 0)
        r.kept[1] = r.kept[0] + jnp.where(row < both, r.came[0], 0.0)
        self.pair_copy().start()

    def third(self):
        r, c = self.r, self.c
        self.pair_copy().wait_recv()
        r.kept[2] = r.kept[1] + r.came[1]
        for k in range(1, c.lines):
            self.line_copy(c.turn(k), c.outer).start()
        r.came[2 + c.outer] = r.kept[2]

    def result(self):
        r, c = self.r, self.c
        for k in range(1, c.lines):
            source = c.turn(k)
            self.line_copy(source, source).wait_recv()
        return sum(r.came[2 + k] for k in range(c.lines))

    def finish(self):
        c = self.c
        self.core_copy().wait_send()
        self.pair_copy().wait_send()
        for k in range(1, c.lines):
            self.line_copy(c.turn(k), c.outer).wait_send()


def small_scratch(lines, shape):
    return dict(
        kept=pltpu.VMEM((3,) + shape, F32),
        came=pltpu.VMEM((2 + lines,) + shape, F32),
        sent_sem=pltpu.SemaphoreType.DMA((2 + lines,)),
        came_sem=pltpu.SemaphoreType.DMA((2 + lines,)),
    )


class NormSum:
    def __init__(self, who, column, refs):
        self.who, self.c, self.r = who, column, refs

    def mp_copy(self, device, target, slot):
        r = self.r
        return copy_to(r.mp_came.at[slot], r.mp_came.at[slot], r.mp_sent.at[target], r.mp_sem.at[slot], device)

    def seq_copy(self, device, target, slot):
        r = self.r
        return copy_to(r.seq_came.at[slot], r.seq_came.at[slot], r.seq_sent.at[target], r.seq_sem.at[slot], device)

    def run(self, value):
        who, c, r = self.who, self.c, self.r
        here = c.here
        r.mp_came[here] = jnp.full((8, 128), 1.0, F32) * value
        for k in range(1, 4):
            target = lax.rem(here + k, 4)
            self.mp_copy((c.index, target), target, here).start()
        for k in range(1, 4):
            source = lax.rem(here + k, 4)
            self.mp_copy((c.index, source), source, source).wait_recv()
        r.seq_came[c.index] = sum(r.mp_came[k] for k in range(4))
        for k in range(1, c.count):
            target = lax.rem(c.index + k, c.count)
            self.seq_copy((target, here), target, c.index).start()
        for k in range(1, c.count):
            source = lax.rem(c.index + k, c.count)
            self.seq_copy((source, here), source, source).wait_recv()
        total = sum(r.seq_came[k] for k in range(c.count))
        for k in range(1, 4):
            target = lax.rem(here + k, 4)
            self.mp_copy((c.index, target), target, here).wait_send()
        for k in range(1, c.count):
            target = lax.rem(c.index + k, c.count)
            self.seq_copy((target, here), target, c.index).wait_send()
        return total


def norm_scratch(count):
    return dict(
        mp_came=pltpu.VMEM((4, 8, 128), F32),
        mp_sent=pltpu.SemaphoreType.DMA((4,)),
        mp_sem=pltpu.SemaphoreType.DMA((4,)),
        seq_came=pltpu.VMEM((count, 8, 128), F32),
        seq_sent=pltpu.SemaphoreType.DMA((count,)),
        seq_sem=pltpu.SemaphoreType.DMA((count,)),
    )


def squares(ref):
    value = ref[...]
    return jnp.sum(value * value)


def ending(back, next_attn, grad_above, low, turn, above, top, count):
    rows, width = back.out_query.shape
    chunks = rows // CHUNK
    lines, block = count // 2, D // count
    units = above.units.shape[1]
    rim = back.out_right.shape[0]

    def body(r):
        who = Partners(chunks, chunks // 2)
        zeroth = Exchange(who, pick(r, "zeroth"))
        out = Gather(who, SimpleNamespace(full=r.output, sent=r.out_sent, came=r.out_came))
        column = Column(count)
        who.meet(column)
        up, down, three = scatter_three(column, r, (r.ffn_grads.at[0], r.ffn_grads.at[1], r.attn_grads.at[0]))
        small = SmallSum(who, column, pick(r, "small"))
        begin, end, back_ticks = projection_back_stage(r, who, column, zeroth)
        begin()
        up.start()
        down.start()

        def start_three():
            pack_attention(r)
            three.start()
            r.small_kept[0, 0:6, :] = r.vectors_low[0:6, :]
            r.small_kept[0, 6:12, :] = r.vectors_top[0:6, :]
            r.small_kept[0, 12:13, :] = r.units_low[0:1, :]
            r.small_kept[0, 13:14, :] = r.units_top[0:1, :]
            pieces = []
            for ref in (r.biases, r.biases_top):
                pieces += [ref[0:1, :width], ref[0:1, 2 * width :]]
            r.small_kept[0, 14:15, :] = jnp.concatenate(pieces, axis=1)
            r.small_kept[0, 15:16, :] = jnp.zeros((1, D), F32)
            small.core_copy().start()

        ticks = [tick for engine, times in zip((up, down, three), END_TIMES) for tick in engine.ticks(times)]
        ticks += [(chunks // 2 + 2, start_three), (3, r.late.grad_above.wait), (3, r.late.turn.wait)]
        ticks += [(chunks // 2 + 4, lambda: small.second(12)), (chunks // 2 + 6, small.third)]
        ticks = back_ticks + ticks
        clear(r.biases, r.sum_three)

        def close(t):
            out.give(t, unturned(r.grad_above[who.half(t), :] + zeroth.take(t), r.turn[...]))

        run_stages(chunks, [(1, zeroth.add), (3, close)], ticks)
        vectors = small.result()
        r.vectors[...] = vectors
        r.ffn_grads[2] = r.up_top[...]
        r.ffn_grads[3] = r.down_top[...]
        r.attn_grads[1] = r.attn_top[...]
        row = lax.broadcasted_iota(jnp.int32, (16, D), 0)
        squared = vectors * vectors
        split = jnp.sum(jnp.where(row >= 12, squared, 0.0))
        shared = jnp.sum(jnp.where(row < 12, squared, 0.0))
        first_seq = column.index == 0
        first_both = jnp.logical_and(first_seq, column.here == 0)
        value = squares(r.ffn_grads) + squares(r.attn_grads)
        value = value + jnp.where(first_seq, split, 0.0) + jnp.where(first_both, shared, 0.0)
        total = NormSum(who, column, pick(r, "norm")).run(value)
        r.norm[...] = jnp.sqrt(total)

        def arrive(t, carry):
            out.wait(t)
            return carry

        lax.fori_loop(0, chunks, arrive, 0)
        finish_all(chunks, (zeroth, out))
        end()
        for engine in (up, down, three, small):
            engine.finish()

    outputs = dict(
        output=((rows, D), F32),
        ffn_grads=((4, block, units), F32),
        attn_grads=((2, block, 4 * width), F32),
        vectors=((16, D), F32),
        norm=((8, 128), F32),
    )
    scratch = dict(
        biases=pltpu.VMEM((8, 3 * width), F32),
        out_sent=pltpu.SemaphoreType.DMA((chunks,)),
        out_came=pltpu.SemaphoreType.DMA((chunks,)),
    )
    scratch.update(projection_back_scratch(rows, rim, width))
    scratch.update(scatter_three_scratch(count, width, units))
    scratch.update(prefixed("zeroth", exchange_scratch(rows)))
    scratch.update(prefixed("small", small_scratch(lines, (16, D))))
    scratch.update(prefixed("norm", norm_scratch(count)))
    return run_kernel(
        body,
        "ending",
        dict(
            grad_query=back.out_query,
            grad_own=back.out_own,
            out_right=back.out_right,
            next_attn=next_attn,
            low=low,
            above_up=above.up.reshape(count, block, units),
            above_down=above.down.reshape(count, block, units),
            above_proj=above.proj,
            up_top=above.up_total,
            down_top=above.down_total,
            attn_top=above.attn_total,
            vectors_low=above.vectors,
            vectors_top=top.vectors,
            units_low=above.units,
            units_top=top.units,
            biases_top=above.biases,
        ),
        outputs,
        scratch,
        collective=4,
        flops=2 * rows * D * 6 * width,
        in_hbm=("above_up", "above_down"),
        late=dict(grad_above=grad_above, turn=turn),
    )


def moments(grad, first, second):
    first_new = BETA_FIRST * first + (1.0 - BETA_FIRST) * grad
    second_new = BETA_SECOND * second + (1.0 - BETA_SECOND) * grad * grad
    size = jnp.sqrt(second_new / (1.0 - BETA_SECOND**STEP)) + ADAM_EPSILON
    return first_new, second_new, first_new / (1.0 - BETA_FIRST**STEP) / size


def update(end, turn, attn, ffn, split, shared):
    block, units = ffn[0].shape[2:]
    width = attn[0].shape[3]
    rates = [0.5 * D ** (-0.5)] * 3 + [0.5 * (WIN / D) ** 0.5]
    names = ("weights", "first", "second", "average", "basis")

    def matrix(grad, weight, first, second, average, basis, rate):
        basis = basis.astype(BF)
        turned = dot(grad.astype(BF), basis)
        first_new, second_new, direction = moments(turned, first, second)
        back = dot_nt(direction.astype(BF), basis)
        weight_new = weight - rate * (back + DECAY_RATE * weight)
        return weight_new, first_new, second_new, AVERAGE_RATE * average + (1.0 - AVERAGE_RATE) * weight_new

    def body(r):
        step = pl.program_id(0)
        factor = CLIP_LEVEL / jnp.maximum(r.norm[0:1, 0:1], CLIP_LEVEL)
        rate = jnp.where(step % 2 == 0, 0.5 * D ** (-0.5), 0.5 * FF ** (-0.5))
        results = matrix(
            factor * r.ffn_grads[...],
            r.ffn_weights[...],
            r.ffn_first[...],
            r.ffn_second[...],
            r.ffn_average[...],
            r.ffn_basis[...],
            rate,
        )
        for key, value in zip(names, results):
            getattr(r, "ffn_" + key + "_new")[...] = value

        for at in range(4):

            @pl.when(step == at)
            def _(at=at):
                layer = at // 2
                for which in (2 * (at % 2), 2 * (at % 2) + 1):
                    grad = factor * r.attn_grads[layer, :, which * width : (which + 1) * width]
                    weight, first, second, average = matrix(
                        grad,
                        r.attn_weights[layer, which],
                        r.attn_first[layer, which],
                        r.attn_second[layer, which],
                        r.attn_average[layer, which],
                        r.attn_basis[layer, which, 0, 0],
                        rates[which],
                    )
                    r.attn_weights_new[layer, which] = weight
                    r.attn_first_new[layer, which] = first
                    r.attn_average_new[layer, which] = average
                    if which < 3:
                        r.attn_second_new[layer, which] = second
                    else:
                        r.projection_second[layer] = second

        @pl.when(step == 0)
        def _():
            r.norm_out[0, 0] = jnp.max(r.norm[0:1, :])
            real = exact(r.vectors[...], lambda part: dot_nt(part, r.turn[...]))
            for layer in range(2):
                tail = r.vectors[14:15, layer * 2 * width : (layer + 1) * 2 * width]
                split_grad = jnp.concatenate([tail, r.vectors[12 + layer : 13 + layer, :]], axis=1)
                grad = factor * split_grad
                first_new, second_new, direction = moments(grad, r.split_first[layer], r.split_second[layer])
                r.split_old_new[layer] = r.split_old[layer] - VECTOR_RATE * direction
                r.split_first_new[layer] = first_new
                r.split_second_new[layer] = second_new
            for k in range(6):
                grad = factor * jnp.concatenate([real[k : k + 1], real[6 + k : 7 + k]], axis=0)
                first_new, second_new, direction = moments(grad, r.shared_first[k], r.shared_second[k])
                r.shared_old_new[k] = r.shared_old[k] - VECTOR_RATE * direction
                r.shared_first_new[k] = first_new
                r.shared_second_new[k] = second_new

    inputs = dict(
        ffn_grads=end.ffn_grads, attn_grads=end.attn_grads, vectors=end.vectors, norm=end.norm, turn=turn
    )
    outputs, specs = {}, {}
    specs["ffn_grads"] = pl.BlockSpec((None, block, units), lambda i: (i, 0, 0))
    matrix_spec = pl.BlockSpec((None, None, block, units), lambda i: (i // 2, i % 2, 0, 0))
    for key, array in zip(names, ffn):
        inputs["ffn_" + key] = array
        specs["ffn_" + key] = matrix_spec
    specs["ffn_basis"] = pl.BlockSpec((None, None, None, None, units, units), lambda i: (i // 2, i % 2, 0, 0, 0, 0))
    for key, array in zip(names, attn):
        inputs["attn_" + key] = array
    for prefix, group in (("split", split), ("shared", shared)):
        for key, array in zip(("old", "first", "second"), group):
            inputs[prefix + "_" + key] = array
    for key in ("weights", "first", "second", "average"):
        outputs["ffn_" + key + "_new"] = (ffn[0].shape, F32)
        specs["ffn_" + key + "_new"] = matrix_spec
        outputs["attn_" + key + "_new"] = (attn[0].shape, F32)
    outputs["attn_second_new"] = ((2, 3, block, width), F32)
    outputs["projection_second"] = ((2, block, width), F32)
    for prefix, group in (("split", split), ("shared", shared)):
        for key in ("old", "first", "second"):
            outputs[prefix + "_" + key + "_new"] = (group[0].shape, F32)
    outputs["norm_out"] = ((1, 1), F32)
    return run_kernel(
        body,
        "update",
        inputs,
        outputs,
        {},
        flops=4 * block * units * units * 4,
        grid=(4,),
        specs=specs,
        in_smem=("norm_out",),
    )


def direct(
    activations,
    cotangent,
    segments,
    dilated_heads,
    owners,
    attn_weights,
    attn_first,
    attn_second,
    attn_average,
    attn_basis,
    ffn_weights,
    ffn_first,
    ffn_second,
    ffn_average,
    ffn_basis,
    split_biases,
    split_first,
    split_second,
    shared_vectors,
    shared_first,
    shared_second,
):
    count = lax.axis_size(SEQ)
    near = opening(
        activations, segments, owners, attn_weights, ffn_weights, split_biases, shared_vectors, count
    )
    near.arranged = near.out
    attn_zero, up_zero, down_zero = (
        full.reshape(D, -1) for full in (near.full_attn, near.full_up, near.full_down)
    )
    mid = middle_forward(
        near.out,
        attn_zero,
        up_zero,
        down_zero,
        near.low,
        near.shared,
        split_biases,
        attn_weights,
        ffn_weights,
        count,
    )
    attn_one, up_one, down_one = (full.reshape(D, -1) for full in (mid.full_attn, mid.full_up, mid.full_down))
    far = attend(mid.query, mid.pair, mid.left, mid.right, near.seg_query, near.seg_keys, dilated_heads)
    top = turning(
        far.out, attn_one, up_one, down_one, mid.result, near.shared, split_biases, cotangent, near.turn
    )
    far_back = attend_back(far, top.grad_mixed, dilated_heads, 2 * WIN, True, count, 6)
    low = middle_backward(
        far_back,
        attn_one,
        top.grad_one,
        mid.last_full,
        mid,
        near.out,
        attn_zero,
        up_zero,
        down_zero,
        near.shared,
        top,
        count,
    )
    near_back = attend_back(near, low.grad_mixed, dilated_heads, WIN, False, count, 7)
    end = ending(near_back, attn_zero, low.grad_one, near.low, near.turn, low, top, count)
    new = update(
        end,
        near.turn,
        (attn_weights, attn_first, attn_second, attn_average, attn_basis),
        (ffn_weights, ffn_first, ffn_second, ffn_average, ffn_basis),
        (split_biases, split_first, split_second),
        tuple(array.transpose(1, 0, 2) for array in (shared_vectors, shared_first, shared_second)),
    )
    return (
        top.output,
        end.output,
        new.attn_weights_new,
        new.attn_first_new,
        new.attn_second_new,
        new.projection_second,
        new.attn_average_new,
        new.ffn_weights_new,
        new.ffn_first_new,
        new.ffn_second_new,
        new.ffn_average_new,
        new.split_old_new,
        new.split_first_new,
        new.split_second_new,
        new.shared_old_new.transpose(1, 0, 2),
        new.shared_first_new.transpose(1, 0, 2),
        new.shared_second_new.transpose(1, 0, 2),
        new.norm_out.reshape(()),
    )


def with_halo(cells, sides, width):
    for axis, dim in sides:
        count = lax.axis_size(axis)
        ends = count - 1
        head = lax.slice_in_dim(cells, 0, width, axis=dim)
        tail = lax.slice_in_dim(cells, cells.shape[dim] - width, cells.shape[dim], axis=dim)
        cells = jnp.concatenate(
            [
                lax.ppermute(tail, axis, [(i, (i + 1) % count) for i in range(ends)]),
                cells,
                lax.ppermute(head, axis, [((i + 1) % count, i) for i in range(ends)]),
            ],
            axis=dim,
        )
    return cells


def from_behind(block, axis, distance):
    devices = range(lax.axis_size(axis))
    route = [(i - distance, i) for i in devices if i - distance in devices]
    return lax.ppermute(block, axis, route)


def normalize_layer(values, gain, shift):
    center = values - jnp.mean(values, axis=-1, keepdims=True)
    spread = jnp.mean(center * center, axis=-1, keepdims=True)
    return center * lax.rsqrt(spread + NORM_EPSILON) * gain + shift


def head_masks(offsets, dilated):
    near = jnp.abs(offsets) <= WIN
    far = jnp.logical_and(jnp.abs(offsets) <= 2 * WIN, offsets % 2 == 0)
    return jnp.where(dilated[:, None, None], far[None, :, :], near[None, :, :])


def join_heads(term):
    return lax.psum(term.astype(jnp.bfloat16), MP).astype(jnp.float32)


def join_grads(term):
    return lax.psum(term, MP)


def fetch_rims(pair, rim_width):
    return with_halo(pair, ((SEQ, 0),), rim_width)


def masked_scores(query_block, key_block, seg_query, seg_keys, dilated, rim_width):
    block_rows = query_block.shape[0]
    key_rows = key_block.shape[0]
    offsets = (
        jnp.arange(block_rows, dtype=jnp.int32)[:, None]
        - jnp.arange(key_rows, dtype=jnp.int32)[None, :]
        + rim_width
    )
    allowed = jnp.logical_and(
        head_masks(offsets, dilated), (seg_query[:, None] == seg_keys[None, :])[None, :, :]
    )
    raw = jnp.einsum(
        "qhd,khd->hqk", query_block, key_block, preferred_element_type=jnp.float32
    ) * DH ** (-0.5)
    return jnp.where(allowed, raw, MASK_FILL)


def plain_attend(query, key_pad, value_pad, seg_own, seg_near, dilated, rim_width):
    row_count = query.shape[0]
    block_rows = min(512, row_count)
    key_rows = block_rows + 2 * rim_width

    def one_block(first_row):
        query_block = lax.dynamic_slice_in_dim(query, first_row, block_rows, 0)
        key_block = lax.dynamic_slice_in_dim(key_pad, first_row, key_rows, 0)
        value_block = lax.dynamic_slice_in_dim(value_pad, first_row, key_rows, 0)
        scores = masked_scores(
            query_block,
            key_block,
            lax.dynamic_slice_in_dim(seg_own, first_row, block_rows, 0),
            lax.dynamic_slice_in_dim(seg_near, first_row, key_rows, 0),
            dilated,
            rim_width,
        )
        row_max = jnp.max(scores, axis=2, keepdims=True)
        exponent = jnp.exp(scores - row_max)
        row_total = jnp.sum(exponent, axis=2, keepdims=True)
        softmax = (exponent / row_total).astype(jnp.bfloat16)
        mixed_block = jnp.einsum(
            "hqk,khd->qhd", softmax, value_block, preferred_element_type=jnp.float32
        )
        return (mixed_block, (row_max + jnp.log(row_total))[:, :, 0])

    starts = jnp.arange(row_count // block_rows, dtype=jnp.int32) * block_rows
    mixed_heads, log_totals = lax.map(one_block, starts)
    return (mixed_heads.reshape(row_count, -1), log_totals)


def plain_attend_back(query, padded, log_totals, grad_mixed, seg_own, seg_near, dilated, rim_width):
    row_count, head_count, _ = query.shape
    head_width = head_count * DH
    block_rows = min(512, row_count)
    key_rows = block_rows + 2 * rim_width
    key_pad = padded[:, :head_width].reshape(-1, head_count, DH)
    value_pad = padded[:, head_width:].reshape(-1, head_count, DH)
    grad_heads = grad_mixed.reshape(row_count, head_count, DH)
    score_scale = DH ** (-0.5)

    def one_step(carry, inputs):
        first_row, totals_block = inputs
        query_block = lax.dynamic_slice_in_dim(query, first_row, block_rows, 0)
        key_block = lax.dynamic_slice_in_dim(key_pad, first_row, key_rows, 0)
        value_block = lax.dynamic_slice_in_dim(value_pad, first_row, key_rows, 0)
        grad_block = lax.dynamic_slice_in_dim(grad_heads, first_row, block_rows, 0)
        scores = masked_scores(
            query_block,
            key_block,
            lax.dynamic_slice_in_dim(seg_own, first_row, block_rows, 0),
            lax.dynamic_slice_in_dim(seg_near, first_row, key_rows, 0),
            dilated,
            rim_width,
        )
        softmax = jnp.exp(scores - totals_block[:, :, None])
        grad_value = jnp.einsum(
            "hqk,qhd->khd",
            softmax.astype(jnp.bfloat16),
            grad_block,
            preferred_element_type=jnp.float32,
        )
        grad_soft = jnp.einsum(
            "qhd,khd->hqk", grad_block, value_block, preferred_element_type=jnp.float32
        )
        row_dot = jnp.sum(grad_soft * softmax, axis=2, keepdims=True)
        grad_scores = (softmax * (grad_soft - row_dot)).astype(jnp.bfloat16)
        grad_query = (
            jnp.einsum("hqk,khd->qhd", grad_scores, key_block, preferred_element_type=jnp.float32)
            * score_scale
        )
        grad_key = (
            jnp.einsum("hqk,qhd->khd", grad_scores, query_block, preferred_element_type=jnp.float32)
            * score_scale
        )
        update = jnp.concatenate(
            [grad_key.reshape(key_rows, head_width), grad_value.reshape(key_rows, head_width)],
            axis=1,
        )
        current = lax.dynamic_slice_in_dim(carry, first_row, key_rows, 0)
        carry = lax.dynamic_update_slice_in_dim(carry, current + update, first_row, 0)
        return (carry, grad_query.reshape(block_rows, head_width))

    starts = jnp.arange(row_count // block_rows, dtype=jnp.int32) * block_rows
    initial = jnp.zeros((row_count + 2 * rim_width, 2 * head_width), jnp.float32)
    grad_pad, grad_query = lax.scan(one_step, initial, (starts, log_totals))
    from_above = from_behind(grad_pad[:rim_width], SEQ, -1)
    from_below = from_behind(grad_pad[row_count + rim_width :], SEQ, 1)
    grad_pair = grad_pad[rim_width : row_count + rim_width]
    grad_pair = (
        grad_pair
        + jnp.pad(from_below, ((0, row_count - rim_width), (0, 0)))
        + jnp.pad(from_above, ((row_count - rim_width, 0), (0, 0)))
    )
    return (grad_query.reshape(row_count, head_width), grad_pair)


def layer_forward(inputs, attn, ffn, shared, split, seg_own, seg_pad, dilated, rim_width):
    head_width = attn.shape[2]
    row_count = inputs.shape[0]
    inputs_low = inputs.astype(jnp.bfloat16)
    biases = jnp.stack(
        [
            split[0, :head_width],
            jnp.zeros((head_width,), jnp.float32),
            split[0, head_width : 2 * head_width],
        ]
    )
    projected = (
        jnp.einsum("td,mdc->tmc", inputs_low, attn[:3], preferred_element_type=jnp.float32)
        + biases[None]
    ).astype(jnp.bfloat16)
    query = projected[:, 0].reshape(row_count, -1, DH)
    padded = fetch_rims(jnp.concatenate([projected[:, 1], projected[:, 2]], axis=1), rim_width)
    key_pad = padded[:, :head_width].reshape(-1, head_width // DH, DH)
    value_pad = padded[:, head_width:].reshape(-1, head_width // DH, DH)
    seg_near = lax.slice_in_dim(
        seg_pad, 2 * WIN - rim_width, 2 * WIN + row_count + rim_width, axis=0
    )
    mixed_heads, log_totals = plain_attend(
        query, key_pad, value_pad, seg_own, seg_near, dilated, rim_width
    )
    mixed_heads = mixed_heads.astype(jnp.bfloat16)
    attn_sum = (
        inputs
        + join_heads(
            dot_nt(mixed_heads, attn[3])
        )
        + shared[0]
    )
    normed = normalize_layer(attn_sum, shared[1], shared[2])
    normed_low = normed.astype(jnp.bfloat16)
    pre_gelu = (
        jnp.dot(normed_low, ffn[0], preferred_element_type=jnp.float32) + split[0, 2 * head_width :]
    )
    hidden = jax.nn.gelu(pre_gelu, approximate=False).astype(jnp.bfloat16)
    ffn_sum = (
        normed
        + join_heads(dot_nt(hidden, ffn[1]))
        + shared[3]
    )
    result = normalize_layer(ffn_sum, shared[4], shared[5])
    return (
        result,
        (
            inputs_low,
            query,
            padded,
            log_totals,
            mixed_heads,
            attn_sum,
            normed_low,
            pre_gelu,
            hidden,
            ffn_sum,
        ),
    )


def layer_backward(grad_out, saved, attn, ffn, shared, seg_own, seg_pad, dilated, rim_width):
    (
        inputs_low,
        query,
        padded,
        log_totals,
        mixed_heads,
        attn_sum,
        normed_low,
        pre_gelu,
        hidden,
        ffn_sum,
    ) = saved
    head_width = attn.shape[2]
    row_count = inputs_low.shape[0]
    seg_near = lax.slice_in_dim(
        seg_pad, 2 * WIN - rim_width, 2 * WIN + row_count + rim_width, axis=0
    )
    _, pull_out = jax.vjp(normalize_layer, ffn_sum, shared[4], shared[5])
    grad_ffn_sum, grad_gain_two, grad_shift_two = pull_out(grad_out)
    grad_branch = grad_ffn_sum.astype(jnp.bfloat16)
    grad_down = dot_tn(grad_branch, hidden)
    grad_hidden = jnp.dot(grad_branch, ffn[1], preferred_element_type=jnp.float32)
    _, pull_gelu = jax.vjp(lambda value: jax.nn.gelu(value, approximate=False), pre_gelu)
    grad_pre = pull_gelu(grad_hidden)[0].astype(jnp.bfloat16)
    grad_up = dot_tn(normed_low, grad_pre)
    grad_normed = grad_ffn_sum + join_grads(
        dot_nt(grad_pre, ffn[0])
    )
    _, pull_mid = jax.vjp(normalize_layer, attn_sum, shared[1], shared[2])
    grad_attn_sum, grad_gain_one, grad_shift_one = pull_mid(grad_normed)
    grad_attn_out = grad_attn_sum.astype(jnp.bfloat16)
    grad_out_proj = dot_tn(grad_attn_out, mixed_heads)
    grad_mixed = jnp.dot(grad_attn_out, attn[3], preferred_element_type=jnp.float32).astype(
        jnp.bfloat16
    )
    grad_query, grad_pair = plain_attend_back(
        query, padded, log_totals, grad_mixed, seg_own, seg_near, dilated, rim_width
    )
    grad_proj = jnp.stack(
        [grad_query, grad_pair[:, :head_width], grad_pair[:, head_width:]], axis=1
    ).astype(jnp.bfloat16)
    grad_in_proj = jnp.einsum(
        "td,tmc->mdc", inputs_low, grad_proj, preferred_element_type=jnp.float32
    )
    grad_inputs = grad_attn_sum + join_grads(
        jnp.einsum("tmc,mdc->td", grad_proj, attn[:3], preferred_element_type=jnp.float32)
    )
    proj_sums = jnp.sum(grad_proj.astype(jnp.float32), axis=0)
    split_grad = jnp.concatenate(
        [proj_sums[0], proj_sums[2], jnp.sum(grad_pre.astype(jnp.float32), axis=0)]
    )
    shared_grad = jnp.stack(
        [
            jnp.sum(grad_attn_sum, axis=0),
            grad_gain_one,
            grad_shift_one,
            jnp.sum(grad_ffn_sum, axis=0),
            grad_gain_two,
            grad_shift_two,
        ]
    )
    attn_grad = jnp.concatenate([grad_in_proj, grad_out_proj[None]], axis=0)
    ffn_grad = jnp.stack([grad_up, grad_down])
    return (grad_inputs, attn_grad, ffn_grad, shared_grad, split_grad)


def from_slots(gathered, owners, slot_count):
    layer_count, matrix_count, row_count, col_count = gathered.shape
    blocks = gathered.reshape(
        layer_count, matrix_count, slot_count, row_count // slot_count, col_count
    )
    return jnp.take(blocks, owners, axis=2).reshape(gathered.shape)


def to_slots(grads, inverse, slot_count):
    matrix_count, row_count, col_count = grads.shape
    blocks = grads.reshape(matrix_count, slot_count, row_count // slot_count, col_count)
    return jnp.take(blocks, inverse, axis=1).reshape(grads.shape)


def rotate_update(weight, grad_now, first, second, running_average, basis, rates):
    turn = basis[:, :, 0, 0]
    turned = jnp.einsum("lmre,lmec->lmrc", grad_now, turn, precision=HIGHEST_PRECISION)
    first_new = BETA_FIRST * first + (1.0 - BETA_FIRST) * turned
    second_new = BETA_SECOND * second + (1.0 - BETA_SECOND) * turned * turned
    direction = (
        first_new
        / (1.0 - BETA_FIRST**STEP)
        / (jnp.sqrt(second_new / (1.0 - BETA_SECOND**STEP)) + ADAM_EPSILON)
    )
    back = jnp.einsum("lmrc,lmec->lmre", direction, turn, precision=HIGHEST_PRECISION)
    weight_new = weight - rates[None, :, None, None] * (back + DECAY_RATE * weight)
    average_new = AVERAGE_RATE * running_average + (1.0 - AVERAGE_RATE) * weight_new
    return (weight_new, first_new, second_new, average_new)


def vector_update(current, grad_now, first, second):
    first_new = BETA_FIRST * first + (1.0 - BETA_FIRST) * grad_now
    second_new = BETA_SECOND * second + (1.0 - BETA_SECOND) * grad_now * grad_now
    direction = (
        first_new
        / (1.0 - BETA_FIRST**STEP)
        / (jnp.sqrt(second_new / (1.0 - BETA_SECOND**STEP)) + ADAM_EPSILON)
    )
    return (current - VECTOR_RATE * direction, first_new, second_new)


def with_collectives(
    activations,
    cotangent,
    segments,
    dilated_heads,
    owners,
    attn_weights,
    attn_first,
    attn_second,
    attn_average,
    attn_basis,
    ffn_weights,
    ffn_first,
    ffn_second,
    ffn_average,
    ffn_basis,
    split_biases,
    split_first,
    split_second,
    shared_vectors,
    shared_first,
    shared_second,
):
    slot_count = lax.axis_size(SEQ)
    layer_count = attn_weights.shape[0]
    attn_full, ffn_full = (
        lax.all_gather(attn_weights.astype(jnp.bfloat16), SEQ, axis=2, tiled=True),
        lax.all_gather(ffn_weights.astype(jnp.bfloat16), SEQ, axis=2, tiled=True),
    )
    attn_full = from_slots(attn_full, owners, slot_count)
    ffn_full = from_slots(ffn_full, owners, slot_count)
    seg_pad = with_halo(segments, ((SEQ, 0),), 2 * WIN)
    head_width = attn_full.shape[3]
    head_count = head_width // DH
    heads_here = lax.axis_index(MP) * head_count + jnp.arange(head_count, dtype=jnp.int32)
    head_flags = jnp.any(heads_here[:, None] == dilated_heads[None, :], axis=1)
    current = activations.astype(jnp.float32)
    saved_list = []
    for layer_index in range(layer_count):
        dilated = jnp.logical_and(head_flags, layer_index % 2 == 1)
        rim_width = 2 * WIN if layer_index % 2 == 1 else WIN
        current, saved = layer_forward(
            current,
            attn_full[layer_index],
            ffn_full[layer_index],
            shared_vectors[layer_index],
            split_biases[layer_index],
            segments,
            seg_pad,
            dilated,
            rim_width,
        )
        saved_list.append(saved)
    slot_range = jnp.arange(slot_count, dtype=jnp.int32)
    inverse = jnp.sum(
        jnp.where(owners[None, :] == slot_range[:, None], slot_range[None, :], 0), axis=1
    )
    grad_now = cotangent.astype(jnp.float32)
    attn_list = [None] * layer_count
    ffn_list = [None] * layer_count
    shared_list = [None] * layer_count
    split_list = [None] * layer_count
    for layer_index in range(layer_count - 1, -1, -1):
        dilated = jnp.logical_and(head_flags, layer_index % 2 == 1)
        rim_width = 2 * WIN if layer_index % 2 == 1 else WIN
        grad_now, attn_grad, ffn_grad, shared_grad, split_grad = layer_backward(
            grad_now,
            saved_list[layer_index],
            attn_full[layer_index],
            ffn_full[layer_index],
            shared_vectors[layer_index],
            segments,
            seg_pad,
            dilated,
            rim_width,
        )
        attn_grad = to_slots(attn_grad, inverse, slot_count)
        ffn_grad = to_slots(ffn_grad, inverse, slot_count)
        attn_list[layer_index] = attn_grad
        ffn_list[layer_index] = ffn_grad
        shared_list[layer_index] = shared_grad
        split_list[layer_index] = split_grad[None, :]
    attn_grads = jnp.stack(attn_list)
    ffn_grads = jnp.stack(ffn_list)
    attn_grads, ffn_grads = (
        lax.psum_scatter(attn_grads, SEQ, scatter_dimension=2, tiled=True),
        lax.psum_scatter(ffn_grads, SEQ, scatter_dimension=2, tiled=True),
    )
    shared_grads, split_grads = lax.psum((jnp.stack(shared_list), jnp.stack(split_list)), SEQ)
    first_seq = lax.axis_index(SEQ) == 0
    first_both = jnp.logical_and(first_seq, lax.axis_index(MP) == 0)
    local_sum = jnp.sum(attn_grads * attn_grads) + jnp.sum(ffn_grads * ffn_grads)
    local_sum = (
        local_sum
        + jnp.where(first_seq, jnp.sum(split_grads * split_grads), 0.0)
        + jnp.where(first_both, jnp.sum(shared_grads * shared_grads), 0.0)
    )
    grad_norm = jnp.sqrt(lax.psum(local_sum, (SEQ, MP)))
    factor = CLIP_LEVEL / jnp.maximum(grad_norm, CLIP_LEVEL)
    attn_rates = jnp.array([0.5 * D ** (-0.5)] * 3 + [0.5 * (WIN / D) ** 0.5], jnp.float32)
    ffn_rates = jnp.array([0.5 * D ** (-0.5), 0.5 * FF ** (-0.5)], jnp.float32)
    attn_out = rotate_update(
        attn_weights,
        factor * attn_grads,
        attn_first,
        attn_second,
        attn_average,
        attn_basis,
        attn_rates,
    )
    ffn_out = rotate_update(
        ffn_weights, factor * ffn_grads, ffn_first, ffn_second, ffn_average, ffn_basis, ffn_rates
    )
    split_out = vector_update(split_biases, factor * split_grads, split_first, split_second)
    shared_out = vector_update(shared_vectors, factor * shared_grads, shared_first, shared_second)
    return (
        current,
        grad_now,
        attn_out[0],
        attn_out[1],
        attn_out[2][:, :3],
        attn_out[2][:, 3],
        attn_out[3],
        ffn_out[0],
        ffn_out[1],
        ffn_out[2],
        ffn_out[3],
        split_out[0],
        split_out[1],
        split_out[2],
        shared_out[0],
        shared_out[1],
        shared_out[2],
        grad_norm,
    )


def solution(mesh):
    placed = (
        P(SEQ, None),
        P(SEQ, None),
        P(SEQ),
        P(),
        P(),
        P(None, None, SEQ, MP),
        P(None, None, SEQ, MP),
        P(None, None, SEQ, MP),
        P(None, None, SEQ, MP),
        P(None, None, SEQ, MP, None, None),
        P(None, None, SEQ, MP),
        P(None, None, SEQ, MP),
        P(None, None, SEQ, MP),
        P(None, None, SEQ, MP),
        P(None, None, SEQ, MP, None, None),
        P(None, MP, None),
        P(None, MP, None),
        P(None, MP, None),
        P(),
        P(),
        P(),
    )
    count = mesh.shape[SEQ]
    fits = count % 4 == 0 and (D // count) % 16 == 0 and mesh.shape[MP] == 4
    return jax.shard_map(
        direct if fits else with_collectives,
        mesh=mesh,
        in_specs=placed,
        out_specs=(
            P(SEQ, None),
            P(SEQ, None),
            P(None, None, SEQ, MP),
            P(None, None, SEQ, MP),
            P(None, None, SEQ, MP),
            P(None, SEQ, MP),
            P(None, None, SEQ, MP),
            P(None, None, SEQ, MP),
            P(None, None, SEQ, MP),
            P(None, None, SEQ, MP),
            P(None, None, SEQ, MP),
            P(None, MP, None),
            P(None, MP, None),
            P(None, MP, None),
            P(),
            P(),
            P(),
            P(),
        ),
        check_vma=False,
    )
```

time: 1490 us -> 388 us (0.26)
  waiting for transfers between devices: 770 us -> 0 us
  Pallas kernels: 0 us -> 377 us
  local copies, waits for them, and re-layouts: 217 us -> 4.69 us
  matrix products: 189 us -> 0 us
  other arithmetic: 152 us -> 0 us
  blocking collectives: 78.1 us -> 0 us
  starting transfers between devices: 28.2 us -> 0 us
  loops' own time: 26.1 us -> 0 us
  between operations: 21 us -> 1.24 us
    psum x8 -> x0, waiting for transfers between devices: 409 us -> none  [the longest x4 248 us: join_grads(): return lax.psum(term, 'mp')]
    pallas_call x0 -> x9, Pallas kernels: none -> 377 us  [run_kernel(): pl.pallas_call(kernel, out_shape=shapes, in_specs=[spec_of(key) for key i...]
    dot_general x55 -> x0, matrix products: 188 us -> none  [the longest x8 27.7 us: masked_scores(): jnp.einsum('qhd,khd->hqk', query_block, key_block, preferred_element_type...]
    reduce_scatter x1 -> x0, waiting for transfers between devices: 164 us -> none  [local(): lax.psum_scatter(ffn_grads, 'seq', scatter_dimension=2, tiled=True)]
    all_gather x2 -> x0, waiting for transfers between devices: 132 us -> none  [the longest x1 79.7 us: local(): lax.all_gather(ffn_weights.astype(jnp.bfloat16), 'seq', axis=2, tiled=True)]
    psum x2 -> x0, blocking collectives: 78.1 us -> none  [the longest x1 39.4 us: local(): grad_norm = jnp.sqrt(lax.psum(local_sum, ('seq', 'mp')))]
    reduce_sum x28 -> x0, other arithmetic: 60.1 us -> none  [the longest x8 19.7 us: normalize_layer(): center = values - jnp.mean(values, axis=-1, keepdims=True)]
    ppermute x10 -> x0, waiting for transfers between devices: 59.6 us -> none  [the longest x4 41.3 us: from_behind(): return lax.ppermute(block, axis, route)]
  transfers between devices with their start and end apart: 22 -> 0, of which waited for: 16 -> 0; matrix products, arithmetic and copies ran while one was open for 7% -> 0% of each run, Pallas kernels for 0% -> 0%
where the time goes in v2:
time: 388 us; the launch traced here: 383 us
  Pallas kernels  377 us (97%)
  local copies, waits for them, and re-layouts  4.69 us (1%)
    pallas_call x9, Pallas kernels, run_kernel(): pl.pallas_call(kernel, out_shape=shapes, in_specs=[spec_of(key) for key i...  377 us

profile of v2, /device:TPU:0, one launch (start us, length us, event | category | flops | bytes accessed | tf_op | source)
XLA Modules:
  0.0 382.5 jit_solution(3529945615546559481)
XLA Ops:
  0.7 58.7 %opening.1 = (bf16[8,96,768]{2,1,0:T(8,128)(2,1)}, bf16[8,96,768]{2,1,0:T(8,128)(2,1)}, bf16[8,96,768]{2,1,0:T(8,128)(2,1)}, bf16[1024,768]{1,0:T(8,128)(2,1)}, ...) custom-call(bf16[1024,768]{1,0:T(8,128)(2,1)} %refs_0_.1, ...), custom_call_target="tpu_custom_call" | custom-call | flops 2113929216 | bytes 16491552 | tf_op jit(solution)/shard_map/opening/pallas_call | solution.py:115
  59.3 60.2 %middle_forward.1 = (f32[512,128]{1,0:T(8,128)}, f32[512,128]{1,0:T(8,128)}, bf16[1024,192]{1,0:T(8,128)(2,1)}, bf16[1024,384]{1,0:T(8,128)(2,1)}, bf16[8,96,768...) custom-call(bf16[1024,192]{1,0:T(8,128)(2,1)} %get-tuple-element.99., ...), custom_call_target="tpu_custom_call" | custom-call | flops 3623878656 | bytes 24372224 | tf_op jit(solution)/shard_map/middle_forward/pallas_call | solution.py:115
  119.5 13.0 %attend.1 = (bf16[1024,192]{1,0:T(8,128)(2,1)}, bf16[1024,192]{1,0:T(8,128)(2,1)}, bf16[1024,192]{1,0:T(8,128)(2,1)}, bf16[2048,192]{1,0:T(8,128)(2,1)}, bf16[20...) custom-call(bf16[1024,192]{1,0:T(8,128)(2,1)} %get-tuple-element.105.refs_0_, ...), custom_call_target="tpu_custom_call" | custom-call | flops 2415919104 | bytes 9510920 | tf_op jit(solution)/shard_map/attend/pallas_call | solution.py:115
  132.6 65.1 %turning.1 = (f32[1024,768]{1,0:T(8,128)}, bf16[768,768]{1,0:T(8,128)(2,1)}, bf16[768,768]{1,0:T(8,128)(2,1)}, bf16[768,192]{1,0:T(8,128)(2,1)}, f32[512,768]{1,...) custom-call(bf16[1024,192]{1,0:T(8,128)(2,1)} %get-tuple-element.111.refs_0_, ...), custom_call_target="tpu_custom_call" | custom-call | flops 8153726976 | bytes 16131072 | tf_op jit(solution)/shard_map/turning/pallas_call | solution.py:115
  197.7 20.1 %attend_back.2 = (bf16[1024,192]{1,0:T(8,128)(2,1)}, bf16[1024,384]{1,0:T(8,128)(2,1)}, bf16[512,384]{1,0:T(8,128)(2,1)}) custom-call(bf16[1024,192]{1,0:T(8,128)(2,1)} %get-tuple-element.118.refs_0_, bf16[1024,192]{1,0:T(8,128)(2,1)} %get-tuple-element.119.refs_1_, bf16[1024,192]{1,0:T(8,128)(2,1)} %get-tuple-element.120.refs_2_, ...), custom_call_target="tpu_custom_call" | custom-call | flops 4831838208 | bytes 9043976 | tf_op jit(solution)/shard_map/attend_back/pallas_call | solution.py:115
  217.8 62.4 %middle_backward.1 = (bf16[768,768]{1,0:T(8,128)(2,1)}, bf16[768,768]{1,0:T(8,128)(2,1)}, bf16[768,192]{1,0:T(8,128)(2,1)}, f32[512,768]{1,0:T(8,128)}, bf16[102...) custom-call(bf16[1024,192]{1,0:T(8,128)(2,1)} %get-tuple-element.124, ...), custom_call_target="tpu_custom_call" | custom-call | flops 7247757312 | bytes 26494976 | tf_op jit(solution)/shard_map/middle_backward/pallas_call | solution.py:115
  280.2 14.0 %attend_back.3 = (bf16[1024,192]{1,0:T(8,128)(2,1)}, bf16[1024,384]{1,0:T(8,128)(2,1)}, bf16[256,384]{1,0:T(8,128)(2,1)}) custom-call(bf16[1024,192]{1,0:T(8,128)(2,1)} %get-tuple-element.139.refs_0_, bf16[1024,192]{1,0:T(8,128)(2,1)} %get-tuple-element.99.refs_0_.refs_20_.refs_1_, bf16[1024,192]{1,0:T(8,128)(2,1)} %get-tuple-element.140.refs_2_, ...), custom_call_target="tpu_custom_call" | custom-call | flops 4831838208 | bytes 8454152 | tf_op jit(solution)/shard_map/attend_back/pallas_call | solution.py:115
  294.2 68.4 %ending.1 = (f32[1024,768]{1,0:T(8,128)}, f32[4,96,768]{2,1,0:T(8,128)}, f32[2,96,768]{2,1,0:T(8,128)}, f32[16,768]{1,0:T(8,128)}, f32[8,128]{1,0:T(8,128)}) custom-call(bf16[1024,192]{1,0:T(8,128)(2,1)} %get-tuple-element.144.refs_0_, bf16[1024,384]{1,0:T(8,128)(2,1)} %get-tuple-element.145.refs_1_, bf16[256,384]{1,0:T(8,128)(2,1)} %get-tuple-element.146.refs_2_, ...), custom_call_target="tpu_custom_call" | custom-call | flops 1811939328 | bytes 15505408 | tf_op jit(solution)/shard_map/ending/pallas_call | solution.py:115
  362.6 0.0 copy-start
  362.6 14.7 %update.1 = (f32[2,2,96,768]{3,2,1,0:T(8,128)}, f32[2,4,96,192]{3,2,1,0:T(8,128)}, f32[2,2,96,768]{3,2,1,0:T(8,128)}, f32[2,4,96,192]{3,2,1,0:T(8,128)}, f32[2,2...) custom-call(f32[4,96,768]{2,1,0:T(8,128)} %get-tuple-element.160.ref, ...), custom_call_target="tpu_custom_call" | custom-call | flops 905969664 | bytes 28051460 | tf_op jit(solution)/shard_map/update/pallas_call | solution.py:115
  377.3 0.0 copy-done
  377.3 0.0 copy-start.1
  377.4 1.7 copy.41
  379.0 1.3 copy-done.1
  380.4 1.7 copy.42
Async XLA Ops:
  362.6 14.7 %copy-start = (f32[1024,768]{1,0:T(8,128)S(1)}, f32[1024,768]{1,0:T(8,128)}, u32[]{:S(2)}) copy-start(f32[1024,768]{1,0:T(8,128)} %get-tuple-element.198) | copy-start | bytes 9437188
  377.3 3.0 copy-start.1

commit v3 on v2

--- a/solution.py
+++ b/solution.py
@@ -30,7 +30,7 @@
 MESH = pl.DeviceIdType.MESH
 BLOCK = 256
 CHUNK = 128
-HALF = 64
+WIDE_CHUNK = 256
 VMEM_LIMIT = 56 * 1024 * 1024
 SCORE_SCALE = DH ** (-0.5)
 
@@ -154,28 +154,18 @@
     return marked > 0
 
 
+def sorted_groups(natural, sort):
+    groups = natural.shape[0] // (2 * BLOCK)
+    return [dot(sort, natural[g * 2 * BLOCK : (g + 1) * 2 * BLOCK]).astype(BF) for g in range(groups)]
+
+
 def arrange_rows(natural, sort):
-    groups = natural.shape[0] // (2 * BLOCK)
-    parts = [
-        dot(sort, natural[g * 2 * BLOCK : (g + 1) * 2 * BLOCK]).astype(BF) for g in range(groups)
-    ]
+    return jnp.concatenate(sorted_groups(natural, sort), axis=0)
+
+
+def split_rows(natural, sort):
+    parts = sorted_groups(natural, sort)
     return jnp.concatenate([p[:BLOCK] for p in parts] + [p[BLOCK:] for p in parts], axis=0)
-
-
-def restore_rows(arranged, sort):
-    groups = arranged.shape[0] // (2 * BLOCK)
-    half = groups * BLOCK
-    parts = []
-    for g in range(groups):
-        pair = jnp.concatenate(
-            [
-                arranged[g * BLOCK : (g + 1) * BLOCK],
-                arranged[half + g * BLOCK : half + (g + 1) * BLOCK],
-            ],
-            axis=0,
-        )
-        parts.append(dot_tn(sort, pair))
-    return jnp.concatenate(parts, axis=0)
 
 
 def soft_weights(query_block, key_block, lanes, allowed):
@@ -193,56 +183,108 @@
     return jnp.abs(row - col + BLOCK) <= WIN
 
 
+def key_starts(step, mixed):
+    natural = pl.ds(pl.multiple_of(step * BLOCK, BLOCK), 3 * BLOCK)
+    if not mixed:
+        return natural, natural
+    first = (step % 2) * 4 + step // 2
+    return natural, pl.ds(pl.multiple_of(first * BLOCK, BLOCK), 3 * BLOCK)
+
+
+class HeadExchange:
+    def __init__(self, who, source, gathered, sent, came):
+        self.who, self.source, self.gathered, self.sent, self.came = who, source, gathered, sent, came
+        here = lax.axis_index(MP)
+        self.here = here
+        self.devices = who.sibling, who.across, who.diagonal
+
+    def copy(self, kind, t, slot):
+        who = self.who
+        rows = who.own(t) if kind == 1 else who.other(t)
+        return copy_to(
+            self.source.at[rows, :],
+            self.gathered.at[slot, who.half(t), :],
+            self.sent.at[kind, t],
+            self.came.at[kind, t],
+            self.devices[kind],
+        )
+
+    def give(self, t):
+        self.gathered[self.here, self.who.half(t), :] = self.source[self.who.own(t), :]
+        for kind in range(3):
+            self.copy(kind, t, self.here).start()
+
+    def take(self, t):
+        for kind in range(3):
+            self.copy(kind, t, self.devices[kind][1]).wait_recv()
+
+    def finish(self, t):
+        for kind in range(3):
+            self.copy(kind, t, self.here).wait_send()
+
+
 def attend(query, pair, left, right, seg_query, seg_keys, dilated):
     rows, width = query.shape
     heads = width // DH
     blocks = rows // BLOCK
     keys = 3 * BLOCK
     slots = 2 * blocks
+    chunks = rows // WIDE_CHUNK
 
     def body(r):
         step = pl.program_id(0)
+        who = Partners(size=WIDE_CHUNK)
+        exchange = HeadExchange(who, r.out, r.landed, r.sent, r.came)
 
         @pl.when(step == 0)
         def _():
+            who.call()
             marked = marked_lanes(r.dilated, heads)
             sort = parity_matrix()
             for which, held in ((0, r.keys), (1, r.values)):
                 lanes = slice(which * width, (which + 1) * width)
                 padded = jnp.concatenate([r.left[:, lanes], r.pair[:, lanes], r.right[:, lanes]], axis=0)
-                middle = jnp.concatenate(
-                    [
-                        padded[BLOCK : (blocks + 1) * BLOCK],
-                        padded[(blocks - 1) * BLOCK : (2 * blocks - 1) * BLOCK],
-                    ],
-                    axis=0,
-                )
-                held[...] = jnp.where(marked, arrange_rows(padded, sort), middle)
+                natural = jnp.concatenate([padded[BLOCK : (blocks + 3) * BLOCK], padded[: 2 * BLOCK]], axis=0)
+                held[...] = jnp.where(marked, split_rows(padded, sort), natural)
             scaled = (r.asked[...].astype(F32) * SCORE_SCALE).astype(BF)
             r.query[...] = jnp.where(marked, arrange_rows(scaled, sort), scaled)
 
         window = window_mask()
-        first = step + 2 * (step >= blocks // 2)
+        natural, dilated_near = key_starts(step, True)
         own = pl.ds(pl.multiple_of(step * BLOCK, BLOCK), BLOCK)
-        near = pl.ds(pl.multiple_of(first * BLOCK, BLOCK), keys)
-        key_block = r.keys[near, :]
-        value_block = r.values[near, :]
+        marked = marked_lanes(r.dilated, heads)
+        key_block = jnp.where(marked, r.keys[dilated_near, :], r.keys[natural, :])
+        value_block = jnp.where(marked, r.values[dilated_near, :], r.values[natural, :])
         query_block = r.query[own, :]
         gathered = jnp.zeros((BLOCK, width), F32)
         flags = head_flags(r.dilated, heads)
         for head, lanes in enumerate(head_lanes(heads)):
             mine = jnp.where(flags[head], r.seg_query[own, 1:2], r.seg_query[own, 0:1])
-            theirs = jnp.where(flags[head], r.seg_keys[1:2, near], r.seg_keys[0:1, near])
+            theirs = jnp.where(flags[head], r.seg_keys[1:2, dilated_near], r.seg_keys[0:1, natural])
             soft = soft_weights(query_block, key_block, lanes, jnp.logical_and(window, mine == theirs))
             r.soft[head] = soft
             gathered = jnp.where(lanes, dot(soft, value_block), gathered)
         r.arranged[own, :] = gathered.astype(BF)
 
+        for group in range(blocks // 2):
+
+            @pl.when(step == 2 * group + 1)
+            def _(group=group):
+                part = slice(group * 2 * BLOCK, (group + 1) * 2 * BLOCK)
+                arranged = r.arranged[part, :]
+                restored = dot_tn(parity_matrix(), arranged).astype(BF)
+                r.out[part, :] = jnp.where(marked, restored, arranged)
+                if group == 0:
+                    who.gather()
+                    for t in range(chunks // 2):
+                        exchange.give(t)
+
         @pl.when(step == blocks - 1)
         def _():
-            arranged = r.arranged[...]
-            natural = restore_rows(arranged, parity_matrix()).astype(BF)
-            r.out[...] = jnp.where(marked_lanes(r.dilated, heads), natural, arranged)
+            for t in range(chunks // 2):
+                exchange.take(t)
+                exchange.finish(t)
+            r.first[...] = r.landed[...]
 
     return run_kernel(
         body,
@@ -258,13 +300,19 @@
         ),
         dict(
             out=((rows, width), BF),
+            first=((4, rows // 4, width), BF),
             arranged=((rows, width), BF),
             query=((rows, width), BF),
             keys=((slots * BLOCK, width), BF),
             values=((slots * BLOCK, width), BF),
             soft=((heads, rows, keys), BF),
         ),
-        {},
+        dict(
+            landed=pltpu.VMEM((4, rows // 4, width), BF),
+            sent=pltpu.SemaphoreType.DMA((3, chunks // 2)),
+            came=pltpu.SemaphoreType.DMA((3, chunks // 2)),
+        ),
+        collective=8,
         flops=4 * rows * keys * 256 * heads,
         grid=(blocks,),
         specs=dict(soft=pl.BlockSpec((heads, BLOCK, keys), lambda i: (0, i, 0))),
@@ -278,21 +326,16 @@
     blocks = rows // BLOCK
     keys = 3 * BLOCK
     slots = 2 * blocks if mixed else blocks + 2
-    half = blocks // 2
-
-    def order(i):
-        return (i % 2) * half + i // 2
 
     def body(r):
-        turn = pl.program_id(0)
-        step = order(turn) if mixed else turn
+        step = pl.program_id(0)
         column = Column(count)
         first, last = column.index == 0, column.index == count - 1
         before = (lax.rem(column.index + count - 1, count), column.here)
         after = (lax.rem(column.index + 1, count), column.here)
         copy = copy_to(r.ready_left, r.from_right, r.sent.at[0], r.came.at[0], before)
 
-        @pl.when(turn == 0)
+        @pl.when(step == 0)
         def _():
             barrier = pltpu.get_barrier_semaphore()
 
@@ -307,15 +350,13 @@
             r.grad_keys[...] = jnp.zeros_like(r.grad_keys)
             r.grad_values[...] = jnp.zeros_like(r.grad_values)
 
-            @pl.when(jnp.logical_not(first))
-            def _():
-                pl.semaphore_wait(barrier, 1)
-
-        start = step + 2 * (step >= half) if mixed else step
+        natural, dilated_near = key_starts(step, mixed)
         own = pl.ds(pl.multiple_of(step * BLOCK, BLOCK), BLOCK)
-        near = pl.ds(pl.multiple_of(start * BLOCK, BLOCK), keys)
-        key_block = r.keys[near, :]
-        value_block = r.values[near, :]
+        marked = marked_lanes(r.dilated, heads)
+        key_block, value_block = r.keys[natural, :], r.values[natural, :]
+        if mixed:
+            key_block = jnp.where(marked, r.keys[dilated_near, :], key_block)
+            value_block = jnp.where(marked, r.values[dilated_near, :], value_block)
         query_block = r.query[own, :]
         grad_block = r.grad[own, :]
         product = grad_block.astype(F32) * r.arranged[own, :].astype(F32)
@@ -332,8 +373,13 @@
             grad_key += dot_tn(grad_scores, jnp.where(lanes, query_block, 0.0).astype(BF))
             grad_query = jnp.where(lanes, dot(grad_scores, key_block), grad_query)
         r.grad_query[own, :] = (grad_query * SCORE_SCALE).astype(BF)
-        r.grad_keys[near, :] += grad_key
-        r.grad_values[near, :] += grad_value
+        if mixed:
+            for held, grad in ((r.grad_keys, grad_key), (r.grad_values, grad_value)):
+                held[dilated_near, :] += jnp.where(marked, grad, 0.0)
+                held[natural, :] += jnp.where(marked, 0.0, grad)
+        else:
+            r.grad_keys[natural, :] += grad_key
+            r.grad_values[natural, :] += grad_value
 
         def natural_group(g, middle):
             both = []
@@ -346,13 +392,12 @@
                     ],
                     axis=0,
                 ).astype(BF)
-                marked = marked_lanes(r.dilated, heads)
                 both.append(jnp.where(marked, dot_tn(parity_matrix(), pair), plain).astype(BF))
             return jnp.concatenate(both, axis=1)
 
         edge = jnp.zeros((BLOCK, width), F32)
 
-        @pl.when(turn == (1 if mixed else 0))
+        @pl.when(step == (1 if mixed else 0))
         def _():
             if mixed:
                 r.ready_left[...] = natural_group(0, lambda held: jnp.concatenate([edge, held[:BLOCK, :]], axis=0))
@@ -363,31 +408,22 @@
 
             @pl.when(jnp.logical_not(first))
             def _():
+                pl.semaphore_wait(pltpu.get_barrier_semaphore(), 1)
                 copy.start()
 
-        @pl.when(turn == blocks - 1)
+        @pl.when(step == blocks - 1)
         def _():
             if mixed:
-                arranged = r.grad_query[...]
-                natural = restore_rows(arranged, parity_matrix()).astype(BF)
-                r.out_query[...] = jnp.where(marked_lanes(r.dilated, heads), natural, arranged)
+                for g in range(blocks // 2):
+                    part = slice(g * 2 * BLOCK, (g + 1) * 2 * BLOCK)
+                    arranged = r.grad_query[part, :]
+                    restored = dot_tn(parity_matrix(), arranged).astype(BF)
+                    r.out_query[part, :] = jnp.where(marked, restored, arranged)
                 lap = 2 * BLOCK
-                middle = blocks * BLOCK
-                r.out_own[:lap, :] = natural_group(
-                    1, lambda held: jnp.concatenate([held[BLOCK:lap, :], held[lap : lap + BLOCK, :] + held[middle : middle + BLOCK, :]], axis=0)
-                )
-                r.out_own[lap:, :] = natural_group(
-                    2,
-                    lambda held: jnp.concatenate(
-                        [
-                            held[lap + BLOCK : middle, :] + held[middle + BLOCK : middle + lap, :],
-                            held[middle + lap : middle + lap + BLOCK, :],
-                        ],
-                        axis=0,
-                    ),
-                )
+                r.out_own[:lap, :] = natural_group(1, lambda held: held[BLOCK : 3 * BLOCK, :])
+                r.out_own[lap:, :] = natural_group(2, lambda held: held[3 * BLOCK : 5 * BLOCK, :])
                 r.out_right[...] = natural_group(
-                    3, lambda held: jnp.concatenate([held[middle + lap + BLOCK :, :], edge], axis=0)
+                    3, lambda held: jnp.concatenate([held[5 * BLOCK : 6 * BLOCK, :], edge], axis=0)
                 )
             else:
                 r.out_query[...] = r.grad_query[...]
@@ -405,7 +441,6 @@
             def _():
                 copy.wait_send()
 
-    soft_index = (lambda i: (0, order(i), 0)) if mixed else (lambda i: (0, i, 0))
     return run_kernel(
         body,
         "attend_back",
@@ -436,47 +471,61 @@
         collective=collective,
         flops=8 * rows * keys * 256 * heads,
         grid=(blocks,),
-        specs=dict(soft=pl.BlockSpec((heads, BLOCK, keys), soft_index)),
+        specs=dict(soft=pl.BlockSpec((heads, BLOCK, keys), lambda i: (0, i, 0))),
         in_smem=("dilated",),
     )
 
 
 class Partners:
-    def __init__(self, count=0, shift=0):
+    def __init__(self, count=0, shift=0, size=CHUNK):
         seq = lax.axis_index(SEQ)
         here = lax.axis_index(MP)
         self.core = lax.rem(here, 2)
         self.sibling = (seq, here + 1 - 2 * self.core)
         self.across = (seq, lax.rem(here + 2, 4))
         self.diagonal = (seq, lax.rem(here + 3 - 2 * self.core, 4))
-        self.count, self.shift = count, shift
+        self.count, self.shift, self.size = count, shift, size
+
+    def others(self, column):
+        found = [self.sibling, self.across, self.diagonal]
+        if column is not None:
+            found += [column.peer(k) for k in range(1, column.count)]
+        return found
+
+    def call(self, column=None):
+        barrier = pltpu.get_barrier_semaphore()
+        for other in self.others(column):
+            pl.semaphore_signal(barrier, inc=1, device_id=other, device_id_type=MESH)
+
+    def gather(self, column=None):
+        pl.semaphore_wait(pltpu.get_barrier_semaphore(), len(self.others(column)))
 
     def meet(self, column=None):
-        barrier = pltpu.get_barrier_semaphore()
-        others = [self.sibling, self.across, self.diagonal]
-        if column is not None:
-            others += [column.peer(k) for k in range(1, column.count)]
-        for other in others:
-            pl.semaphore_signal(barrier, inc=1, device_id=other, device_id_type=MESH)
-        pl.semaphore_wait(barrier, len(others))
+        self.call(column)
+        self.gather(column)
 
     def place(self, t):
         return lax.rem(t + self.shift, self.count) if self.shift else t
 
     def chunk(self, t):
-        return pl.ds(pl.multiple_of(self.place(t) * CHUNK, CHUNK), CHUNK)
+        return pl.ds(pl.multiple_of(self.place(t) * self.size, self.size), self.size)
 
     def two_chunks(self, t):
-        return pl.ds(pl.multiple_of(self.place(t - 1) * CHUNK, 2 * CHUNK), 2 * CHUNK)
+        return pl.ds(pl.multiple_of(self.place(t - 1) * self.size, 2 * self.size), 2 * self.size)
+
+    def part(self, t, core):
+        half = self.size // 2
+        return pl.ds(pl.multiple_of(self.place(t) * self.size + core * half, half), half)
 
     def own(self, t):
-        return pl.ds(pl.multiple_of(self.place(t) * CHUNK + self.core * HALF, HALF), HALF)
+        return self.part(t, self.core)
 
     def other(self, t):
-        return pl.ds(pl.multiple_of(self.place(t) * CHUNK + (1 - self.core) * HALF, HALF), HALF)
+        return self.part(t, 1 - self.core)
 
     def half(self, t):
-        return pl.ds(pl.multiple_of(self.place(t) * HALF, HALF), HALF)
+        half = self.size // 2
+        return pl.ds(pl.multiple_of(self.place(t) * half, half), half)
 
 
 def copy_to(source, target, sent, arrived, device):
@@ -1086,11 +1135,6 @@
     return product(high) + product(rest) + product(low)
 
 
-def unturned(value, turn):
-    high, rest = split_two(value)
-    return dot_nt(high, turn) + dot_nt(rest, turn)
-
-
 def wide(column):
     return jnp.broadcast_to(column, (column.shape[0], 128))
 
@@ -1108,13 +1152,10 @@
     return dict(inverse_one=((rows // 2, 128), F32), inverse_two=((rows // 2, 128), F32))
 
 
-def forward_stages(r, who, first, second, spread):
-    def project(t):
-        first.give(t, dot_nt(r.mixed[who.chunk(t), :], r.out_proj[...]))
-
+def forward_stages(r, who, projected, second, spread):
     def middle(t):
         rows = who.own(t) if r.residual.shape[0] == r.mixed.shape[0] else who.half(t)
-        total = r.residual[rows, :].astype(F32) + first.take(t) + r.shared[r.base + 0 : r.base + 1, :]
+        total = r.residual[rows, :].astype(F32) + projected(t) + r.shared[r.base + 0 : r.base + 1, :]
         unit, inverse, normed = norm_forward(total, r.shared[r.base + 1 : r.base + 2, :], r.shared[r.base + 2 : r.base + 3, :])
         r.unit_one[who.half(t), :] = unit
         r.inverse_one[who.half(t), :] = wide(inverse)
@@ -1137,7 +1178,7 @@
         r.inverse_two[who.half(t), :] = wide(inverse)
         return unit, inverse, result
 
-    return project, middle, feed, final
+    return middle, feed, final
 
 
 def backward_stages(r, who, ends, third, mids):
@@ -1155,7 +1196,7 @@
         grad_pre = (dot(grad, r.ffn_down[...]) * r.slope[rows, :].astype(F32)).astype(BF)
         r.units[0:1, :] += column_sum(grad_pre.astype(F32))
         third.give(t, dot_nt(grad_pre, r.ffn_up[...]))
-        r.grad_pre[pl.ds(pl.multiple_of(lax.rem(t, 2) * CHUNK, CHUNK), CHUNK), :] = grad_pre
+        r.grad_pre[pl.ds(pl.multiple_of(lax.rem(t, 2) * who.size, who.size), who.size), :] = grad_pre
 
         @pl.when(lax.rem(t, 2) == 1)
         def _():
@@ -1170,7 +1211,8 @@
         r.vectors[0:1, :] += column_sum(grad_total)
         r.vectors[1:2, :] += column_sum(grad * unit)
         r.vectors[2:3, :] += column_sum(grad)
-        r.grad_one[who.half(t), :] = grad_total
+        if r.grad_one is not None:
+            r.grad_one[who.half(t), :] = grad_total
         mids.give(t, grad_total)
 
     def project_back(t):
@@ -1292,18 +1334,14 @@
         sorted_ids = [
             dot_nt(r.id_row[:, g * lap : (g + 1) * lap].astype(BF), sort) for g in range(2 * blocks // 2)
         ]
-        natural = jnp.concatenate(
-            [padded[:, WIN : rows + WIN], padded[:, rows - WIN : 2 * rows - WIN]], axis=1
-        )
+        natural = jnp.concatenate([padded[:, WIN : rows + 3 * WIN], padded[:, : 2 * WIN]], axis=1)
         arranged = jnp.concatenate(
             [part[0:1, :BLOCK] for part in sorted_ids] + [part[0:1, BLOCK:] for part in sorted_ids], axis=1
         )
         r.seg_keys[0:1, :] = natural
         r.seg_keys[1:2, :] = arranged
         middle = sorted_ids[1:-1]
-        own_arranged = jnp.concatenate(
-            [part[0:1, :BLOCK] for part in middle] + [part[0:1, BLOCK:] for part in middle], axis=1
-        )
+        own_arranged = jnp.concatenate([part[0:1, :] for part in middle], axis=1)
         for which, row in ((0, own_ids), (1, own_arranged)):
             for k in range(rows // 128):
                 square = jnp.broadcast_to(row[:, k * 128 : (k + 1) * 128], (128, 128))
@@ -1468,17 +1506,34 @@
         r.hidden_bias = r.split[0][:, 2 * width :]
         next_bias = projection_bias(r.split[1], width)
 
+        def share(kind, slot):
+            device = who.across if kind == 1 else who.sibling
+            return copy_to(
+                r.next_out.at[slot], r.next_out.at[slot], r.share_sent.at[kind], r.share_came.at[kind], device
+            )
+
+        def hand_on():
+            share(1, who.across[1]).wait_recv()
+            share(2, who.across[1]).start()
+
         def unpack():
             wide_attn.arrive()
-            r.next_proj[...] = r.full_attn[...].reshape(D, 4 * width)[:, : 3 * width]
-
-        ticks = [(3, r.late.residual.wait), (4, r.late.ffn_up.wait), (4, r.late.ffn_down.wait), (chunks, unpack)]
+            packed_attn = r.full_attn[...].reshape(D, 4 * width)
+            r.next_proj[...] = packed_attn[:, : 3 * width]
+            r.next_out[column.here] = packed_attn[:, 3 * width :].astype(F32).T.astype(BF)
+            share(0, column.here).start()
+            share(1, column.here).start()
+
+        ticks = [(3, r.late.residual.wait), (4, r.late.ffn_up.wait), (4, r.late.ffn_down.wait), (chunks, unpack), (chunks + 6, hand_on)]
         ticks += [(when, lambda k=k: wide_attn.relay(k + 1)) for k, when in enumerate(GATHER_TIMES[0])]
         ticks += [(GATHER_TIMES[1][0], wide_up.start_line), (GATHER_TIMES[1][1], wide_up.start_pair)]
         ticks += [(when, lambda k=k: wide_up.relay(k + 1)) for k, when in enumerate(GATHER_TIMES[2])]
         ticks += [(GATHER_TIMES[3][0], wide_down.begin)]
         ticks += [(when, lambda k=k: wide_down.relay(k + 1)) for k, when in enumerate(GATHER_TIMES[3][1:])]
-        project, middle, feed, final = forward_stages(r, who, first, second, spread)
+        middle, feed, final = forward_stages(r, who, first.take, second, spread)
+
+        def project(t):
+            first.give(t, dot_nt(r.mixed[who.chunk(t), :], r.out_proj[...]))
 
         def middle_out(t):
             middle(t)
@@ -1491,9 +1546,7 @@
 
         def close(t):
             _, _, result = final(t)
-            r.result[who.half(t), :] = result
-            for flush in (r.flush.unit_two, r.flush.result):
-                flush.copy(who.half(t), t).start()
+            r.flush.unit_two.copy(who.half(t), t).start()
             last.give(t, result)
 
         def next_project(t):
@@ -1518,6 +1571,10 @@
         )
         finish_all(chunks, (first, second, spread, last))
         halo.arrive()
+        share(0, who.sibling[1]).wait_recv()
+        share(2, who.diagonal[1]).wait_recv()
+        for kind, slot in enumerate((column.here, column.here, who.across[1])):
+            share(kind, slot).wait_send()
         wide_up.arrive()
         halo.finish()
         for engine in (wide_attn, wide_up, wide_down):
@@ -1526,7 +1583,7 @@
         def written(t, carry):
             for flush in (r.flush.hidden, r.flush.slope, r.flush.spread_full, r.flush.last_full):
                 flush.copy(who.chunk(t), t).wait()
-            for flush in (r.flush.unit_one, r.flush.unit_two, r.flush.result):
+            for flush in (r.flush.unit_one, r.flush.unit_two):
                 flush.copy(who.half(t), t).wait()
             return carry
 
@@ -1537,17 +1594,20 @@
         query=((rows, width), BF),
         pair=((rows, 2 * width), BF),
         full_attn=((count, block, 4 * width), BF),
+        next_out=((4, width, D), BF),
         full_up=((count, block, units), BF),
         full_down=((count, block, units), BF),
         left=((2 * WIN, 2 * width), BF),
         right=((2 * WIN, 2 * width), BF),
     )
     flushed = forward_refs(rows, width, units)
-    flushed.update(spread_full=((rows, D), BF), last_full=((rows, D), BF), result=((rows // 2, D), F32))
+    flushed.update(spread_full=((rows, D), BF), last_full=((rows, D), BF))
     scratch = dict(
         normed=pltpu.VMEM((rows // 2, D), F32),
         out_proj=pltpu.VMEM((D, width), BF),
         next_proj=pltpu.VMEM((D, 3 * width), BF),
+        share_sent=pltpu.SemaphoreType.DMA((3,)),
+        share_came=pltpu.SemaphoreType.DMA((3,)),
     )
     scratch.update(prefixed("first", exchange_scratch(rows)))
     scratch.update(prefixed("second", exchange_scratch(rows)))
@@ -1578,48 +1638,59 @@
     )
 
 
-def turning(mixed, attn, ffn_up, ffn_down, residual, shared, split_biases, cotangent, turn):
+def turning(mixed, first_mixed, out_proj, attn, ffn_up, ffn_down, residual, shared, split_biases, cotangent, turn):
     rows, width = mixed.shape
     units = ffn_up.shape[1]
-    chunks = rows // CHUNK
+    chunks = rows // WIDE_CHUNK
 
     def body(r):
-        who = Partners()
-        r.base = 6
-        first, second = Exchange(who, pick(r, "first")), Exchange(who, pick(r, "second"))
-        third = Exchange(who, pick(r, "third"))
+        who = Partners(size=WIDE_CHUNK)
+        r.base, r.grad_one = 6, None
+        second, third = Exchange(who, pick(r, "second")), Exchange(who, pick(r, "third"))
+        heads = HeadExchange(who, r.mixed, r.gathered, r.heads_sent, r.heads_came)
         spread = Gather(who, pick(r, "spread"))
-        ends, mids = Gather(who, pick(r, "ends")), Gather(who, pick(r, "mids"))
+        ends = Gather(who, pick(r, "ends"))
+        mids = Gather(who, SimpleNamespace(full=r.grad_low, sent=r.mids_sent, came=r.mids_came))
         out = Gather(who, SimpleNamespace(full=r.output, sent=r.out_sent, came=r.out_came))
         who.meet()
+        for t in range(chunks // 2, chunks):
+            heads.give(t)
+        r.gathered[:, : rows // 4, :] = r.first_mixed[...]
         r.out_proj[...] = r.attn[:, 3 * width :]
         r.hidden_bias = r.split[1][:, 2 * width :]
         clear(r.vectors, r.units, r.sum_up, r.sum_down, r.sum_out)
-        project, middle, feed, final = forward_stages(r, who, first, second, spread)
+
+        def projected(t):
+            @pl.when(t >= chunks // 2)
+            def _():
+                heads.take(t)
+
+            mine = jnp.concatenate([r.gathered[k, who.half(t), :] for k in range(4)], axis=1)
+            return dot(mine, r.full_out[...].reshape(D, D))
+
+        middle, feed, final = forward_stages(r, who, projected, second, spread)
         enter, feed_back, leave, project_back = backward_stages(r, who, ends, third, mids)
 
-        ticks = [(3, r.late.residual.wait), (4, r.late.ffn_up.wait), (4, r.late.ffn_down.wait)]
-        ticks += [(7, r.late.cotangent.wait), (7, r.late.turn.wait)]
+        ticks = [(0, r.late.residual.wait), (1, r.late.ffn_up.wait), (1, r.late.ffn_down.wait)]
+        ticks += [(4, r.late.cotangent.wait), (4, r.late.turn.wait)]
 
         def close(t):
             unit, inverse, result = final(t)
             grad = dot(r.cotangent[who.own(t), :], r.turn[...])
             enter(t, grad, unit, inverse)
-            out.give(t, unturned(result, r.turn[...]))
+            out.give(t, result)
 
         run_stages(
             chunks,
             [
-                (9, third.add),
-                (5, second.add),
-                (1, first.add),
-                (11, leave),
-                (7, close),
-                (3, middle),
-                (12, project_back),
-                (8, feed_back),
-                (4, feed),
-                (0, project),
+                (6, third.add),
+                (2, second.add),
+                (8, leave),
+                (4, close),
+                (0, middle),
+                (9, project_back),
+                (5, feed_back),
+                (1, feed),
             ],
             ticks,
         )
@@ -1629,17 +1700,19 @@
             return carry
 
         lax.fori_loop(0, chunks, arrive, 0)
-        finish_all(chunks, (first, second, third, spread, ends, mids, out))
+        finish_all(chunks, (second, third, spread, ends, mids, out))
+        for t in range(chunks // 2, chunks):
+            heads.finish(t)
         r.up[...] = r.sum_up[...].astype(BF)
         r.down[...] = r.sum_down[...].astype(BF)
         r.proj[...] = r.sum_out[...].astype(BF)
 
     outputs = dict(
-        output=((rows, D), F32),
+        output=((rows, D), BF),
         up=((D, units), BF),
         down=((D, units), BF),
         proj=((D, width), BF),
-        grad_one=((rows // 2, D), F32),
+        grad_low=((rows, D), BF),
         grad_mixed=((rows, width), BF),
         vectors=((8, D), F32),
         units=((8, units), F32),
@@ -1647,25 +1720,32 @@
     scratch = dict(
         normed=pltpu.VMEM((rows // 2, D), F32),
         kept=pltpu.VMEM((rows // 2, D), F32),
-        grad_pre=pltpu.VMEM((2 * CHUNK, units), BF),
+        grad_pre=pltpu.VMEM((2 * WIDE_CHUNK, units), BF),
         out_proj=pltpu.VMEM((D, width), BF),
+        gathered=pltpu.VMEM((4, rows // 2, width), BF),
+        heads_sent=pltpu.SemaphoreType.DMA((3, chunks)),
+        heads_came=pltpu.SemaphoreType.DMA((3, chunks)),
         sum_up=pltpu.VMEM((D, units), F32),
         sum_down=pltpu.VMEM((D, units), F32),
         sum_out=pltpu.VMEM((D, width), F32),
+        mids_sent=pltpu.SemaphoreType.DMA((chunks,)),
+        mids_came=pltpu.SemaphoreType.DMA((chunks,)),
         out_sent=pltpu.SemaphoreType.DMA((chunks,)),
         out_came=pltpu.SemaphoreType.DMA((chunks,)),
     )
     for key, (shape, dtype) in {**forward_refs(rows, width, units), **forward_small(rows)}.items():
         scratch[key] = pltpu.VMEM(shape, dtype)
-    for key in ("first", "second", "third"):
+    for key in ("second", "third"):
         scratch.update(prefixed(key, exchange_scratch(rows)))
-    for key in ("spread", "ends", "mids"):
+    for key in ("spread", "ends"):
         scratch.update(prefixed(key, gather_scratch(rows)))
     return run_kernel(
         body,
         "turning",
         dict(
             mixed=mixed,
+            first_mixed=first_mixed,
+            full_out=out_proj,
             attn=attn,
             shared=shared,
             split=split_biases,
@@ -1788,7 +1868,7 @@
 
         def start(t):
             half = who.half(t)
-            enter(t, r.grad_above[half, :] + zeroth.take(t), r.unit_two[half, :], r.inverse_two[half, 0:1])
+            enter(t, r.grad_above[who.own(t), :].astype(F32) + zeroth.take(t), r.unit_two[half, :], r.inverse_two[half, 0:1])
 
         run_stages(
             chunks,
@@ -1987,7 +2067,7 @@
     return jnp.sum(value * value)
 
 
-def ending(back, next_attn, grad_above, low, turn, above, top, count):
+def ending(back, next_attn, grad_above, low, above, top, count):
     rows, width = back.out_query.shape
     chunks = rows // CHUNK
     lines, block = count // 2, D // count
@@ -2022,13 +2102,13 @@
             small.core_copy().start()
 
         ticks = [tick for engine, times in zip((up, down, three), END_TIMES) for tick in engine.ticks(times)]
-        ticks += [(chunks // 2 + 2, start_three), (3, r.late.grad_above.wait), (3, r.late.turn.wait)]
+        ticks += [(chunks // 2 + 2, start_three), (3, r.late.grad_above.wait)]
         ticks += [(chunks // 2 + 4, lambda: small.second(12)), (chunks // 2 + 6, small.third)]
         ticks = back_ticks + ticks
         clear(r.biases, r.sum_three)
 
         def close(t):
-            out.give(t, unturned(r.grad_above[who.half(t), :] + zeroth.take(t), r.turn[...]))
+            out.give(t, r.grad_above[who.half(t), :] + zeroth.take(t))
 
         run_stages(chunks, [(1, zeroth.add), (3, close)], ticks)
         vectors = small.result()
@@ -2058,7 +2138,7 @@
             engine.finish()
 
     outputs = dict(
-        output=((rows, D), F32),
+        output=((rows, D), BF),
         ffn_grads=((4, block, units), F32),
         attn_grads=((2, block, 4 * width), F32),
         vectors=((16, D), F32),
@@ -2100,7 +2180,7 @@
         collective=4,
         flops=2 * rows * D * 6 * width,
         in_hbm=("above_up", "above_down"),
-        late=dict(grad_above=grad_above, turn=turn),
+        late=dict(grad_above=grad_above),
     )
 
 
@@ -2111,7 +2191,7 @@
     return first_new, second_new, first_new / (1.0 - BETA_FIRST**STEP) / size
 
 
-def update(end, turn, attn, ffn, split, shared):
+def update(result, end, turn, attn, ffn, split, shared):
     block, units = ffn[0].shape[2:]
     width = attn[0].shape[3]
     rates = [0.5 * D ** (-0.5)] * 3 + [0.5 * (WIN / D) ** 0.5]
@@ -2128,6 +2208,8 @@
     def body(r):
         step = pl.program_id(0)
         factor = CLIP_LEVEL / jnp.maximum(r.norm[0:1, 0:1], CLIP_LEVEL)
+        r.result_real[...] = dot_nt(r.result[...], r.turn[...])
+        r.grad_real[...] = dot_nt(r.grad[...], r.turn[...])
         rate = jnp.where(step % 2 == 0, 0.5 * D ** (-0.5), 0.5 * FF ** (-0.5))
         results = matrix(
             factor * r.ffn_grads[...],
@@ -2187,7 +2269,11 @@
     inputs = dict(
         ffn_grads=end.ffn_grads, attn_grads=end.attn_grads, vectors=end.vectors, norm=end.norm, turn=turn
     )
-    outputs, specs = {}, {}
+    rows = result.shape[0]
+    inputs.update(result=result, grad=end.output)
+    outputs = dict(result_real=((rows, D), F32), grad_real=((rows, D), F32))
+    row_spec = pl.BlockSpec((rows // 4, D), lambda i: (i, 0))
+    specs = dict(result=row_spec, grad=row_spec, result_real=row_spec, grad_real=row_spec)
     specs["ffn_grads"] = pl.BlockSpec((None, block, units), lambda i: (i, 0, 0))
     matrix_spec = pl.BlockSpec((None, None, block, units), lambda i: (i // 2, i % 2, 0, 0))
     for key, array in zip(names, ffn):
@@ -2268,13 +2354,13 @@
     attn_one, up_one, down_one = (full.reshape(D, -1) for full in (mid.full_attn, mid.full_up, mid.full_down))
     far = attend(mid.query, mid.pair, mid.left, mid.right, near.seg_query, near.seg_keys, dilated_heads)
     top = turning(
-        far.out, attn_one, up_one, down_one, mid.result, near.shared, split_biases, cotangent, near.turn
+        far.out, far.first, mid.next_out, attn_one, up_one, down_one, mid.last_full, near.shared, split_biases, cotangent, near.turn
     )
     far_back = attend_back(far, top.grad_mixed, dilated_heads, 2 * WIN, True, count, 6)
     low = middle_backward(
         far_back,
         attn_one,
-        top.grad_one,
+        top.grad_low,
         mid.last_full,
         mid,
         near.out,
@@ -2286,8 +2372,9 @@
         count,
     )
     near_back = attend_back(near, low.grad_mixed, dilated_heads, WIN, False, count, 7)
-    end = ending(near_back, attn_zero, low.grad_one, near.low, near.turn, low, top, count)
+    end = ending(near_back, attn_zero, low.grad_one, near.low, low, top, count)
     new = update(
+        top.output,
         end,
         near.turn,
         (attn_weights, attn_first, attn_second, attn_average, attn_basis),
@@ -2296,8 +2383,8 @@
         tuple(array.transpose(1, 0, 2) for array in (shared_vectors, shared_first, shared_second)),
     )
     return (
-        top.output,
-        end.output,
+        new.result_real,
+        new.grad_real,
         new.attn_weights_new,
         new.attn_first_new,
         new.attn_second_new,

time: 388 us -> 379 us (0.977)
  local copies, waits for them, and re-layouts: 4.69 us -> 0 us
  Pallas kernels: 377 us -> 373 us
    unnamed x6 -> x0, local copies, waits for them, and re-layouts: 4.69 us -> none
where the time goes in v3:
time: 379 us; the launch traced here: 374 us
  Pallas kernels  373 us (98%)
    pallas_call x9, Pallas kernels, run_kernel(): pl.pallas_call(kernel, out_shape=shapes, in_specs=[spec_of(key) for key i...  373 us

profile of v3, /device:TPU:0, one launch (start us, length us, event | category | flops | bytes accessed | tf_op | source)
XLA Modules:
  0.0 374.4 jit_solution(8398018501030554422)
XLA Ops:
  0.7 58.7 %opening.1 = (bf16[8,96,768]{2,1,0:T(8,128)(2,1)}, bf16[8,96,768]{2,1,0:T(8,128)(2,1)}, bf16[8,96,768]{2,1,0:T(8,128)(2,1)}, bf16[1024,768]{1,0:T(8,128)(2,1)}, ...) custom-call(bf16[1024,768]{1,0:T(8,128)(2,1)} %refs_0_.1, ...), custom_call_target="tpu_custom_call" | custom-call | flops 2113929216 | bytes 16491552 | tf_op jit(solution)/shard_map/opening/pallas_call | solution.py:115
  59.3 61.9 %middle_forward.1 = (f32[512,128]{1,0:T(8,128)}, f32[512,128]{1,0:T(8,128)}, bf16[1024,192]{1,0:T(8,128)(2,1)}, bf16[1024,384]{1,0:T(8,128)(2,1)}, bf16[8,96,768...) custom-call(bf16[1024,192]{1,0:T(8,128)(2,1)} %get-tuple-element.102, ...), custom_call_target="tpu_custom_call" | custom-call | flops 3623878656 | bytes 23979008 | tf_op jit(solution)/shard_map/middle_forward/pallas_call | solution.py:115
  121.2 16.2 %attend.1 = (bf16[1024,192]{1,0:T(8,128)(2,1)}, bf16[4,256,192]{2,1,0:T(8,128)(2,1)}, bf16[1024,192]{1,0:T(8,128)(2,1)}, bf16[1024,192]{1,0:T(8,128)(2,1)}, bf16...) custom-call(bf16[1024,192]{1,0:T(8,128)(2,1)} %get-tuple-element.108.refs_0_, ...), custom_call_target="tpu_custom_call" | custom-call | flops 2415919104 | bytes 9904136 | tf_op jit(solution)/shard_map/attend/pallas_call | solution.py:115
  137.5 50.2 %turning.1 = (bf16[1024,768]{1,0:T(8,128)(2,1)}, bf16[768,768]{1,0:T(8,128)(2,1)}, bf16[768,768]{1,0:T(8,128)(2,1)}, bf16[768,192]{1,0:T(8,128)(2,1)}, bf16[1024...) custom-call(bf16[1024,192]{1,0:T(8,128)(2,1)} %get-tuple-element.114.refs_0_, ...), custom_call_target="tpu_custom_call" | custom-call | flops 8153726976 | bytes 16131072 | tf_op jit(solution)/shard_map/turning/pallas_call | solution.py:115
  187.7 20.6 %attend_back.2 = (bf16[1024,192]{1,0:T(8,128)(2,1)}, bf16[1024,384]{1,0:T(8,128)(2,1)}, bf16[512,384]{1,0:T(8,128)(2,1)}) custom-call(bf16[1024,192]{1,0:T(8,128)(2,1)} %get-tuple-element.122.refs_0_, bf16[1024,192]{1,0:T(8,128)(2,1)} %get-tuple-element.123.refs_1_, bf16[1024,192]{1,0:T(8,128)(2,1)} %get-tuple-element.124.refs_2_, ...), custom_call_target="tpu_custom_call" | custom-call | flops 4831838208 | bytes 9043976 | tf_op jit(solution)/shard_map/attend_back/pallas_call | solution.py:115
  208.3 66.5 %middle_backward.1 = (bf16[768,768]{1,0:T(8,128)(2,1)}, bf16[768,768]{1,0:T(8,128)(2,1)}, bf16[768,192]{1,0:T(8,128)(2,1)}, f32[512,768]{1,0:T(8,128)}, bf16[102...) custom-call(bf16[1024,192]{1,0:T(8,128)(2,1)} %get-tuple-element.128, ...), custom_call_target="tpu_custom_call" | custom-call | flops 7247757312 | bytes 26494976 | tf_op jit(solution)/shard_map/middle_backward/pallas_call | solution.py:115
  274.9 14.0 %attend_back.3 = (bf16[1024,192]{1,0:T(8,128)(2,1)}, bf16[1024,384]{1,0:T(8,128)(2,1)}, bf16[256,384]{1,0:T(8,128)(2,1)}) custom-call(bf16[1024,192]{1,0:T(8,128)(2,1)} %get-tuple-element.142.refs_0_, bf16[1024,192]{1,0:T(8,128)(2,1)} %get-tuple-element.102.refs_0_.refs_20_.refs_1_, bf16[1024,192]{1,0:T(8,128)(2,1)} %get-tuple-element.143.refs_2_, ...), custom_call_target="tpu_custom_call" | custom-call | flops 4831838208 | bytes 8454152 | tf_op jit(solution)/shard_map/attend_back/pallas_call | solution.py:115
  288.8 66.8 %ending.1 = (bf16[1024,768]{1,0:T(8,128)(2,1)}, f32[4,96,768]{2,1,0:T(8,128)}, f32[2,96,768]{2,1,0:T(8,128)}, f32[16,768]{1,0:T(8,128)}, f32[8,128]{1,0:T(8,128)}) custom-call(bf16[1024,192]{1,0:T(8,128)(2,1)} %get-tuple-element.147.refs_0_, bf16[1024,384]{1,0:T(8,128)(2,1)} %get-tuple-element.148.refs_1_, bf16[256,384]{1,0:T(8,128)(2,1)} %get-tuple-element.149.refs_2_, ...), custom_call_target="tpu_custom_call" | custom-call | flops 1811939328 | bytes 12752896 | tf_op jit(solution)/shard_map/ending/pallas_call | solution.py:115
  355.6 18.5 %update.1 = (f32[1024,768]{1,0:T(8,128)}, f32[1024,768]{1,0:T(8,128)}, f32[2,2,96,768]{3,2,1,0:T(8,128)}, f32[2,4,96,192]{3,2,1,0:T(8,128)}, f32[2,2,96,768]{3,2...) custom-call(f32[4,96,768]{2,1,0:T(8,128)} %get-tuple-element.162.ref, ...), custom_call_target="tpu_custom_call" | custom-call | flops 905969664 | bytes 37488644 | tf_op jit(solution)/shard_map/update/pallas_call | solution.py:115

commit v4 on v3

--- a/solution.py
+++ b/solution.py
@@ -34,9 +34,10 @@
 VMEM_LIMIT = 56 * 1024 * 1024
 SCORE_SCALE = DH ** (-0.5)
 
-GATHER_TIMES = ((2, 4, 5), (3, 5), (6, 7, 9), (7, 10, 13, 16))
+GATHER_TIMES = ((2, 3, 5), (3, 5), (6, 7, 9), (7, 10, 13, 16))
 BACK_TIMES = ((1, 4, 7, 10, 12), (6, 8, 10, 12), (10, 13, 15, 17))
 END_TIMES = ((1, 4, 7, 10, 13), (5, 8, 10, 12), (11, 14, 15, 16))
+SMALL_TIMES = (8, 10)
 
 
 def dot(left, right):
@@ -73,9 +74,10 @@
     in_hbm=(),
     late=None,
     flushed=None,
+    whole=None,
     pieces=0,
 ):
-    specs, late, flushed = specs or {}, late or {}, flushed or {}
+    specs, late, flushed, whole = specs or {}, late or {}, flushed or {}, whole or {}
 
     def kernel(*refs):
         refs = list(refs)
@@ -85,9 +87,18 @@
             del refs[: len(keys)]
             return dict(zip(keys, got))
 
-        given, distant, made, written, held = (take(keys) for keys in (inputs, late, outputs, flushed, scratch))
+        given, distant, made, written, far, held = (
+            take(keys) for keys in (inputs, late, outputs, flushed, whole, scratch)
+        )
         fetched, fetched_sems, filled, filled_sems = (take(keys) for keys in (late, late, flushed, flushed))
-        r = SimpleNamespace(**given, **made, **held, **fetched, **filled)
+        kept, kept_sems = take(whole), take(whole)
+        r = SimpleNamespace(**given, **made, **held, **fetched, **filled, **kept)
+        if whole:
+            *first, last = whole
+            r.flush_whole = SimpleNamespace(
+                **{key: pltpu.make_async_copy(kept[key], far[key], kept_sems[key].at[0]) for key in first}
+            )
+            r.soft_hbm, r.soft_sem = far[last], kept_sems[last]
         r.late = SimpleNamespace(
             **{key: pltpu.make_async_copy(distant[key], fetched[key], fetched_sems[key]) for key in late}
         )
@@ -99,12 +110,12 @@
     def spec_of(key):
         if key in specs:
             return specs[key]
-        if key in in_hbm or key in late or key in flushed:
+        if key in in_hbm or key in late or key in flushed or key in whole:
             return pl.BlockSpec(memory_space=pl.ANY)
         return pl.BlockSpec(memory_space=pltpu.SMEM if key in in_smem else pltpu.VMEM)
 
     arguments = {**inputs, **late}
-    gives = {**outputs, **flushed}
+    gives = {**outputs, **flushed, **whole}
     shapes = [jax.ShapeDtypeStruct(shape, dtype) for shape, dtype in gives.values()]
     moved = sum(v.size * v.dtype.itemsize for v in arguments.values())
     moved += sum(v.size * v.dtype.itemsize for v in shapes)
@@ -121,7 +132,9 @@
         + [pltpu.VMEM(v.shape, v.dtype) for v in late.values()]
         + [pltpu.SemaphoreType.DMA for _ in late]
         + [pltpu.VMEM(shape, dtype) for shape, dtype in flushed.values()]
-        + [pltpu.SemaphoreType.DMA((pieces,)) for _ in flushed],
+        + [pltpu.SemaphoreType.DMA((pieces,)) for _ in flushed]
+        + [pltpu.VMEM(shape, dtype) for shape, dtype in whole.values()]
+        + [pltpu.SemaphoreType.DMA((pieces,)) for _ in whole],
         compiler_params=pltpu.CompilerParams(**params),
         cost_estimate=pl.CostEstimate(flops=int(flops), bytes_accessed=int(moved), transcendentals=0),
         name=name,
@@ -181,6 +194,35 @@
     row = lax.broadcasted_iota(jnp.int32, (BLOCK, 3 * BLOCK), 0)
     col = lax.broadcasted_iota(jnp.int32, (BLOCK, 3 * BLOCK), 1)
     return jnp.abs(row - col + BLOCK) <= WIN
+
+
+class OutShare:
+    def __init__(self, who, refs):
+        self.who, self.r, self.here = who, refs, lax.axis_index(MP)
+
+    def copy(self, kind, slot):
+        r = self.r
+        device = self.who.across if kind == 1 else self.who.sibling
+        return copy_to(r.full.at[slot], r.full.at[slot], r.sent.at[kind], r.came.at[kind], device)
+
+    def begin(self, own):
+        self.r.full[self.here] = own.astype(F32).T.astype(BF)
+        self.copy(0, self.here).start()
+        self.copy(1, self.here).start()
+
+    def hand_on(self):
+        self.copy(1, self.who.across[1]).wait_recv()
+        self.copy(2, self.who.across[1]).start()
+
+    def finish(self):
+        self.copy(0, self.who.sibling[1]).wait_recv()
+        self.copy(2, self.who.diagonal[1]).wait_recv()
+        for kind, slot in enumerate((self.here, self.here, self.who.across[1])):
+            self.copy(kind, slot).wait_send()
+
+
+def share_scratch():
+    return dict(share_sent=pltpu.SemaphoreType.DMA((3,)), share_came=pltpu.SemaphoreType.DMA((3,)))
 
 
 def key_starts(step, mixed):
@@ -1154,8 +1196,7 @@
 
 def forward_stages(r, who, projected, second, spread):
     def middle(t):
-        rows = who.own(t) if r.residual.shape[0] == r.mixed.shape[0] else who.half(t)
-        total = r.residual[rows, :].astype(F32) + projected(t) + r.shared[r.base + 0 : r.base + 1, :]
+        total = r.residual[who.own(t), :].astype(F32) + projected(t) + r.shared[r.base + 0 : r.base + 1, :]
         unit, inverse, normed = norm_forward(total, r.shared[r.base + 1 : r.base + 2, :], r.shared[r.base + 2 : r.base + 3, :])
         r.unit_one[who.half(t), :] = unit
         r.inverse_one[who.half(t), :] = wide(inverse)
@@ -1270,6 +1311,7 @@
         first, last = column.index == 0, column.index == count - 1
         to_before = copy_to(r.ids, r.ids_right, r.ids_sent.at[0], r.ids_came.at[0], halo.before)
         to_after = copy_to(r.ids, r.ids_left, r.ids_sent.at[1], r.ids_came.at[1], halo.after)
+        r.late.attn.wait()
         wide_attn.put(packed(r.attn.at[0]))
         wide_attn.start_line()
         wide_attn.start_pair()
@@ -1292,6 +1334,7 @@
             to_after.start()
 
         halo.clear()
+        r.late.ffn.wait()
         wide_down.put(r.ffn[0, 1].astype(BF))
         wide_down.start_pair()
         wide_up.put(r.ffn[0, 0].astype(BF))
@@ -1306,7 +1349,10 @@
             r.low[chunk, :] = dot(r.activations[chunk, :], r.turn[...]).astype(BF)
             return carry
 
+        r.flush_whole.turn.start()
+        r.late.activations.wait()
         lax.fori_loop(0, blocks, sort_chunk, 0)
+        r.flush_whole.low.start()
         wide_attn.relay(1)
         padding = jnp.zeros((16 - 6 * layers, D), F32)
         stacked = [r.shared_vectors[k, layer : layer + 1, :] for layer in range(layers) for k in range(6)]
@@ -1352,7 +1398,12 @@
         wide_up.start_pair()
         wide_up.relay(1)
         wide_attn.arrive()
-        r.proj[...] = r.full_attn[...].reshape(D, 4 * width)[:, : 3 * width]
+        r.flush_whole.full_attn.start()
+        whole_attn = r.full_attn[...].reshape(D, 4 * width)
+        r.proj[...] = whole_attn[:, : 3 * width]
+        share = OutShare(who, SimpleNamespace(full=r.full_out, sent=r.share_sent, came=r.share_came))
+        share.begin(whole_attn[:, 3 * width :])
+        exchange = HeadExchange(who, r.out, r.gathered, r.heads_sent, r.heads_came)
         bias = projection_bias(r.split[0], width)
 
         def project(t):
@@ -1381,6 +1432,10 @@
         lax.fori_loop(1, blocks - 1, inner_project, 0)
         for k in range(3, lines):
             wide_up.relay(k)
+
+        def written(step):
+            rows_of = pl.ds(pl.multiple_of(step * BLOCK, BLOCK), BLOCK)
+            return pltpu.make_async_copy(r.soft.at[:, rows_of, :], r.soft_hbm.at[:, rows_of, :], r.soft_sem.at[step])
 
         def attend_block(step):
             own = pl.ds(pl.multiple_of(step * BLOCK, BLOCK), BLOCK)
@@ -1395,6 +1450,9 @@
                 r.soft[head, own, :] = soft
                 gathered = jnp.where(lanes, dot(soft, value_block), gathered)
             r.out[own, :] = gathered.astype(BF)
+            written(step).start()
+            for k in range(BLOCK // CHUNK):
+                exchange.give(BLOCK // CHUNK * step + k)
 
         def inner_attend(i, carry):
             attend_block(i)
@@ -1406,6 +1464,7 @@
 
         lax.fori_loop(1, blocks - 1, inner_attend, 0)
         wide_down.relay(1)
+        share.hand_on()
         halo.arrive()
         for part, start in ((r.left, 0), (r.right, (blocks + 1) * BLOCK)):
             r.keys[pl.ds(start, BLOCK), :] = part[:, :width]
@@ -1414,6 +1473,18 @@
         for k in range(2, lines):
             wide_down.relay(k)
         wide_up.arrive()
+
+        def exchanged(t, carry):
+            exchange.take(t)
+            exchange.finish(t)
+            return carry
+
+        lax.fori_loop(0, rows // CHUNK, exchanged, 0)
+        share.finish()
+        for step in range(blocks):
+            written(step).wait()
+        for copy in vars(r.flush_whole).values():
+            copy.wait()
         halo.finish()
         for engine in (wide_attn, wide_up, wide_down):
             engine.finish()
@@ -1438,6 +1509,11 @@
         ids_came=pltpu.SemaphoreType.DMA((2,)),
         id_row=pltpu.VMEM((8, rows + 4 * WIN), F32),
     )
+    scratch.update(
+        heads_sent=pltpu.SemaphoreType.DMA((3, rows // CHUNK)),
+        heads_came=pltpu.SemaphoreType.DMA((3, rows // CHUNK)),
+        **share_scratch(),
+    )
     scratch.update(prefixed("ga", gather_sems(lines)))
     scratch.update(prefixed("gu", gather_sems(lines)))
     scratch.update(prefixed("gd", gather_sems(lines)))
@@ -1446,38 +1522,41 @@
         body,
         "opening",
         dict(
-            activations=activations,
             segments=segments.reshape(rows // 128, 128),
             owners=owners,
-            attn=attn_weights,
-            ffn=ffn_weights,
             split=split_biases,
             shared_vectors=shared_vectors.transpose(1, 0, 2),
         ),
         dict(
-            full_attn=((count, block, 4 * width), BF),
             full_up=((count, block, units), BF),
             full_down=((count, block, units), BF),
-            low=((rows, D), BF),
-            turn=((D, D), BF),
             shared=((16, D), F32),
             seg_query=((rows, 2), F32),
             seg_keys=((8, 2 * rows), F32),
             out=((rows, width), BF),
+            gathered=((4, rows // 2, width), BF),
+            full_out=((4, width, D), BF),
             query=((rows, width), BF),
             keys=((rows + 2 * BLOCK, width), BF),
             values=((rows + 2 * BLOCK, width), BF),
-            soft=((heads, rows, 3 * BLOCK), BF),
         ),
         scratch,
         collective=5,
         flops=2 * rows * D * (D + 3 * width),
         in_smem=("owners",),
-    )
-
-
-def middle_forward(mixed, attn, ffn_up, ffn_down, residual, shared, split_biases, attn_weights, ffn_weights, count):
-    rows, width = mixed.shape
+        late=dict(attn=attn_weights, ffn=ffn_weights, activations=activations),
+        whole=dict(
+            full_attn=((count, block, 4 * width), BF),
+            low=((rows, D), BF),
+            turn=((D, D), BF),
+            soft=((heads, rows, 3 * BLOCK), BF),
+        ),
+        pieces=blocks,
+    )
+
+
+def middle_forward(gathered, full_out, ffn_up, ffn_down, residual, shared, split_biases, attn_weights, ffn_weights, count):
+    rows, width = 2 * gathered.shape[1], gathered.shape[2]
     units = ffn_up.shape[1]
     chunks = rows // CHUNK
     lines = count // 2
@@ -1486,7 +1565,7 @@
     def body(r):
         who = Partners()
         r.base = 0
-        first, second = Exchange(who, pick(r, "first")), Exchange(who, pick(r, "second"))
+        second = Exchange(who, pick(r, "second"))
         spread = Gather(who, SimpleNamespace(full=r.spread_full, sent=r.spread_sent, came=r.spread_came))
         last = Gather(who, SimpleNamespace(full=r.last_full, sent=r.last_sent, came=r.last_came))
         column = Column(count)
@@ -1494,46 +1573,40 @@
         wide_attn = GatherBlocks(column, SimpleNamespace(full=r.full_attn, **vars(pick(r, "ga"))))
         wide_up = GatherBlocks(column, SimpleNamespace(full=r.full_up, **vars(pick(r, "gu"))))
         wide_down = GatherPairs(column, SimpleNamespace(full=r.full_down, **vars(pick(r, "gd"))))
+        share = OutShare(who, SimpleNamespace(full=r.next_out, sent=r.share_sent, came=r.share_came))
         halo = Halo(column, SimpleNamespace(left=r.left, right=r.right, **vars(pick(r, "halo"))), r.pair, 2 * WIN, CHUNK)
+        r.late.next_attn.wait()
         wide_attn.put(packed(r.next_attn.at[1]))
         wide_attn.start_line()
         wide_attn.start_pair()
+        r.late.next_ffn.wait()
         wide_down.put(r.next_ffn[1, 1].astype(BF))
         wide_down.start_pair()
         wide_up.put(r.next_ffn[1, 0].astype(BF))
         halo.clear()
-        r.out_proj[...] = r.attn[:, 3 * width :]
+        r.late.full_out.wait()
+        r.late.gathered.wait()
         r.hidden_bias = r.split[0][:, 2 * width :]
         next_bias = projection_bias(r.split[1], width)
-
-        def share(kind, slot):
-            device = who.across if kind == 1 else who.sibling
-            return copy_to(
-                r.next_out.at[slot], r.next_out.at[slot], r.share_sent.at[kind], r.share_came.at[kind], device
-            )
-
-        def hand_on():
-            share(1, who.across[1]).wait_recv()
-            share(2, who.across[1]).start()
 
         def unpack():
             wide_attn.arrive()
             packed_attn = r.full_attn[...].reshape(D, 4 * width)
             r.next_proj[...] = packed_attn[:, : 3 * width]
-            r.next_out[column.here] = packed_attn[:, 3 * width :].astype(F32).T.astype(BF)
-            share(0, column.here).start()
-            share(1, column.here).start()
-
-        ticks = [(3, r.late.residual.wait), (4, r.late.ffn_up.wait), (4, r.late.ffn_down.wait), (chunks, unpack), (chunks + 6, hand_on)]
+            share.begin(packed_attn[:, 3 * width :])
+
+        ticks = [(0, r.late.residual.wait), (1, r.late.ffn_up.wait), (1, r.late.ffn_down.wait), (chunks, unpack), (chunks + 6, share.hand_on)]
         ticks += [(when, lambda k=k: wide_attn.relay(k + 1)) for k, when in enumerate(GATHER_TIMES[0])]
         ticks += [(GATHER_TIMES[1][0], wide_up.start_line), (GATHER_TIMES[1][1], wide_up.start_pair)]
         ticks += [(when, lambda k=k: wide_up.relay(k + 1)) for k, when in enumerate(GATHER_TIMES[2])]
         ticks += [(GATHER_TIMES[3][0], wide_down.begin)]
         ticks += [(when, lambda k=k: wide_down.relay(k + 1)) for k, when in enumerate(GATHER_TIMES[3][1:])]
-        middle, feed, final = forward_stages(r, who, first.take, second, spread)
-
-        def project(t):
-            first.give(t, dot_nt(r.mixed[who.chunk(t), :], r.out_proj[...]))
+
+        def projected(t):
+            mine = jnp.concatenate([r.gathered[k, who.half(t), :] for k in range(4)], axis=1)
+            return dot(mine, r.full_out[...].reshape(D, D))
+
+        middle, feed, final = forward_stages(r, who, projected, second, spread)
 
         def middle_out(t):
             middle(t)
@@ -1559,22 +1632,17 @@
         run_stages(
             chunks,
             [
-                (5, second.add),
-                (1, first.add),
-                (7, close),
-                (3, middle_out),
+                (2, second.add),
+                (4, close),
+                (0, middle_out),
                 (8, next_project),
-                (4, feed_out),
-                (0, project),
+                (1, feed_out),
             ],
             ticks,
         )
-        finish_all(chunks, (first, second, spread, last))
+        finish_all(chunks, (second, spread, last))
         halo.arrive()
-        share(0, who.sibling[1]).wait_recv()
-        share(2, who.diagonal[1]).wait_recv()
-        for kind, slot in enumerate((column.here, column.here, who.across[1])):
-            share(kind, slot).wait_send()
+        share.finish()
         wide_up.arrive()
         halo.finish()
         for engine in (wide_attn, wide_up, wide_down):
@@ -1604,12 +1672,9 @@
     flushed.update(spread_full=((rows, D), BF), last_full=((rows, D), BF))
     scratch = dict(
         normed=pltpu.VMEM((rows // 2, D), F32),
-        out_proj=pltpu.VMEM((D, width), BF),
         next_proj=pltpu.VMEM((D, 3 * width), BF),
-        share_sent=pltpu.SemaphoreType.DMA((3,)),
-        share_came=pltpu.SemaphoreType.DMA((3,)),
-    )
-    scratch.update(prefixed("first", exchange_scratch(rows)))
+        **share_scratch(),
+    )
     scratch.update(prefixed("second", exchange_scratch(rows)))
     for key in ("spread", "last"):
         for part in ("sent", "came"):
@@ -1620,19 +1685,20 @@
     return run_kernel(
         body,
         "middle_forward",
-        dict(
-            mixed=mixed,
-            attn=attn,
-            shared=shared,
-            split=split_biases,
-            next_attn=attn_weights,
-            next_ffn=ffn_weights,
-        ),
+        dict(shared=shared, split=split_biases),
         outputs,
         scratch,
         collective=1,
         flops=2 * rows * D * (4 * width + 2 * units),
-        late=dict(residual=residual, ffn_up=ffn_up, ffn_down=ffn_down),
+        late=dict(
+            next_attn=attn_weights,
+            next_ffn=ffn_weights,
+            full_out=full_out,
+            gathered=gathered,
+            residual=residual,
+            ffn_up=ffn_up,
+            ffn_down=ffn_down,
+        ),
         flushed=flushed,
         pieces=chunks,
     )
@@ -1653,9 +1719,13 @@
         mids = Gather(who, SimpleNamespace(full=r.grad_low, sent=r.mids_sent, came=r.mids_came))
         out = Gather(who, SimpleNamespace(full=r.output, sent=r.out_sent, came=r.out_came))
         who.meet()
+        r.late.mixed.wait()
         for t in range(chunks // 2, chunks):
             heads.give(t)
+        r.late.first_mixed.wait()
         r.gathered[:, : rows // 4, :] = r.first_mixed[...]
+        r.late.full_out.wait()
+        r.late.attn.wait()
         r.out_proj[...] = r.attn[:, 3 * width :]
         r.hidden_bias = r.split[1][:, 2 * width :]
         clear(r.vectors, r.units, r.sum_up, r.sum_down, r.sum_out)
@@ -1743,10 +1813,6 @@
         body,
         "turning",
         dict(
-            mixed=mixed,
-            first_mixed=first_mixed,
-            full_out=out_proj,
-            attn=attn,
             shared=shared,
             split=split_biases,
         ),
@@ -1754,7 +1820,17 @@
         scratch,
         collective=2,
         flops=2 * rows * D * (3 * width + 6 * units),
-        late=dict(residual=residual, ffn_up=ffn_up, ffn_down=ffn_down, cotangent=cotangent, turn=turn),
+        late=dict(
+            mixed=mixed,
+            first_mixed=first_mixed,
+            full_out=out_proj,
+            attn=attn,
+            residual=residual,
+            ffn_up=ffn_up,
+            ffn_down=ffn_down,
+            cotangent=cotangent,
+            turn=turn,
+        ),
     )
 
 
@@ -1848,6 +1924,8 @@
         who.meet(column)
         up, down, three = scatter_three(column, r, (r.up_total, r.down_total, r.attn_total))
         begin, end, back_ticks = projection_back_stage(r, who, column, zeroth)
+        for copy in (r.late.out_right, r.late.grad_own, r.late.grad_query, r.late.next_attn, r.late.low):
+            copy.wait()
         begin()
         up.start()
         down.start()
@@ -1862,6 +1940,7 @@
         ticks += [(4, r.late.ffn_down.wait), (4, r.late.slope.wait), (4, r.late.hidden.wait)]
         ticks += [(4, r.late.spread_full.wait), (7, r.late.unit_one.wait), (8, r.late.mixed.wait)]
         ticks = back_ticks + ticks
+        r.late.attn.wait()
         r.out_proj[...] = r.attn[:, 3 * width :]
         clear(r.vectors, r.units, r.biases, r.sum_up, r.sum_down, r.sum_out, r.sum_three)
         enter, feed_back, leave, project_back = backward_stages(r, who, ends, third, mids)
@@ -1921,14 +2000,8 @@
         body,
         "middle_backward",
         dict(
-            grad_query=back.out_query,
-            grad_own=back.out_own,
-            out_right=back.out_right,
-            next_attn=next_attn,
-            low=low,
             inverse_one=saved.inverse_one,
             inverse_two=saved.inverse_two,
-            attn=attn,
             shared=shared,
             above_up=above.up.reshape(count, block, units),
             above_down=above.down.reshape(count, block, units),
@@ -1940,6 +2013,12 @@
         flops=2 * rows * D * (8 * width + 4 * units),
         in_hbm=("above_up", "above_down"),
         late=dict(
+            out_right=back.out_right,
+            grad_own=back.out_own,
+            grad_query=back.out_query,
+            next_attn=next_attn,
+            low=low,
+            attn=attn,
             unit_two=saved.unit_two,
             grad_above=grad_above,
             ffn_down=ffn_down,
@@ -2083,6 +2162,8 @@
         up, down, three = scatter_three(column, r, (r.ffn_grads.at[0], r.ffn_grads.at[1], r.attn_grads.at[0]))
         small = SmallSum(who, column, pick(r, "small"))
         begin, end, back_ticks = projection_back_stage(r, who, column, zeroth)
+        for copy in (r.late.out_right, r.late.grad_own, r.late.grad_query, r.late.next_attn, r.late.low):
+            copy.wait()
         begin()
         up.start()
         down.start()
@@ -2103,7 +2184,7 @@
 
         ticks = [tick for engine, times in zip((up, down, three), END_TIMES) for tick in engine.ticks(times)]
         ticks += [(chunks // 2 + 2, start_three), (3, r.late.grad_above.wait)]
-        ticks += [(chunks // 2 + 4, lambda: small.second(12)), (chunks // 2 + 6, small.third)]
+        ticks += [(SMALL_TIMES[0], lambda: small.second(12)), (SMALL_TIMES[1], small.third)]
         ticks = back_ticks + ticks
         clear(r.biases, r.sum_three)
 
@@ -2158,11 +2239,6 @@
         body,
         "ending",
         dict(
-            grad_query=back.out_query,
-            grad_own=back.out_own,
-            out_right=back.out_right,
-            next_attn=next_attn,
-            low=low,
             above_up=above.up.reshape(count, block, units),
             above_down=above.down.reshape(count, block, units),
             above_proj=above.proj,
@@ -2180,7 +2256,14 @@
         collective=4,
         flops=2 * rows * D * 6 * width,
         in_hbm=("above_up", "above_down"),
-        late=dict(grad_above=grad_above),
+        late=dict(
+            out_right=back.out_right,
+            grad_own=back.out_own,
+            grad_query=back.out_query,
+            next_attn=next_attn,
+            low=low,
+            grad_above=grad_above,
+        ),
     )
 
 
@@ -2340,8 +2423,8 @@
         full.reshape(D, -1) for full in (near.full_attn, near.full_up, near.full_down)
     )
     mid = middle_forward(
-        near.out,
-        attn_zero,
+        near.gathered,
+        near.full_out,
         up_zero,
         down_zero,
         near.low,
@@ -2351,8 +2434,16 @@
         ffn_weights,
         count,
     )
+    far = attend(
+        mid.query,
+        mid.pair,
+        mid.left,
+        mid.right,
+        near.seg_query,
+        near.seg_keys,
+        dilated_heads,
+    )
     attn_one, up_one, down_one = (full.reshape(D, -1) for full in (mid.full_attn, mid.full_up, mid.full_down))
-    far = attend(mid.query, mid.pair, mid.left, mid.right, near.seg_query, near.seg_keys, dilated_heads)
     top = turning(
         far.out, far.first, mid.next_out, attn_one, up_one, down_one, mid.last_full, near.shared, split_biases, cotangent, near.turn
     )

time: 379 us -> 363 us (0.958)
  Pallas kernels: 373 us -> 357 us
    pallas_call x9, Pallas kernels: 373 us -> 357 us  [run_kernel(): pl.pallas_call(kernel, out_shape=shapes, in_specs=[spec_of(key) for key i...]
where the time goes in v4:
time: 363 us; the launch traced here: 358 us
  Pallas kernels  357 us (98%)
    pallas_call x9, Pallas kernels, run_kernel(): pl.pallas_call(kernel, out_shape=shapes, in_specs=[spec_of(key) for key i...  357 us

profile of v4, /device:TPU:0, one launch (start us, length us, event | category | flops | bytes accessed | tf_op | source)
XLA Modules:
  0.0 357.9 jit_solution(11528684421143523565)
XLA Ops:
  0.7 56.4 %opening.1 = (bf16[8,96,768]{2,1,0:T(8,128)(2,1)}, bf16[8,96,768]{2,1,0:T(8,128)(2,1)}, f32[16,768]{1,0:T(8,128)}, f32[1024,2]{1,0:T(8,128)}, f32[8,2048]{1,0:T(...) custom-call(s32[8,128]{1,0:T(8,128)} %bitcast.29, ...), custom_call_target="tpu_custom_call" | custom-call | flops 2113929216 | bytes 18457632 | tf_op jit(solution)/shard_map/opening/pallas_call | solution.py:126
  57.1 59.6 %middle_forward.1 = (f32[512,128]{1,0:T(8,128)}, f32[512,128]{1,0:T(8,128)}, bf16[1024,192]{1,0:T(8,128)(2,1)}, bf16[1024,384]{1,0:T(8,128)(2,1)}, bf16[8,96,768...) custom-call(f32[16,768]{1,0:T(8,128)} %get-tuple-element.104.refs_0_, ...), custom_call_target="tpu_custom_call" | custom-call | flops 3623878656 | bytes 24372224 | tf_op jit(solution)/shard_map/middle_forward/pallas_call | solution.py:126
  116.7 15.4 %attend.1 = (bf16[1024,192]{1,0:T(8,128)(2,1)}, bf16[4,256,192]{2,1,0:T(8,128)(2,1)}, bf16[1024,192]{1,0:T(8,128)(2,1)}, bf16[1024,192]{1,0:T(8,128)(2,1)}, bf16...) custom-call(bf16[1024,192]{1,0:T(8,128)(2,1)} %get-tuple-element.112.refs_0_, ...), custom_call_target="tpu_custom_call" | custom-call | flops 2415919104 | bytes 9904136 | tf_op jit(solution)/shard_map/attend/pallas_call | solution.py:126
  132.1 48.9 %turning.1 = (bf16[1024,768]{1,0:T(8,128)(2,1)}, bf16[768,768]{1,0:T(8,128)(2,1)}, bf16[768,768]{1,0:T(8,128)(2,1)}, bf16[768,192]{1,0:T(8,128)(2,1)}, bf16[1024...) custom-call(f32[16,768]{1,0:T(8,128)} %get-tuple-element.104.refs_0_.refs_2_, ...), custom_call_target="tpu_custom_call" | custom-call | flops 8153726976 | bytes 16131072 | tf_op jit(solution)/shard_map/turning/pallas_call | solution.py:126
  181.0 18.5 %attend_back.2 = (bf16[1024,192]{1,0:T(8,128)(2,1)}, bf16[1024,384]{1,0:T(8,128)(2,1)}, bf16[512,384]{1,0:T(8,128)(2,1)}) custom-call(bf16[1024,192]{1,0:T(8,128)(2,1)} %get-tuple-element.129.refs_0_, bf16[1024,192]{1,0:T(8,128)(2,1)} %get-tuple-element.130.refs_1_, bf16[1024,192]{1,0:T(8,128)(2,1)} %get-tuple-element.131.refs_2_, ...), custom_call_target="tpu_custom_call" | custom-call | flops 4831838208 | bytes 9043976 | tf_op jit(solution)/shard_map/attend_back/pallas_call | solution.py:126
  199.6 60.1 %middle_backward.1 = (bf16[768,768]{1,0:T(8,128)(2,1)}, bf16[768,768]{1,0:T(8,128)(2,1)}, bf16[768,192]{1,0:T(8,128)(2,1)}, f32[512,768]{1,0:T(8,128)}, bf16[102...) custom-call(f32[512,128]{1,0:T(8,128)} %get-tuple-element.110.refs_0, ...), custom_call_target="tpu_custom_call" | custom-call | flops 7247757312 | bytes 26494976 | tf_op jit(solution)/shard_map/middle_backward/pallas_call | solution.py:126
  259.7 14.0 %attend_back.3 = (bf16[1024,192]{1,0:T(8,128)(2,1)}, bf16[1024,384]{1,0:T(8,128)(2,1)}, bf16[256,384]{1,0:T(8,128)(2,1)}) custom-call(bf16[1024,192]{1,0:T(8,128)(2,1)} %get-tuple-element.157.refs_0_, bf16[1024,192]{1,0:T(8,128)(2,1)} %get-tuple-element.145.refs_20_.refs_1_, bf16[1024,192]{1,0:T(8,128)(2,1)} %get-tuple-element.158.refs_2_, ...), custom_call_target="tpu_custom_call" | custom-call | flops 4831838208 | bytes 8454152 | tf_op jit(solution)/shard_map/attend_back/pallas_call | solution.py:126
  273.6 65.5 %ending.1 = (bf16[1024,768]{1,0:T(8,128)(2,1)}, f32[4,96,768]{2,1,0:T(8,128)}, f32[2,96,768]{2,1,0:T(8,128)}, f32[16,768]{1,0:T(8,128)}, f32[8,128]{1,0:T(8,128)}) custom-call(bf16[8,96,768]{2,1,0:T(8,128)(2,1)} %bitcast.20, bf16[8,96,768]{2,1,0:T(8,128)(2,1)} %bitcast.21, bf16[768,192]{1,0:T(8,128)(2,1)} %get-tuple-element.148.refs_2_, ...), custom_call_target="tpu_custom_call" | custom-call | flops 1811939328 | bytes 12752896 | tf_op jit(solution)/shard_map/ending/pallas_call | solution.py:126
  339.1 18.5 %update.1 = (f32[1024,768]{1,0:T(8,128)}, f32[1024,768]{1,0:T(8,128)}, f32[2,2,96,768]{3,2,1,0:T(8,128)}, f32[2,4,96,192]{3,2,1,0:T(8,128)}, f32[2,2,96,768]{3,2...) custom-call(f32[4,96,768]{2,1,0:T(8,128)} %get-tuple-element.166.ref, ...), custom_call_target="tpu_custom_call" | custom-call | flops 905969664 | bytes 37488644 | tf_op jit(solution)/shard_map/update/pallas_call | solution.py:126

commit v5 on v4

--- a/solution.py
+++ b/solution.py
@@ -35,9 +35,9 @@
 SCORE_SCALE = DH ** (-0.5)
 
 GATHER_TIMES = ((2, 3, 5), (3, 5), (6, 7, 9), (7, 10, 13, 16))
-BACK_TIMES = ((1, 4, 7, 10, 12), (6, 8, 10, 12), (10, 13, 15, 17))
+BACK_TIMES = ((1, 4, 7, 10, 12), (6, 8, 10, 12), (9, 12, 14, 16))
 END_TIMES = ((1, 4, 7, 10, 13), (5, 8, 10, 12), (11, 14, 15, 16))
-SMALL_TIMES = (8, 10)
+SMALL_TIMES = (7, 12)
 
 
 def dot(left, right):
@@ -2169,8 +2169,11 @@
         down.start()
 
         def start_three():
+            small.second(12)
             pack_attention(r)
             three.start()
+
+        def start_small():
             r.small_kept[0, 0:6, :] = r.vectors_low[0:6, :]
             r.small_kept[0, 6:12, :] = r.vectors_top[0:6, :]
             r.small_kept[0, 12:13, :] = r.units_low[0:1, :]
@@ -2183,8 +2186,8 @@
             small.core_copy().start()
 
         ticks = [tick for engine, times in zip((up, down, three), END_TIMES) for tick in engine.ticks(times)]
-        ticks += [(chunks // 2 + 2, start_three), (3, r.late.grad_above.wait)]
-        ticks += [(SMALL_TIMES[0], lambda: small.second(12)), (SMALL_TIMES[1], small.third)]
+        ticks += [(3, r.late.grad_above.wait)]
+        ticks += [(chunks // 2 + 2, start_small), (SMALL_TIMES[0], start_three), (SMALL_TIMES[1], small.third)]
         ticks = back_ticks + ticks
         clear(r.biases, r.sum_three)
 
@@ -2306,29 +2309,31 @@
         for key, value in zip(names, results):
             getattr(r, "ffn_" + key + "_new")[...] = value
 
-        for at in range(4):
-
-            @pl.when(step == at)
-            def _(at=at):
-                layer = at // 2
-                for which in (2 * (at % 2), 2 * (at % 2) + 1):
-                    grad = factor * r.attn_grads[layer, :, which * width : (which + 1) * width]
-                    weight, first, second, average = matrix(
-                        grad,
-                        r.attn_weights[layer, which],
-                        r.attn_first[layer, which],
-                        r.attn_second[layer, which],
-                        r.attn_average[layer, which],
-                        r.attn_basis[layer, which, 0, 0],
-                        rates[which],
-                    )
-                    r.attn_weights_new[layer, which] = weight
-                    r.attn_first_new[layer, which] = first
-                    r.attn_average_new[layer, which] = average
-                    if which < 3:
-                        r.attn_second_new[layer, which] = second
-                    else:
-                        r.projection_second[layer] = second
+        for k in range(2):
+            last = jnp.logical_and(step % 2 == 1, k == 1)
+            weight, first, second, average = matrix(
+                factor * r.attn_grads[:, k * width : (k + 1) * width],
+                r.attn_weights[k],
+                r.attn_first[k],
+                r.attn_second[k],
+                r.attn_average[k],
+                r.attn_basis[k],
+                jnp.where(last, rates[3], rates[0]),
+            )
+            r.attn_weights_new[k] = weight
+            r.attn_first_new[k] = first
+            r.attn_average_new[k] = average
+
+            @pl.when(step % 2 == 0)
+            def _(k=k, second=second):
+                r.attn_second_new[step // 2, k] = second
+
+            @pl.when(step % 2 == 1)
+            def _(k=k, second=second):
+                if k == 0:
+                    r.attn_second_new[step // 2, 2] = second
+                else:
+                    r.projection_second[step // 2] = second
 
         @pl.when(step == 0)
         def _():
@@ -2363,8 +2368,12 @@
         inputs["ffn_" + key] = array
         specs["ffn_" + key] = matrix_spec
     specs["ffn_basis"] = pl.BlockSpec((None, None, None, None, units, units), lambda i: (i // 2, i % 2, 0, 0, 0, 0))
+    pair_spec = pl.BlockSpec((None, 2, block, width), lambda i: (i // 2, i % 2, 0, 0))
     for key, array in zip(names, attn):
         inputs["attn_" + key] = array
+        specs["attn_" + key] = pair_spec
+    specs["attn_basis"] = pl.BlockSpec((None, 2, None, None, width, width), lambda i: (i // 2, i % 2, 0, 0, 0, 0))
+    specs["attn_grads"] = pl.BlockSpec((None, block, 2 * width), lambda i: (i // 2, 0, i % 2))
     for prefix, group in (("split", split), ("shared", shared)):
         for key, array in zip(("old", "first", "second"), group):
             inputs[prefix + "_" + key] = array
@@ -2372,7 +2381,9 @@
         outputs["ffn_" + key + "_new"] = (ffn[0].shape, F32)
         specs["ffn_" + key + "_new"] = matrix_spec
         outputs["attn_" + key + "_new"] = (attn[0].shape, F32)
+        specs["attn_" + key + "_new"] = pair_spec
     outputs["attn_second_new"] = ((2, 3, block, width), F32)
+    del specs["attn_second_new"]
     outputs["projection_second"] = ((2, block, width), F32)
     for prefix, group in (("split", split), ("shared", shared)):
         for key in ("old", "first", "second"):

time: 363 us -> 361 us (level)
  no operation moved by 1% of the time
where the time goes in v5:
time: 361 us; the launch traced here: 356 us
  Pallas kernels  355 us (98%)
    pallas_call x9, Pallas kernels, run_kernel(): pl.pallas_call(kernel, out_shape=shapes, in_specs=[spec_of(key) for key i...  355 us

profile of v5, /device:TPU:0, one launch (start us, length us, event | category | flops | bytes accessed | tf_op | source)
XLA Modules:
  0.0 356.0 jit_solution(1287656629612890308)
XLA Ops:
  0.7 56.4 %opening.1 = (bf16[8,96,768]{2,1,0:T(8,128)(2,1)}, bf16[8,96,768]{2,1,0:T(8,128)(2,1)}, f32[16,768]{1,0:T(8,128)}, f32[1024,2]{1,0:T(8,128)}, f32[8,2048]{1,0:T(...) custom-call(s32[8,128]{1,0:T(8,128)} %bitcast.29, ...), custom_call_target="tpu_custom_call" | custom-call | flops 2113929216 | bytes 18457632 | tf_op jit(solution)/shard_map/opening/pallas_call | solution.py:126
  57.1 59.6 %middle_forward.1 = (f32[512,128]{1,0:T(8,128)}, f32[512,128]{1,0:T(8,128)}, bf16[1024,192]{1,0:T(8,128)(2,1)}, bf16[1024,384]{1,0:T(8,128)(2,1)}, bf16[8,96,768...) custom-call(f32[16,768]{1,0:T(8,128)} %get-tuple-element.104.refs_0_, ...), custom_call_target="tpu_custom_call" | custom-call | flops 3623878656 | bytes 24372224 | tf_op jit(solution)/shard_map/middle_forward/pallas_call | solution.py:126
  116.7 15.4 %attend.1 = (bf16[1024,192]{1,0:T(8,128)(2,1)}, bf16[4,256,192]{2,1,0:T(8,128)(2,1)}, bf16[1024,192]{1,0:T(8,128)(2,1)}, bf16[1024,192]{1,0:T(8,128)(2,1)}, bf16...) custom-call(bf16[1024,192]{1,0:T(8,128)(2,1)} %get-tuple-element.112.refs_0_, ...), custom_call_target="tpu_custom_call" | custom-call | flops 2415919104 | bytes 9904136 | tf_op jit(solution)/shard_map/attend/pallas_call | solution.py:126
  132.1 48.9 %turning.1 = (bf16[1024,768]{1,0:T(8,128)(2,1)}, bf16[768,768]{1,0:T(8,128)(2,1)}, bf16[768,768]{1,0:T(8,128)(2,1)}, bf16[768,192]{1,0:T(8,128)(2,1)}, bf16[1024...) custom-call(f32[16,768]{1,0:T(8,128)} %get-tuple-element.104.refs_0_.refs_2_, ...), custom_call_target="tpu_custom_call" | custom-call | flops 8153726976 | bytes 16131072 | tf_op jit(solution)/shard_map/turning/pallas_call | solution.py:126
  181.0 18.5 %attend_back.2 = (bf16[1024,192]{1,0:T(8,128)(2,1)}, bf16[1024,384]{1,0:T(8,128)(2,1)}, bf16[512,384]{1,0:T(8,128)(2,1)}) custom-call(bf16[1024,192]{1,0:T(8,128)(2,1)} %get-tuple-element.129.refs_0_, bf16[1024,192]{1,0:T(8,128)(2,1)} %get-tuple-element.130.refs_1_, bf16[1024,192]{1,0:T(8,128)(2,1)} %get-tuple-element.131.refs_2_, ...), custom_call_target="tpu_custom_call" | custom-call | flops 4831838208 | bytes 9043976 | tf_op jit(solution)/shard_map/attend_back/pallas_call | solution.py:126
  199.6 59.8 %middle_backward.1 = (bf16[768,768]{1,0:T(8,128)(2,1)}, bf16[768,768]{1,0:T(8,128)(2,1)}, bf16[768,192]{1,0:T(8,128)(2,1)}, f32[512,768]{1,0:T(8,128)}, bf16[102...) custom-call(f32[512,128]{1,0:T(8,128)} %get-tuple-element.110.refs_0, ...), custom_call_target="tpu_custom_call" | custom-call | flops 7247757312 | bytes 26494976 | tf_op jit(solution)/shard_map/middle_backward/pallas_call | solution.py:126
  259.4 12.6 %attend_back.3 = (bf16[1024,192]{1,0:T(8,128)(2,1)}, bf16[1024,384]{1,0:T(8,128)(2,1)}, bf16[256,384]{1,0:T(8,128)(2,1)}) custom-call(bf16[1024,192]{1,0:T(8,128)(2,1)} %get-tuple-element.157.refs_0_, bf16[1024,192]{1,0:T(8,128)(2,1)} %get-tuple-element.145.refs_20_.refs_1_, bf16[1024,192]{1,0:T(8,128)(2,1)} %get-tuple-element.158.refs_2_, ...), custom_call_target="tpu_custom_call" | custom-call | flops 4831838208 | bytes 8454152 | tf_op jit(solution)/shard_map/attend_back/pallas_call | solution.py:126
  271.9 65.5 %ending.1 = (bf16[1024,768]{1,0:T(8,128)(2,1)}, f32[4,96,768]{2,1,0:T(8,128)}, f32[2,96,768]{2,1,0:T(8,128)}, f32[16,768]{1,0:T(8,128)}, f32[8,128]{1,0:T(8,128)}) custom-call(bf16[8,96,768]{2,1,0:T(8,128)(2,1)} %bitcast.20, bf16[8,96,768]{2,1,0:T(8,128)(2,1)} %bitcast.21, bf16[768,192]{1,0:T(8,128)(2,1)} %get-tuple-element.148.refs_2_, ...), custom_call_target="tpu_custom_call" | custom-call | flops 1811939328 | bytes 12752896 | tf_op jit(solution)/shard_map/ending/pallas_call | solution.py:126
  337.4 18.4 %update.1 = (f32[1024,768]{1,0:T(8,128)}, f32[1024,768]{1,0:T(8,128)}, f32[2,2,96,768]{3,2,1,0:T(8,128)}, f32[2,4,96,192]{3,2,1,0:T(8,128)}, f32[2,2,96,768]{3,2...) custom-call(f32[4,96,768]{2,1,0:T(8,128)} %get-tuple-element.166.ref, ...), custom_call_target="tpu_custom_call" | custom-call | flops 905969664 | bytes 37488644 | tf_op jit(solution)/shard_map/update/pallas_call | solution.py:126

commit v6 on v5

--- a/solution.py
+++ b/solution.py
@@ -35,6 +35,7 @@
 SCORE_SCALE = DH ** (-0.5)
 
 GATHER_TIMES = ((2, 3, 5), (3, 5), (6, 7, 9), (7, 10, 13, 16))
+PROJECT_TIMES = (8, 9, 10, 12)
 BACK_TIMES = ((1, 4, 7, 10, 12), (6, 8, 10, 12), (9, 12, 14, 16))
 END_TIMES = ((1, 4, 7, 10, 13), (5, 8, 10, 12), (11, 14, 15, 16))
 SMALL_TIMES = (7, 12)
@@ -1622,12 +1623,19 @@
             r.flush.unit_two.copy(who.half(t), t).start()
             last.give(t, result)
 
-        def next_project(t):
-            value = (dot(last.take(t), r.next_proj[...]) + next_bias).astype(BF)
-            r.query[who.chunk(t), :] = value[:, :width]
-            r.pair[who.chunk(t), :] = value[:, width:]
-            halo.send(t)
-            r.flush.last_full.copy(who.chunk(t), t).start()
+        def next_project(k):
+            chunk_pair = (2 * k, 2 * k + 1)
+            for t in chunk_pair:
+                last.wait(t)
+            both = who.two_chunks(2 * k + 1)
+            value = (dot(r.last_full[both, :], r.next_proj[...]) + next_bias).astype(BF)
+            r.query[both, :] = value[:, :width]
+            r.pair[both, :] = value[:, width:]
+            for t in chunk_pair:
+                halo.send(t)
+                r.flush.last_full.copy(who.chunk(t), t).start()
+
+        ticks += [(when, lambda k=k: next_project(k)) for k, when in enumerate(PROJECT_TIMES)]
 
         run_stages(
             chunks,
@@ -1635,7 +1643,6 @@
                 (2, second.add),
                 (4, close),
                 (0, middle_out),
-                (8, next_project),
                 (1, feed_out),
             ],
             ticks,

time: 361 us -> 361 us (level)
  no operation moved by 1% of the time
where the time goes in v6:
time: 361 us; the launch traced here: 355 us
  Pallas kernels  354 us (98%)
    pallas_call x9, Pallas kernels, run_kernel(): pl.pallas_call(kernel, out_shape=shapes, in_specs=[spec_of(key) for key i...  354 us

profile of v6, /device:TPU:0, one launch (start us, length us, event | category | flops | bytes accessed | tf_op | source)
XLA Modules:
  0.0 355.1 jit_solution(17917064150186479489)
XLA Ops:
  0.7 56.4 %opening.1 = (bf16[8,96,768]{2,1,0:T(8,128)(2,1)}, bf16[8,96,768]{2,1,0:T(8,128)(2,1)}, f32[16,768]{1,0:T(8,128)}, f32[1024,2]{1,0:T(8,128)}, f32[8,2048]{1,0:T(...) custom-call(s32[8,128]{1,0:T(8,128)} %bitcast.29, ...), custom_call_target="tpu_custom_call" | custom-call | flops 2113929216 | bytes 18457632 | tf_op jit(solution)/shard_map/opening/pallas_call | solution.py:127
  57.1 59.6 %middle_forward.1 = (f32[512,128]{1,0:T(8,128)}, f32[512,128]{1,0:T(8,128)}, bf16[1024,192]{1,0:T(8,128)(2,1)}, bf16[1024,384]{1,0:T(8,128)(2,1)}, bf16[8,96,768...) custom-call(f32[16,768]{1,0:T(8,128)} %get-tuple-element.104.refs_0_, ...), custom_call_target="tpu_custom_call" | custom-call | flops 3623878656 | bytes 24372224 | tf_op jit(solution)/shard_map/middle_forward/pallas_call | solution.py:127
  116.7 15.3 %attend.1 = (bf16[1024,192]{1,0:T(8,128)(2,1)}, bf16[4,256,192]{2,1,0:T(8,128)(2,1)}, bf16[1024,192]{1,0:T(8,128)(2,1)}, bf16[1024,192]{1,0:T(8,128)(2,1)}, bf16...) custom-call(bf16[1024,192]{1,0:T(8,128)(2,1)} %get-tuple-element.112.refs_0_, ...), custom_call_target="tpu_custom_call" | custom-call | flops 2415919104 | bytes 9904136 | tf_op jit(solution)/shard_map/attend/pallas_call | solution.py:127
  132.0 49.3 %turning.1 = (bf16[1024,768]{1,0:T(8,128)(2,1)}, bf16[768,768]{1,0:T(8,128)(2,1)}, bf16[768,768]{1,0:T(8,128)(2,1)}, bf16[768,192]{1,0:T(8,128)(2,1)}, bf16[1024...) custom-call(f32[16,768]{1,0:T(8,128)} %get-tuple-element.104.refs_0_.refs_2_, ...), custom_call_target="tpu_custom_call" | custom-call | flops 8153726976 | bytes 16131072 | tf_op jit(solution)/shard_map/turning/pallas_call | solution.py:127
  181.3 16.6 %attend_back.2 = (bf16[1024,192]{1,0:T(8,128)(2,1)}, bf16[1024,384]{1,0:T(8,128)(2,1)}, bf16[512,384]{1,0:T(8,128)(2,1)}) custom-call(bf16[1024,192]{1,0:T(8,128)(2,1)} %get-tuple-element.129.refs_0_, bf16[1024,192]{1,0:T(8,128)(2,1)} %get-tuple-element.130.refs_1_, bf16[1024,192]{1,0:T(8,128)(2,1)} %get-tuple-element.131.refs_2_, ...), custom_call_target="tpu_custom_call" | custom-call | flops 4831838208 | bytes 9043976 | tf_op jit(solution)/shard_map/attend_back/pallas_call | solution.py:127
  197.9 60.5 %middle_backward.1 = (bf16[768,768]{1,0:T(8,128)(2,1)}, bf16[768,768]{1,0:T(8,128)(2,1)}, bf16[768,192]{1,0:T(8,128)(2,1)}, f32[512,768]{1,0:T(8,128)}, bf16[102...) custom-call(f32[512,128]{1,0:T(8,128)} %get-tuple-element.110.refs_0, ...), custom_call_target="tpu_custom_call" | custom-call | flops 7247757312 | bytes 26494976 | tf_op jit(solution)/shard_map/middle_backward/pallas_call | solution.py:127
  258.4 12.6 %attend_back.3 = (bf16[1024,192]{1,0:T(8,128)(2,1)}, bf16[1024,384]{1,0:T(8,128)(2,1)}, bf16[256,384]{1,0:T(8,128)(2,1)}) custom-call(bf16[1024,192]{1,0:T(8,128)(2,1)} %get-tuple-element.157.refs_0_, bf16[1024,192]{1,0:T(8,128)(2,1)} %get-tuple-element.145.refs_20_.refs_1_, bf16[1024,192]{1,0:T(8,128)(2,1)} %get-tuple-element.158.refs_2_, ...), custom_call_target="tpu_custom_call" | custom-call | flops 4831838208 | bytes 8454152 | tf_op jit(solution)/shard_map/attend_back/pallas_call | solution.py:127
  271.0 65.4 %ending.1 = (bf16[1024,768]{1,0:T(8,128)(2,1)}, f32[4,96,768]{2,1,0:T(8,128)}, f32[2,96,768]{2,1,0:T(8,128)}, f32[16,768]{1,0:T(8,128)}, f32[8,128]{1,0:T(8,128)}) custom-call(bf16[8,96,768]{2,1,0:T(8,128)(2,1)} %bitcast.20, bf16[8,96,768]{2,1,0:T(8,128)(2,1)} %bitcast.21, bf16[768,192]{1,0:T(8,128)(2,1)} %get-tuple-element.148.refs_2_, ...), custom_call_target="tpu_custom_call" | custom-call | flops 1811939328 | bytes 12752896 | tf_op jit(solution)/shard_map/ending/pallas_call | solution.py:127
  336.5 18.4 %update.1 = (f32[1024,768]{1,0:T(8,128)}, f32[1024,768]{1,0:T(8,128)}, f32[2,2,96,768]{3,2,1,0:T(8,128)}, f32[2,4,96,192]{3,2,1,0:T(8,128)}, f32[2,2,96,768]{3,2...) custom-call(f32[4,96,768]{2,1,0:T(8,128)} %get-tuple-element.166.ref, ...), custom_call_target="tpu_custom_call" | custom-call | flops 905969664 | bytes 37488644 | tf_op jit(solution)/shard_map/update/pallas_call | solution.py:127
